TPU v7x, 32 devices: a whole 2x2x4 slice. The times are simulated.
32 devices in a mesh: gx: 4 (over x, core), gy: 8 (over z, y).
Axes of the slice: x: 2, y: 2, z: 4, core: 2. Of those that a mesh axis runs over, the one named last changes fastest.
Arguments:
- fields_old: float32 [4, 8, 8, 5, 16, 256], P('gx', 'gy'), may hold values from -6 to 6
- coeff_old: float32 [4, 8, 8, 5], P('gx', 'gy'), may hold values from 0.1 to 4
- new_place: int32 [4, 8, 8], P('gx', 'gy'), may hold values from 0 to 255, as said below
- cf_mask: int32 [4, 8, 3, 8], P('gx', 'gy'), may hold values 0 or 1
Outputs:
- smoothed: float32 [4, 8, 8, 5, 16, 256], P('gx', 'gy')
- registers: float32 [4, 8, 5, 6, 256], P('gx', 'gy')
Inputs may be any that keep to these rules, and one draw needn't show every extreme that they name: `new_place`: owners are ordered by row, then column. Each box's new owner is its old owner or the owner just before or after it in that order; at most 2 boxes go from one owner to each of these two neighbours, exactly 2 between the first two owners in every draw; every new slot receives exactly one box.
All inputs are finite; a program needn't handle non-finite values. No bound on the sum of `cf_mask` on one device may be relied on, other than what follows from the above.
Results may differ from a plain program's by a relative error of at most 0.00002.
Values sent between devices are 32-bit elements; how exact they have to be, the bound alone decides.
No kernel may reach another device: no remote copies, remote signals or barrier semaphores. Data moves between devices by JAX's collectives and lax.ppermute only.
A program may use at most 64 MiB of HBM per device.

v0:
```python
import jax
import jax.numpy as jnp
from jax import lax
from jax.sharding import PartitionSpec as P

NC = 5
E = 16
BZ = 8
MOVE = 2


def from_behind(value, axis, steps):
    count = lax.axis_size(axis)
    leading, last = (max(0, -steps), min(count, count - steps))
    return lax.ppermute(value, axis, [(source, source + steps) for source in range(leading, last)])


def padded_2(block, sides, width):
    for axis, dim in sides:
        count = lax.axis_size(axis)
        forward = [(i, i + 1) for i in range(count - 1)]
        backward = [(target, source) for source, target in forward]
        low = lax.ppermute(
            lax.slice_in_dim(block, block.shape[dim] - width, None, axis=dim), axis, forward
        )
        high = lax.ppermute(lax.slice_in_dim(block, 0, width, axis=dim), axis, backward)
        block = jnp.concatenate([low, block, high], axis=dim)
    return block


def partner(x, axis, apart):
    return lax.ppermute(x, axis, [(i, i ^ 1 << apart) for i in range(lax.axis_size(axis))])


def column_face(face, by):
    return from_behind(face, "gy", by)


def neighbours(field):
    padded = padded_2(field, (("gx", 2),), 1)
    zpos = jnp.arange(E * E, dtype=jnp.int32) % E
    y_low = jnp.concatenate(
        [column_face(field[..., E * E - E :], 1), field[..., : E * E - E]], axis=-1
    )
    y_high = jnp.concatenate([field[..., E:], column_face(field[..., :E], -1)], axis=-1)
    blank = jnp.zeros_like(field[:1])
    prev_slot = jnp.concatenate([blank, field[:-1]], axis=0)
    next_slot = jnp.concatenate([field[1:], blank], axis=0)
    below = jnp.where(zpos == 0, jnp.roll(prev_slot, 1 - E, axis=-1), jnp.roll(field, 1, axis=-1))
    above = jnp.where(
        zpos == E - 1, jnp.roll(next_slot, E - 1, axis=-1), jnp.roll(field, -1, axis=-1)
    )
    total = padded[:, :, :-2] + padded[:, :, 2:]
    total = total + y_low + y_high
    total = total + below + above
    return (total, padded, y_low, y_high, below, above)


def place(quarter, axis, parity):
    blank = jnp.zeros_like(quarter)
    return jnp.where(
        parity == 0,
        jnp.concatenate([quarter, blank], axis),
        jnp.concatenate([blank, quarter], axis),
    )


def coarsen(flux):
    lead, comps = (flux.shape[0], flux.shape[1])
    return flux.reshape(lead, comps, E // 2, 2, E // 2, 2).sum(axis=(3, 5)) * 0.25


def by_coarse(quarter, parity):
    halves = (
        quarter.reshape(BZ // 2, 2, NC, E // 2, E // 2)
        .transpose(0, 2, 3, 1, 4)
        .reshape(BZ // 2, NC, E // 2, E)
    )
    return place(halves, 2, parity)


def select_slots(boxes, rates, delta, slot, direction):
    chosen = delta == direction
    order = jnp.cumsum(chosen.astype(jnp.int32)) - 1
    positions = jnp.arange(BZ, dtype=jnp.int32)
    sources = []
    labels = []
    for number in range(MOVE):
        taken = chosen & (order == number)
        sources.append(jnp.sum(jnp.where(taken, positions, 0)))
        labels.append(jnp.sum(jnp.where(taken, slot + 1, 0)))
    sources = jnp.stack(sources)
    return (
        jnp.take(boxes, sources, axis=0),
        jnp.take(rates, sources, axis=0),
        jnp.stack(labels).astype(jnp.float32),
    )


def travel(parcel, direction):
    result = from_behind((parcel[0], parcel[1], parcel[2]), ("gx", "gy"), direction)
    return result


def pick(values, axis, index):
    return lax.dynamic_index_in_dim(values, index, axis, keepdims=False)


def body(fields_old, coeff_old, new_place, cf_mask):
    boxes = fields_old[0, 0]
    rates = coeff_old[0, 0]
    places = new_place[0, 0]
    linear = lax.axis_index("gx") * lax.axis_size("gy") + lax.axis_index("gy")
    owner = places // BZ
    slot = places % BZ
    delta = owner - linear
    arrived = []
    for direction in (1, -1):
        arrived.append(travel(select_slots(boxes, rates, delta, slot, direction), direction))
    pool = jnp.concatenate([boxes, arrived[0][0], arrived[1][0]], axis=0)
    pool_rates = jnp.concatenate([rates, arrived[0][1], arrived[1][1]], axis=0)
    labels = jnp.concatenate(
        [
            jnp.where(delta == 0, slot + 1, 0),
            arrived[0][2].astype(jnp.int32),
            arrived[1][2].astype(jnp.int32),
        ]
    )
    wanted = jnp.arange(BZ, dtype=jnp.int32) + 1
    match = labels[None, :] == wanted[:, None]
    anchor = jnp.sum(
        jnp.where(match, jnp.arange(labels.shape[0], dtype=jnp.int32)[None, :], 0), axis=1
    )
    residual = jnp.take(pool, anchor, axis=0)
    moved_rates = jnp.take(pool_rates, anchor, axis=0)
    coeff = moved_rates[:, :, None, None]
    total = neighbours(residual)[0]
    first = (residual + coeff * total) / (1.0 + 6.0 * coeff)
    total, padded, y_low, y_high, below, above = neighbours(first)
    smoothed = (residual + coeff * total) / (1.0 + 6.0 * coeff)
    par_x = lax.axis_index("gx") % 2
    par_y = lax.axis_index("gy") % 2
    masks = cf_mask[0, 0].astype(jnp.float32)
    rate = moved_rates[:, :, None]
    x_low = rate * (padded[:, :, 0] - first[:, :, 0])
    x_high = rate * (padded[:, :, -1] - first[:, :, -1])
    flux_x = jnp.where(par_x == 0, x_low, x_high) * masks[0][:, None, None]
    reg_x = by_coarse(coarsen(flux_x), par_y)
    y_lower = coeff * (y_low[..., :E] - first[..., :E])
    y_upper = coeff * (y_high[..., E * E - E :] - first[..., E * E - E :])
    flux_y = jnp.where(par_y == 0, y_lower, y_upper) * masks[1][:, None, None, None]
    reg_y = by_coarse(coarsen(flux_y), par_x)
    z_low = (
        coeff[0::2]
        * (below[0::2][..., 0::E] - first[0::2][..., 0::E])
        * masks[2, 0::2][:, None, None, None]
    )
    z_high = (
        coeff[1::2]
        * (above[1::2][..., E - 1 :: E] - first[1::2][..., E - 1 :: E])
        * masks[2, 1::2][:, None, None, None]
    )

    def z_faces(flux):
        return place(place(coarsen(flux), 2, par_x), 3, par_y)

    blank = jnp.zeros_like(reg_x)
    faces = [
        jnp.where(par_x == 0, reg_x, blank),
        jnp.where(par_x == 1, reg_x, blank),
        jnp.where(par_y == 0, reg_y, blank),
        jnp.where(par_y == 1, reg_y, blank),
        z_faces(z_low),
        z_faces(z_high),
    ]
    partial_value = jnp.stack(faces, axis=2).reshape(2, 2, NC, 6, E * E)
    half = pick(partial_value, 1, par_y) + partner(pick(partial_value, 1, 1 - par_y), "gy", 0)
    total_reg = pick(half, 0, par_x) + partner(pick(half, 0, 1 - par_x), "gx", 0)
    return (smoothed[None, None], total_reg[None, None])


def solution(mesh):
    return jax.shard_map(
        body,
        mesh=mesh,
        in_specs=(
            P("gx", "gy", None, None, None, None),
            P("gx", "gy", None, None),
            P("gx", "gy", None),
            P("gx", "gy", None, None),
        ),
        out_specs=(P("gx", "gy", None, None, None, None), P("gx", "gy", None, None, None)),
        check_vma=False,
    )
```

profile of v0, /device:TPU:25, one launch (start us, length us, event | category | flops | bytes accessed | tf_op | source)
XLA Modules:
  0.0 115.1 jit_solution(13679239363945296228)
XLA Ops:
  3.2 2.6 %compare_and_fusion = (pred[2]{0:T(512)(128)(4,1)S(1)}, s32[2]{0:T(128)S(1)}, pred[2]{0:T(512)(128)(4,1)S(1)}, s32[2]{0:T(128)S(1)}) fusion(s32[1]{0:T(128)} %bitcast.14, s32[1]{0:T(128)} %bitcast.13, s32[1]{0:T(128)} %bitcast.12, s32[1]{0:T(128)} %bitcast.11), kind=kLoop, calls=%fused_computation.88 | loop fusion | flops 28 | bytes 36 | tf_op jit(solution)/shard_map/jit(_take)/and | solution.py:94
  5.8 1.6 %gather_fusion.2 = f32[2,5,16,256]{3,2,1,0:T(8,128)S(1)} fusion(f32[8,5,16,256]{3,2,1,0:T(8,128)} %bitcast.123, s32[1024]{0:T(1024)S(1)} %pad_clamp_fusion.2), kind=kCustom, calls=%fused_computation.clone | custom fusion | bytes 327688 | tf_op jit(solution)/shard_map/jit(_take)/gather | solution.py:94
  7.5 3.1 %collective-permute-start.2 = (f32[2,5,16,256]{3,2,1,0:T(8,128)S(1)}, f32[2,5,16,256]{3,2,1,0:T(8,128)S(1)}, u32[]{:S(2)}, u32[]{:S(2)}) collective-permute-start(f32[2,5,16,256]{3,2,1,0:T(8,128)S(1)} %broadcast_select_fusion.2), channel_id=1, source_target_pairs={{0,1},{1,2},{2,3},{3,4},{4,5},{5,6},{6,7},{7,8},{8,9},{9,10},{10,1... | collective-permute-start | bytes 491528 | tf_op jit(solution)/shard_map/ppermute | solution.py:15
  11.4 3.0 %collective-permute-start.3 = (f32[2,5,16,256]{3,2,1,0:T(8,128)S(1)}, f32[2,5,16,256]{3,2,1,0:T(8,128)S(1)}, u32[]{:S(2)}, u32[]{:S(2)}) collective-permute-start(f32[2,5,16,256]{3,2,1,0:T(8,128)S(1)} %broadcast_select_fusion.1), channel_id=1, source_target_pairs={{1,0},{2,1},{3,2},{4,3},{5,4},{6,5},{7,6},{8,7},{9,8},{10,9},{11,1... | collective-permute-start | bytes 491528 | tf_op jit(solution)/shard_map/ppermute | solution.py:15
  14.4 2.6 %add_convert_fusion = (f32[2]{0:T(128)S(1)}, f32[2]{0:T(128)S(1)}) fusion(s32[1]{0:T(128)} %bitcast.5, s32[1]{0:T(128)} %bitcast.3, s32[1]{0:T(128)} %bitcast.9, s32[1]{0:T(128)} %bitcast.7), kind=kLoop, calls=%fused_computation.114 | loop fusion | flops 8 | bytes 32 | tf_op jit(solution)/shard_map/convert_element_type | solution.py:96
  17.0 2.4 %collective-permute-start = (f32[2]{0:T(128)S(1)}, f32[2]{0:T(128)S(1)}, u32[]{:S(2)}, u32[]{:S(2)}) collective-permute-start(f32[2]{0:T(128)S(1)} %get-tuple-element.70), channel_id=1, source_target_pairs={{0,1},{1,2},{2,3},{3,4},{4,5},{5,6},{6,7},{7,8},{8,9},{9,10},{10,1... | collective-permute-start | bytes 32 | tf_op jit(solution)/shard_map/ppermute | solution.py:15
  19.4 3.9 %collective-permute-start.1 = (f32[2]{0:T(128)S(1)}, f32[2]{0:T(128)S(1)}, u32[]{:S(2)}, u32[]{:S(2)}) collective-permute-start(f32[2]{0:T(128)S(1)} %get-tuple-element.71), channel_id=1, source_target_pairs={{1,0},{2,1},{3,2},{4,3},{5,4},{6,5},{7,6},{8,7},{9,8},{10,9},{11,1... | collective-permute-start | bytes 32 | tf_op jit(solution)/shard_map/ppermute | solution.py:15
  24.1 5.1 %collective-permute-start.4 = (f32[2,5]{1,0:T(2,128)S(1)}, f32[2,5]{1,0:T(2,128)S(1)}, u32[]{:S(2)}, u32[]{:S(2)}) collective-permute-start(f32[2,5]{1,0:T(2,128)S(1)} %broadcast_select_fusion.5), channel_id=1, source_target_pairs={{0,1},{1,2},{2,3},{3,4},{4,5},{5,6},{6,7},{7,8},{8,9},{9,10},{10,1... | collective-permute-start | bytes 128 | tf_op jit(solution)/shard_map/ppermute | solution.py:15
  32.4 1.9 %collective-permute-start.5 = (f32[2,5]{1,0:T(2,128)S(1)}, f32[2,5]{1,0:T(2,128)S(1)}, u32[]{:S(2)}, u32[]{:S(2)}) collective-permute-start(f32[2,5]{1,0:T(2,128)S(1)} %broadcast_select_fusion.4), channel_id=1, source_target_pairs={{1,0},{2,1},{3,2},{4,3},{5,4},{6,5},{7,6},{8,7},{9,8},{10,9},{11,1... | collective-permute-start | bytes 128 | tf_op jit(solution)/shard_map/ppermute | solution.py:15
  34.6 5.9 %collective-permute-done.5 = f32[2,5]{1,0:T(2,128)S(1)} collective-permute-done((f32[2,5]{1,0:T(2,128)S(1)}, f32[2,5]{1,0:T(2,128)S(1)}, u32[]{:S(2)}, u32[]{:S(2)}) %collective-permute-start.5) | collective-permute-done | bytes 72 | tf_op jit(solution)/shard_map/ppermute | solution.py:15
  43.7 7.5 %collective-permute-start.8 = (f32[8,5,16,16]{3,2,1,0:T(8,128)S(1)}, f32[8,5,16,16]{3,2,1,0:T(8,128)S(1)}, u32[]{:S(2)}, u32[]{:S(2)}) collective-permute-start(f32[8,5,16,16]{3,2,1,0:T(8,128)S(1)} %get-tuple-element.55), channel_id=1, source_target_pairs={{0,1},{1,2},{2,3},{3,4},{4,5},{5,6},{6,7},{8,9},{9,10},{10,11},{11... | collective-permute-start | bytes 122888 | tf_op jit(solution)/shard_map/ppermute | solution.py:15
  51.2 1.9 %collective-permute-start.9 = (f32[8,5,16,16]{3,2,1,0:T(8,128)S(1)}, f32[8,5,16,16]{3,2,1,0:T(8,128)S(1)}, u32[]{:S(2)}, u32[]{:S(2)}) collective-permute-start(f32[8,5,16,16]{3,2,1,0:T(8,128)S(1)} %get-tuple-element.54), channel_id=1, source_target_pairs={{1,0},{2,1},{3,2},{4,3},{5,4},{6,5},{7,6},{9,8},{10,9},{11,10},{12... | collective-permute-start | bytes 122888 | tf_op jit(solution)/shard_map/ppermute | solution.py:15
  53.1 1.9 %collective-permute-start.6 = (f32[8,5,1,256]{3,2,1,0:T(1,128)S(1)}, f32[8,5,1,256]{3,2,1,0:T(1,128)S(1)}, u32[]{:S(2)}, u32[]{:S(2)}) collective-permute-start(f32[8,5,1,256]{3,2,1,0:T(1,128)S(1)} %get-tuple-element.56), channel_id=1, source_target_pairs={{0,8},{8,16},{16,24},{1,9},{9,17},{17,25},{2,10},{10,18},{18,26},{... | collective-permute-start | bytes 122888 | tf_op jit(solution)/shard_map/ppermute | solution.py:23
  55.0 2.4 %collective-permute-start.7 = (f32[8,5,1,256]{3,2,1,0:T(1,128)S(1)}, f32[8,5,1,256]{3,2,1,0:T(1,128)S(1)}, u32[]{:S(2)}, u32[]{:S(2)}) collective-permute-start(f32[8,5,1,256]{3,2,1,0:T(1,128)S(1)} %get-tuple-element.57), channel_id=1, source_target_pairs={{8,0},{16,8},{24,16},{9,1},{17,9},{25,17},{10,2},{18,10},{26,18},{... | collective-permute-start | bytes 122888 | tf_op jit(solution)/shard_map/ppermute | solution.py:26
  57.5 4.2 %collective-permute-done.9 = f32[8,5,16,16]{3,2,1,0:T(8,128)S(1)} collective-permute-done((f32[8,5,16,16]{3,2,1,0:T(8,128)S(1)}, f32[8,5,16,16]{3,2,1,0:T(8,128)S(1)}, u32[]{:S(2)}, u32[]{:S(2)}) %collective-permute-start.9) | collective-permute-done | bytes 40992 | tf_op jit(solution)/shard_map/ppermute | solution.py:15
  70.6 2.0 %collective-permute-start.12 = (f32[8,5,16,16]{3,2,1,0:T(8,128)}, f32[8,5,16,16]{3,2,1,0:T(8,128)}, u32[]{:S(2)}, u32[]{:S(2)}) collective-permute-start(f32[8,5,16,16]{3,2,1,0:T(8,128)} %get-tuple-element.42), channel_id=1, source_target_pairs={{0,1},{1,2},{2,3},{3,4},{4,5},{5,6},{6,7},{8,9},{9,10},{10,11},{11... | collective-permute-start | bytes 122888 | tf_op jit(solution)/shard_map/ppermute | solution.py:15
  72.6 4.2 %collective-permute-start.13 = (f32[8,5,16,16]{3,2,1,0:T(8,128)}, f32[8,5,16,16]{3,2,1,0:T(8,128)}, u32[]{:S(2)}, u32[]{:S(2)}) collective-permute-start(f32[8,5,16,16]{3,2,1,0:T(8,128)} %get-tuple-element.43), channel_id=1, source_target_pairs={{1,0},{2,1},{3,2},{4,3},{5,4},{6,5},{7,6},{9,8},{10,9},{11,10},{12... | collective-permute-start | bytes 122888 | tf_op jit(solution)/shard_map/ppermute | solution.py:15
  76.8 1.9 %collective-permute-start.10 = (f32[8,5,1,256]{3,2,1,0:T(1,128)}, f32[8,5,1,256]{3,2,1,0:T(1,128)S(1)}, u32[]{:S(2)}, u32[]{:S(2)}) collective-permute-start(f32[8,5,1,256]{3,2,1,0:T(1,128)} %get-tuple-element.40), channel_id=1, source_target_pairs={{0,8},{8,16},{16,24},{1,9},{9,17},{17,25},{2,10},{10,18},{18,26},{... | collective-permute-start | bytes 122888 | tf_op jit(solution)/shard_map/ppermute | solution.py:23
  78.7 2.6 %collective-permute-start.11 = (f32[8,5,1,256]{3,2,1,0:T(1,128)}, f32[8,5,1,256]{3,2,1,0:T(1,128)S(1)}, u32[]{:S(2)}, u32[]{:S(2)}) collective-permute-start(f32[8,5,1,256]{3,2,1,0:T(1,128)} %get-tuple-element.41), channel_id=1, source_target_pairs={{8,0},{16,8},{24,16},{9,1},{17,9},{25,17},{10,2},{18,10},{26,18},{... | collective-permute-start | bytes 122888 | tf_op jit(solution)/shard_map/ppermute | solution.py:26
  82.1 3.5 %slice.216 = f32[4,5,16,16]{3,2,1,0:T(8,128)} slice(f32[4,5,16,256]{3,2,1,0:T(8,128)} %get-tuple-element.30), slice={[0:4:1], [0:5:1], [0:16:1], [15:256:16]} | slice | bytes 40960 | tf_op jit(solution)/shard_map/slice | solution.py:160
  85.6 2.5 %slice.210 = f32[4,5,16,16]{3,2,1,0:T(8,128)S(1)} slice(f32[4,5,16,256]{3,2,1,0:T(8,128)} %get-tuple-element.31), slice={[0:4:1], [0:5:1], [0:16:1], [0:256:16]} | slice | bytes 40960 | tf_op jit(solution)/shard_map/slice | solution.py:155
  88.1 2.4 %collective-permute-done.13 = f32[8,5,16,16]{3,2,1,0:T(8,128)} collective-permute-done((f32[8,5,16,16]{3,2,1,0:T(8,128)}, f32[8,5,16,16]{3,2,1,0:T(8,128)}, u32[]{:S(2)}, u32[]{:S(2)}) %collective-permute-start.13) | collective-permute-done | bytes 40992 | tf_op jit(solution)/shard_map/ppermute | solution.py:15
  91.1 4.1 %fusion.16 = (f32[1,1,8,5,16,256]{5,4,3,2,1,0:T(8,128)}, f32[8,5,16,256]{3,2,1,0:T(8,128)}, f32[8,5,16,256]{3,2,1,0:T(8,128)S(1)}) fusion(f32[8,5,16,16]{3,2,1,0:T(8,128)} %collective-permute-done.13, f32[8,5,16,240]{3,2,1,0:T(8,128)} %get-tuple-element.45, f32[8,5,16,240]{3,2,1,0:T(8,128)S(1)} %get-tuple-element.44, ...), kind=kLoop, calls=%fused_computation.40 | loop fusion | flops 3112960 | bytes 7291720 | tf_op jit(solution)/shard_map/broadcast_in_dim | solution.py:179
  108.8 3.0 %collective-permute-done.14 = f32[2,5,6,256]{3,0,1,2:T(2,128)S(1)} collective-permute-done((f32[2,5,6,256]{3,0,1,2:T(2,128)S(1)}, f32[2,5,6,256]{3,0,1,2:T(2,128)S(1)}, u32[]{:S(2)}, u32[]{:S(2)}) %collective-permute-start.14) | collective-permute-done | bytes 61472 | tf_op jit(solution)/shard_map/ppermute | solution.py:32
  (146 shorter events, 37.3 us)
Async XLA Ops:
  0.6 10.1 %copy-start.1 = (f32[1,1,8,5,16,256]{5,4,3,2,1,0:T(8,128)S(1)}, f32[1,1,8,5,16,256]{5,4,3,2,1,0:T(8,128)}, u32[]{:S(2)}) copy-start(f32[1,1,8,5,16,256]{5,4,3,2,1,0:T(8,128)} %param.8) | copy-start | bytes 1966084
  7.5 33.9 %collective-permute-start.2 = (f32[2,5,16,256]{3,2,1,0:T(8,128)S(1)}, f32[2,5,16,256]{3,2,1,0:T(8,128)S(1)}, u32[]{:S(2)}, u32[]{:S(2)}) collective-permute-start(f32[2,5,16,256]{3,2,1,0:T(8,128)S(1)} %broadcast_select_fusion.2), channel_id=1, source_target_pairs={{0,1},{1,2},{2,3},{3,4},{4,5},{5,6},{6,7},{7,8},{8,9},{9,10},{10,1... | collective-permute-start | bytes 491528 | tf_op jit(solution)/shard_map/ppermute | solution.py:15
  11.4 30.1 %collective-permute-start.3 = (f32[2,5,16,256]{3,2,1,0:T(8,128)S(1)}, f32[2,5,16,256]{3,2,1,0:T(8,128)S(1)}, u32[]{:S(2)}, u32[]{:S(2)}) collective-permute-start(f32[2,5,16,256]{3,2,1,0:T(8,128)S(1)} %broadcast_select_fusion.1), channel_id=1, source_target_pairs={{1,0},{2,1},{3,2},{4,3},{5,4},{6,5},{7,6},{8,7},{9,8},{10,9},{11,1... | collective-permute-start | bytes 491528 | tf_op jit(solution)/shard_map/ppermute | solution.py:15
  17.0 6.3 %copy-start.3 = (f32[1,1,8,5]{2,1,3,0:T(1,128)S(1)}, f32[1,1,8,5]{2,1,3,0:T(1,128)}, u32[]{:S(2)}) copy-start(f32[1,1,8,5]{2,1,3,0:T(1,128)} %param.9) | copy-start | bytes 484
  17.0 15.4 %collective-permute-start = (f32[2]{0:T(128)S(1)}, f32[2]{0:T(128)S(1)}, u32[]{:S(2)}, u32[]{:S(2)}) collective-permute-start(f32[2]{0:T(128)S(1)} %get-tuple-element.70), channel_id=1, source_target_pairs={{0,1},{1,2},{2,3},{3,4},{4,5},{5,6},{6,7},{7,8},{8,9},{9,10},{10,1... | collective-permute-start | bytes 32 | tf_op jit(solution)/shard_map/ppermute | solution.py:15
  19.4 14.9 %collective-permute-start.1 = (f32[2]{0:T(128)S(1)}, f32[2]{0:T(128)S(1)}, u32[]{:S(2)}, u32[]{:S(2)}) collective-permute-start(f32[2]{0:T(128)S(1)} %get-tuple-element.71), channel_id=1, source_target_pairs={{1,0},{2,1},{3,2},{4,3},{5,4},{6,5},{7,6},{8,7},{9,8},{10,9},{11,1... | collective-permute-start | bytes 32 | tf_op jit(solution)/shard_map/ppermute | solution.py:15
  24.1 10.6 %collective-permute-start.4 = (f32[2,5]{1,0:T(2,128)S(1)}, f32[2,5]{1,0:T(2,128)S(1)}, u32[]{:S(2)}, u32[]{:S(2)}) collective-permute-start(f32[2,5]{1,0:T(2,128)S(1)} %broadcast_select_fusion.5), channel_id=1, source_target_pairs={{0,1},{1,2},{2,3},{3,4},{4,5},{5,6},{6,7},{7,8},{8,9},{9,10},{10,1... | collective-permute-start | bytes 128 | tf_op jit(solution)/shard_map/ppermute | solution.py:15
  29.8 32.0 %copy-start.4 = (pred[256]{0:T(512)(128)(4,1)}, pred[256]{0:T(512)(128)(4,1)S(1)}, u32[]{:S(2)}) copy-start(pred[256]{0:T(512)(128)(4,1)S(1)} %get-tuple-element.73) | copy-start | bytes 772
  29.8 0.7 copy-start.7
  32.4 8.2 %collective-permute-start.5 = (f32[2,5]{1,0:T(2,128)S(1)}, f32[2,5]{1,0:T(2,128)S(1)}, u32[]{:S(2)}, u32[]{:S(2)}) collective-permute-start(f32[2,5]{1,0:T(2,128)S(1)} %broadcast_select_fusion.4), channel_id=1, source_target_pairs={{1,0},{2,1},{3,2},{4,3},{5,4},{6,5},{7,6},{8,7},{9,8},{10,9},{11,1... | collective-permute-start | bytes 128 | tf_op jit(solution)/shard_map/ppermute | solution.py:15
  43.7 13.8 %collective-permute-start.8 = (f32[8,5,16,16]{3,2,1,0:T(8,128)S(1)}, f32[8,5,16,16]{3,2,1,0:T(8,128)S(1)}, u32[]{:S(2)}, u32[]{:S(2)}) collective-permute-start(f32[8,5,16,16]{3,2,1,0:T(8,128)S(1)} %get-tuple-element.55), channel_id=1, source_target_pairs={{0,1},{1,2},{2,3},{3,4},{4,5},{5,6},{6,7},{8,9},{9,10},{10,11},{11... | collective-permute-start | bytes 122888 | tf_op jit(solution)/shard_map/ppermute | solution.py:15
  51.2 10.6 %collective-permute-start.9 = (f32[8,5,16,16]{3,2,1,0:T(8,128)S(1)}, f32[8,5,16,16]{3,2,1,0:T(8,128)S(1)}, u32[]{:S(2)}, u32[]{:S(2)}) collective-permute-start(f32[8,5,16,16]{3,2,1,0:T(8,128)S(1)} %get-tuple-element.54), channel_id=1, source_target_pairs={{1,0},{2,1},{3,2},{4,3},{5,4},{6,5},{7,6},{9,8},{10,9},{11,10},{12... | collective-permute-start | bytes 122888 | tf_op jit(solution)/shard_map/ppermute | solution.py:15
  53.1 8.6 %collective-permute-start.6 = (f32[8,5,1,256]{3,2,1,0:T(1,128)S(1)}, f32[8,5,1,256]{3,2,1,0:T(1,128)S(1)}, u32[]{:S(2)}, u32[]{:S(2)}) collective-permute-start(f32[8,5,1,256]{3,2,1,0:T(1,128)S(1)} %get-tuple-element.56), channel_id=1, source_target_pairs={{0,8},{8,16},{16,24},{1,9},{9,17},{17,25},{2,10},{10,18},{18,26},{... | collective-permute-start | bytes 122888 | tf_op jit(solution)/shard_map/ppermute | solution.py:23
  55.0 6.7 %collective-permute-start.7 = (f32[8,5,1,256]{3,2,1,0:T(1,128)S(1)}, f32[8,5,1,256]{3,2,1,0:T(1,128)S(1)}, u32[]{:S(2)}, u32[]{:S(2)}) collective-permute-start(f32[8,5,1,256]{3,2,1,0:T(1,128)S(1)} %get-tuple-element.57), channel_id=1, source_target_pairs={{8,0},{16,8},{24,16},{9,1},{17,9},{25,17},{10,2},{18,10},{26,18},{... | collective-permute-start | bytes 122888 | tf_op jit(solution)/shard_map/ppermute | solution.py:26
  70.6 17.4 %collective-permute-start.12 = (f32[8,5,16,16]{3,2,1,0:T(8,128)}, f32[8,5,16,16]{3,2,1,0:T(8,128)}, u32[]{:S(2)}, u32[]{:S(2)}) collective-permute-start(f32[8,5,16,16]{3,2,1,0:T(8,128)} %get-tuple-element.42), channel_id=1, source_target_pairs={{0,1},{1,2},{2,3},{3,4},{4,5},{5,6},{6,7},{8,9},{9,10},{10,11},{11... | collective-permute-start | bytes 122888 | tf_op jit(solution)/shard_map/ppermute | solution.py:15
  72.6 17.8 %collective-permute-start.13 = (f32[8,5,16,16]{3,2,1,0:T(8,128)}, f32[8,5,16,16]{3,2,1,0:T(8,128)}, u32[]{:S(2)}, u32[]{:S(2)}) collective-permute-start(f32[8,5,16,16]{3,2,1,0:T(8,128)} %get-tuple-element.43), channel_id=1, source_target_pairs={{1,0},{2,1},{3,2},{4,3},{5,4},{6,5},{7,6},{9,8},{10,9},{11,10},{12... | collective-permute-start | bytes 122888 | tf_op jit(solution)/shard_map/ppermute | solution.py:15
  76.8 13.6 %collective-permute-start.10 = (f32[8,5,1,256]{3,2,1,0:T(1,128)}, f32[8,5,1,256]{3,2,1,0:T(1,128)S(1)}, u32[]{:S(2)}, u32[]{:S(2)}) collective-permute-start(f32[8,5,1,256]{3,2,1,0:T(1,128)} %get-tuple-element.40), channel_id=1, source_target_pairs={{0,8},{8,16},{16,24},{1,9},{9,17},{17,25},{2,10},{10,18},{18,26},{... | collective-permute-start | bytes 122888 | tf_op jit(solution)/shard_map/ppermute | solution.py:23
  78.7 11.7 %collective-permute-start.11 = (f32[8,5,1,256]{3,2,1,0:T(1,128)}, f32[8,5,1,256]{3,2,1,0:T(1,128)S(1)}, u32[]{:S(2)}, u32[]{:S(2)}) collective-permute-start(f32[8,5,1,256]{3,2,1,0:T(1,128)} %get-tuple-element.41), channel_id=1, source_target_pairs={{8,0},{16,8},{24,16},{9,1},{17,9},{25,17},{10,2},{18,10},{26,18},{... | collective-permute-start | bytes 122888 | tf_op jit(solution)/shard_map/ppermute | solution.py:26
  90.5 0.7 copy-start.5
  95.3 1.1 copy-start.2
  96.3 0.7 copy-start.9
  98.1 1.1 copy-start
  108.7 3.1 %collective-permute-start.14 = (f32[2,5,6,256]{3,0,1,2:T(2,128)S(1)}, f32[2,5,6,256]{3,0,1,2:T(2,128)S(1)}, u32[]{:S(2)}, u32[]{:S(2)}) collective-permute-start(f32[2,5,6,256]{3,0,1,2:T(2,128)S(1)} %bitcast.133), channel_id=1, source_target_pairs={{0,1},{1,0},{2,3},{3,2},{4,5},{5,4},{6,7},{7,6},{8,9},{9,8},{10,11... | collective-permute-start | bytes 184328 | tf_op jit(solution)/shard_map/ppermute | solution.py:32
  112.0 2.5 %collective-permute-start.15 = (f32[5,6,256]{2,1,0:T(8,128)S(1)}, f32[5,6,256]{2,1,0:T(8,128)S(1)}, u32[]{:S(2)}, u32[]{:S(2)}) collective-permute-start(f32[5,6,256]{2,1,0:T(8,128)S(1)} %bitcast.134), channel_id=1, source_target_pairs={{0,8},{8,0},{16,24},{24,16},{1,9},{9,1},{17,25},{25,17},{2,10},{10... | collective-permute-start | bytes 92168 | tf_op jit(solution)/shard_map/ppermute | solution.py:32
  (2 other events, 1.2 us)
where the time goes:
time: 116 us; the launch traced here: 115 us
  starting transfers between devices  45.7 us (39%)
  local copies, waits for them, and re-layouts  33.5 us (29%)
  other arithmetic  18.1 us (16%)
  waiting for transfers between devices  16.5 us (14%)
  between operations  1.35 us (1%)
    ppermute x10, starting transfers between devices, from_behind(): lax.ppermute(value, axis, [(source, source + steps) for source in range(l...  35.2 us
    ppermute x10, waiting for transfers between devices, from_behind(): lax.ppermute(value, axis, [(source, source + steps) for source in range(l...  12.6 us
    ppermute x2, starting transfers between devices, padded_2(): lax.ppermute(lax.slice_in_dim(block, 0, width, axis=dim), axis, backward)  4.99 us
    slice x2, local copies, waits for them, and re-layouts, body(): first[1::2][..., E - 1::E]  4.39 us
    unnamed x28, local copies, waits for them, and re-layouts  4.24 us
    broadcast_in_dim x1, other arithmetic, body(): return (smoothed[None, None], total_reg[None, None])  4.11 us
    ppermute x2, waiting for transfers between devices, partner(): lax.ppermute(x, axis, [(i, i ^ 1 << apart) for i in range(lax.axis_size(a...  3.92 us
    ppermute x2, starting transfers between devices, padded_2(): lax.ppermute(lax.slice_in_dim(block, block.shape[dim] - width, None, axis...  3.84 us
  transfers between devices with their start and end apart: 16, of which 5 were waited for; matrix products, arithmetic and copies ran while one was open for 12% of the time, Pallas kernels for 0%

commit v1 on v0

v1 whole, which is shorter than its diff:
```python
import functools

import jax
import jax.numpy as jnp
from jax import lax
from jax.experimental import pallas as pl
from jax.experimental.pallas import tpu as pltpu
from jax.sharding import PartitionSpec as P

NC = 5
E = 16
BZ = 8
MOVE = 2
L = 128
F32 = jnp.float32
I32 = jnp.int32

PLANE = NC * BZ
FACE = 4 * PLANE
BOXROWS = NC * E
LABELS = MOVE * BOXROWS + MOVE * NC
PARCEL = 176

VM = pltpu.VMEM
SM = pltpu.SMEM


def call(kernel, ins, outs, scratch=(), aliases=None, flops=1000, **kw):
    given, in_specs = [], []
    for array, space in ins:
        if space == "vmem":
            given.append(pltpu.with_memory_space_constraint(array, VM))
            in_specs.append(pl.BlockSpec(memory_space=VM))
        elif space == "smem":
            given.append(array)
            in_specs.append(pl.BlockSpec(memory_space=SM))
        else:
            given.append(array)
            in_specs.append(pl.BlockSpec(memory_space=pl.ANY))
    shapes, out_specs = [], []
    for shape, space in outs:
        if space == "vmem":
            shapes.append(VM(shape, F32))
            out_specs.append(pl.BlockSpec(memory_space=VM))
        else:
            shapes.append(jax.ShapeDtypeStruct(shape, F32))
            out_specs.append(pl.BlockSpec(memory_space=VM))
    return pl.pallas_call(
        kernel,
        out_shape=shapes,
        in_specs=in_specs,
        out_specs=out_specs,
        scratch_shapes=list(scratch),
        input_output_aliases=aliases or {},
        cost_estimate=pl.CostEstimate(flops=flops, bytes_accessed=0, transcendentals=0),
        compiler_params=pltpu.CompilerParams(vmem_limit_bytes=24 * 1024 * 1024),
        **kw,
    )(*given)


def lanes():
    return lax.broadcasted_iota(I32, (BZ, L), 1)


def subs():
    return lax.broadcasted_iota(I32, (BZ, L), 0)


def rl(x, shift):
    shift %= L
    return x if shift == 0 else pltpu.roll(x, shift, 1)


def rs(x, shift):
    shift %= BZ
    return x if shift == 0 else pltpu.roll(x, shift, 0)


def pick_lanes(x, index):
    return jnp.take_along_axis(x, index, axis=1)


def place_of(mesh_shape):
    gx = lax.axis_index("gx")
    gy = lax.axis_index("gy")
    return gx, gy, gx * mesh_shape[1] + gy


def pack_kernel(shape, place_hbm, coeff_hbm, fields_hbm, boxes, even, odd, place, coeff, sem):
    big = pltpu.make_async_copy(fields_hbm.at[0, 0], boxes, sem.at[0])
    small = pltpu.make_async_copy(place_hbm, place, sem.at[1])
    other = pltpu.make_async_copy(coeff_hbm, coeff, sem.at[2])
    big.start()
    small.start()
    other.start()
    _, _, me = place_of(shape)
    ahead = 1 - 2 * (me % 2)
    small.wait()
    other.wait()
    chosen = []
    for out, owner in ((even, me + ahead), (odd, me - ahead)):
        count = jnp.int32(0)
        sources = [jnp.int32(0)] * MOVE
        labels = [jnp.int32(0)] * MOVE
        for s in range(BZ):
            value = place[0, 0, s]
            hit = value // BZ == owner
            for k in range(MOVE):
                taken = hit & (count == k)
                sources[k] = jnp.where(taken, s, sources[k])
                labels[k] = jnp.where(taken, value % BZ + 1, labels[k])
            count = count + hit.astype(I32)
        chosen.append(sources)
        out[LABELS + MOVE : PARCEL, :] = jnp.zeros((PARCEL - LABELS - MOVE, 2 * L), F32)
        for k in range(MOVE):
            out[LABELS + k : LABELS + k + 1, :] = jnp.full((1, 2 * L), labels[k].astype(F32), F32)
            for c in range(NC):
                row = MOVE * BOXROWS + k * NC + c
                out[row : row + 1, :] = jnp.full((1, 2 * L), coeff[0, 0, sources[k], c], F32)
    big.wait()
    for out, sources in zip((even, odd), chosen):
        for k in range(MOVE):
            for c in range(NC):
                row = (k * NC + c) * E
                out[row : row + E, :] = boxes[sources[k], c]


def stay_kernel(shape, place, coeff, mask, boxes, moved, rates, masks):
    _, _, me = place_of(shape)
    for s in range(BZ):
        value = place[0, 0, s]
        slot = value % BZ

        @pl.when(value // BZ == me)
        def _():
            for c in range(NC):
                for h in range(2):
                    moved[h, pl.ds(c * E * BZ + slot, E, stride=BZ), :] = boxes[s, c, :, h * L : h * L + L]
                rates[pl.ds(c * BZ + slot, 1), :] = jnp.full((1, L), coeff[0, 0, s, c], F32)

    for d in range(3):
        for s in range(BZ):
            masks[d * BZ + s : d * BZ + s + 1, :] = jnp.full((1, L), mask[0, 0, d, s].astype(F32), F32)


def arrivals(even, odd):
    sub = subs()
    found = []
    for parcel in (even, odd):
        for k in range(MOVE):
            label = parcel[LABELS + k : LABELS + k + 1, :L]
            found.append((parcel, k, label == (sub + 1).astype(F32)))
    return found


def merged(found, moved, c, x, h):
    row = (c * E + x) * BZ
    tile = moved[h, row : row + BZ, :]
    for parcel, k, hit in found:
        at = (k * NC + c) * E + x
        tile = jnp.where(hit, parcel[at : at + 1, h * L : h * L + L], tile)
    return tile


def plane_row(layer, h, c):
    return ((layer * 2 + h) * NC + c) * BZ


def xsend_kernel(shape, even, odd, moved, rates, core, link, all_rates):
    gx, _, _ = place_of(shape)
    first = gx % 2 == 0
    found = arrivals(even, odd)
    for c in range(NC):
        tile = rates[c * BZ : c * BZ + BZ, :]
        for parcel, k, hit in found:
            at = MOVE * BOXROWS + k * NC + c
            tile = jnp.where(hit, parcel[at : at + 1, :L], tile)
        all_rates[c * BZ : c * BZ + BZ, :] = tile
        core[FACE + c * BZ : FACE + c * BZ + BZ, :] = tile
        link[FACE + c * BZ : FACE + c * BZ + BZ, :] = tile
        for layer in range(2):
            for h in range(2):
                low = merged(found, moved, c, layer, h)
                high = merged(found, moved, c, E - 1 - layer, h)
                at = plane_row(layer, h, c)
                core[at : at + BZ, :] = jnp.where(first, high, low)
                link[at : at + BZ, :] = jnp.where(first, low, high)


def merge_kernel(shape, even, odd, moved, out, near, far):
    _, gy, _ = place_of(shape)
    first = gy % 2 == 0
    found = arrivals(even, odd)
    lane = lanes()
    for c in range(NC):
        low = [[None, None], [None, None]]
        high = [[None, None], [None, None]]
        for x in range(E):
            row = (c * E + x) * BZ
            at = L // 8 * (x % 8)
            here = lane // E == x % 8
            half = x // 8
            for h in range(2):
                tile = merged(found, moved, c, x, h)
                out[h, row : row + BZ, :] = tile
                for layer in range(2):
                    keep, start = ((low, E * layer) if h == 0 else (high, L - E - E * layer))
                    strip = rl(tile, at - start)
                    old = keep[layer][half]
                    keep[layer][half] = strip if old is None else jnp.where(here, strip, old)
        for layer in range(2):
            for h in range(2):
                at = plane_row(layer, h, c)
                near[at : at + BZ, :] = jnp.where(first, high[layer][h], low[layer][h])
                far[at : at + BZ, :] = jnp.where(first, low[layer][h], high[layer][h])


def ends(shape):
    gx, gy, _ = place_of(shape)
    x_first, y_first = gx % 2 == 0, gy % 2 == 0
    link_ok = jnp.where(x_first, gx > 0, gx < shape[0] - 1)
    far_ok = jnp.where(y_first, gy > 0, gy < shape[1] - 1)
    return x_first, y_first, link_ok, far_ok


def ysend_kernel(shape, core, link, rates, near, far, near_out, far_out):
    x_first, y_first, link_ok, _ = ends(shape)
    lane = lanes()
    near_out[:FACE, :] = near[...]
    far_out[:FACE, :] = far[...]
    for c in range(NC):
        lines = []
        for h in range(2):
            at = plane_row(0, h, c)
            a = core[at : at + BZ, :]
            b = jnp.where(link_ok, link[at : at + BZ, :], 0.0)
            lines.append((jnp.where(x_first, b, a), jnp.where(x_first, a, b)))
        rate = rates[c * BZ : c * BZ + BZ, :]
        bottom = jnp.where(lane < E, lines[0][0], rl(lines[0][1], E))
        top = jnp.where(lane < E, rl(lines[1][0], E), rl(lines[1][1], 2 * E))
        bottom = jnp.where(lane < 2 * E, bottom, rate)
        top = jnp.where(lane < 2 * E, top, rate)
        at = FACE + c * BZ
        near_out[at : at + BZ, :] = jnp.where(y_first, top, bottom)
        far_out[at : at + BZ, :] = jnp.where(y_first, bottom, top)


def z_parts(x, lane, sub, swap):
    z = lane % E
    down = jnp.where(sub == 0, 0.0, rs(x, 1))
    up = jnp.where(sub == BZ - 1, 0.0, rs(x, -1))
    ends_ = pick_lanes(jnp.where(z == E - 1, down, up), swap)
    return jnp.where(z == 0, ends_, rl(x, 1)) + jnp.where(z == E - 1, ends_, rl(x, -1))


def swap_index(lane):
    z = lane % E
    return jnp.where(z == 0, lane + E - 1, jnp.where(z == E - 1, lane - E + 1, lane))


def inner(pair, lane, sub, swap):
    a, b = pair
    a1, b1, a2, b2 = rl(a, E), rl(b, E), rl(a, -E), rl(b, -E)
    low, high = lane < E, lane >= L - E
    first = jnp.where(low, 0.0, a1) + jnp.where(high, b2, a2) + z_parts(a, lane, sub, swap)
    second = jnp.where(low, a1, b1) + jnp.where(high, 0.0, b2) + z_parts(b, lane, sub, swap)
    return first, second


def pair_at(ref, layer, c):
    return tuple(ref[plane_row(layer, h, c) : plane_row(layer, h, c) + BZ, :] for h in range(2))


def tile_at(ref, c, x):
    row = (c * E + x) * BZ
    return tuple(ref[h, row : row + BZ, :] for h in range(2))


def sweep_kernel(shape, moved, rates, core, link, core_sent, link_sent, out, core_first, link_first):
    x_first, _, link_ok, _ = ends(shape)
    lane, sub = lanes(), subs()
    swap = swap_index(lane)
    for c in range(NC):
        rate = rates[c * BZ : c * BZ + BZ, :]
        scale = 1.0 / (1.0 + 6.0 * rate)
        ghost = []
        for got, sent, kept, ok in ((core, core_sent, core_first, None), (link, link_sent, link_first, link_ok)):
            g0, g1, own = pair_at(got, 0, c), pair_at(got, 1, c), pair_at(sent, 0, c)
            g_rate = got[FACE + c * BZ : FACE + c * BZ + BZ, :]
            if ok is not None:
                g0, g1 = (tuple(jnp.where(ok, t, 0.0) for t in g) for g in (g0, g1))
                g_rate = jnp.where(ok, g_rate, 0.0)
            ghost.append(g0)
            g_scale = 1.0 / (1.0 + 6.0 * g_rate)
            sums = inner(g0, lane, sub, swap)
            for h in range(2):
                value = (g0[h] + g_rate * (sums[h] + g1[h] + own[h])) * g_scale
                if ok is not None:
                    value = jnp.where(ok, value, 0.0)
                row = (h * NC + c) * BZ
                kept[row : row + BZ, :] = value
        low = [jnp.where(x_first, b, a) for a, b in zip(*ghost)]
        high = [jnp.where(x_first, a, b) for a, b in zip(*ghost)]
        for x in range(E):
            here = tile_at(moved, c, x)
            before = low if x == 0 else tile_at(moved, c, x - 1)
            after = high if x == E - 1 else tile_at(moved, c, x + 1)
            sums = inner(here, lane, sub, swap)
            row = (c * E + x) * BZ
            for h in range(2):
                out[h, row : row + BZ, :] = (here[h] + rate * (sums[h] + before[h] + after[h])) * scale


def coarse_plane(pair, parity, lane, sub):
    sums = []
    for t in pair:
        t = t + rl(t, -1)
        sums.append(t + rl(t, -E))
    source = (lane // E % 4) * (2 * E) + 2 * (lane % 8)
    out = jnp.where(lane < L // 2, pick_lanes(sums[0], source), pick_lanes(sums[1], source))
    return jnp.where(lane % E // 8 == sub % 2, 0.25 * out, 0.0)


def flux_kernel(
    shape, partial, moved_rates, masks, core_first, link_first, near, far, near_sent, far_sent,
    first, x_core, x_link, y_near, y_far, kept, sent,
):
    x_first, y_first, link_ok, far_ok = ends(shape)
    gx, gy, _ = place_of(shape)
    par_x, par_y = gx % 2, gy % 2
    lane, sub = lanes(), subs()
    swap = swap_index(lane)
    upper = sub % 2 == 1
    z = lane % E
    low_lane, high_lane = lane < E, lane >= L - E
    for c in range(NC):
        rate = moved_rates[c * BZ : c * BZ + BZ, :]
        scale = 1.0 / (1.0 + 6.0 * rate)
        weight = rate * scale
        lines, ghost_r, ghost_f = [], [], []
        for got, sent_, kept_, ok in ((near, near_sent, y_near, None), (far, far_sent, y_far, far_ok)):
            g0, g1, own = pair_at(got, 0, c), pair_at(got, 1, c), pair_at(sent_, 0, c)
            extra = got[FACE + c * BZ : FACE + c * BZ + BZ, :]
            if ok is not None:
                g0, g1 = (tuple(jnp.where(ok, t, 0.0) for t in g) for g in (g0, g1))
                extra = jnp.where(ok, extra, 0.0)
            g_rate = jnp.where(lane < L // 2, rl(extra, L // 2), extra)
            g_scale = 1.0 / (1.0 + 6.0 * g_rate)
            sums = inner(g0, lane, sub, swap)
            line = (jnp.where(low_lane, extra, 0.0), jnp.where(high_lane, rl(extra, L - 2 * E), 0.0))
            first_g = []
            for h in range(2):
                value = (g0[h] + g_rate * (sums[h] + line[h] + g1[h] + own[h])) * g_scale
                if ok is not None:
                    value = jnp.where(ok, value, 0.0)
                row = (h * NC + c) * BZ
                kept_[row : row + BZ, :] = value
                first_g.append(value)
            lines.append(extra)
            ghost_r.append(g0)
            ghost_f.append(first_g)
        own, own1 = pair_at(far_sent, 0, c), pair_at(far_sent, 1, c)
        extra = far_sent[FACE + c * BZ : FACE + c * BZ + BZ, :]
        sums = inner(own, lane, sub, swap)
        line = (jnp.where(low_lane, extra, 0.0), jnp.where(high_lane, rl(extra, L - 2 * E), 0.0))
        flux_y = []
        for h in range(2):
            value = (own[h] + rate * (sums[h] + line[h] + own1[h] + ghost_r[1][h])) * scale
            flux_y.append(ghost_f[1][h] - value)
        low_r = [jnp.where(y_first, b, a) for a, b in zip(*ghost_r)]
        high_r = [jnp.where(y_first, a, b) for a, b in zip(*ghost_r)]
        low_line = jnp.where(y_first, lines[1], lines[0])
        high_line = jnp.where(y_first, lines[0], lines[1])
        for x in range(E):
            a, b = tile_at(partial, c, x)
            shift = E * (x % 8)
            a = a + weight * jnp.where(low_lane, rl(low_r[x // 8], -shift), 0.0)
            b = b + weight * jnp.where(high_lane, rl(high_r[x // 8], L - E - shift), 0.0)
            row = (c * E + x) * BZ
            first[0, row : row + BZ, :] = a
            first[1, row : row + BZ, :] = b
        planes = []
        for part, kept_, at_low, ok in ((core_first, x_core, ~x_first, None), (link_first, x_link, x_first, link_ok)):
            g_rate = kept_rate(part, c)
            g_weight = g_rate / (1.0 + 6.0 * g_rate)
            bottom = jnp.where(at_low, low_line, rl(low_line, -E))
            top = jnp.where(at_low, rl(high_line, L - E), rl(high_line, L - 2 * E))
            plane = []
            for h, (line_, there) in enumerate(((bottom, low_lane), (top, high_lane))):
                row = (h * NC + c) * BZ
                value = part[row : row + BZ, :] + g_weight * jnp.where(there, line_, 0.0)
                if ok is not None:
                    value = jnp.where(ok, value, 0.0)
                kept_[row : row + BZ, :] = value
                plane.append(value)
            planes.append(plane)
        flux_x = []
        for h in range(2):
            low = first[h, c * E * BZ : c * E * BZ + BZ, :]
            row = (c * E + E - 1) * BZ
            high = first[h, row : row + BZ, :]
            flux_x.append(planes[1][h] - jnp.where(x_first, low, high))
        faces_z = []
        for h in range(2):
            face = None
            for k in range(E // 2):
                row = (c * E + 2 * k) * BZ
                t = first[h, row : row + BZ, :] + first[h, row + BZ : row + 2 * BZ, :]
                down = jnp.where(sub == 0, 0.0, rs(t, 1))
                up = jnp.where(sub == BZ - 1, 0.0, rs(t, -1))
                high = rl(jnp.where(upper, t, down), 1 - E)
                d = high - jnp.where(upper, up, t)
                d = jnp.where(upper, -d, d)
                d = rl(d + rl(d, -E), k)
                face = d if face is None else jnp.where(z == k, d, face)
            faces_z.append(face)
        face_x = coarse_plane(flux_x, par_y, lane, sub) * (rate * masks[0:BZ, :])
        face_y = coarse_plane(flux_y, par_x, lane, sub) * (rate * masks[BZ : 2 * BZ, :])
        y8 = lane % 8
        source = (y8 % 4) * (2 * E) + lane // E
        face_z = jnp.where(y8 < 4, pick_lanes(faces_z[0], source), pick_lanes(faces_z[1], source))
        face_z = jnp.where(z // 8 == par_y, face_z, 0.0) * (0.25 * rate * masks[2 * BZ :, :])
        face_x = face_x + rs(face_x, -1)
        face_y = face_y + rs(face_y, 1)
        for h in range(2):
            sides = jnp.where(upper, jnp.where(par_x == h, face_y, 0.0), jnp.where(par_y == h, face_x, 0.0))
            tops = jnp.where(par_x == h, face_z, 0.0)
            left = sub % 4 < 2
            columns = (
                jnp.where(left, sides, rs(tops, 2)),
                jnp.where(left, rs(sides, -2), tops),
            )
            row = (h * NC + c) * BZ
            kept[row : row + BZ, :] = jnp.where(y_first, columns[0], columns[1])
            sent[row : row + BZ, :] = jnp.where(y_first, columns[1], columns[0])


def kept_rate(part, c):
    return part[2 * PLANE + c * BZ : 2 * PLANE + c * BZ + BZ, :]


def half_kernel(shape, kept, got, mine, sent):
    gx, _, _ = place_of(shape)
    first = gx % 2 == 0
    top = subs() < 4
    for i in range(2 * NC):
        a, b = kept[i * BZ : i * BZ + BZ, :], got[i * BZ : i * BZ + BZ, :]
        rows = (jnp.where(top, a, rs(b, 4)), jnp.where(top, rs(a, 4), b))
        mine[i * BZ : i * BZ + BZ, :] = jnp.where(first, rows[0], rows[1])
        sent[i * BZ : i * BZ + BZ, :] = jnp.where(first, rows[1], rows[0])


def register_kernel(shape, mine, got, out):
    x_first, y_first, _, _ = ends(shape)
    sub = subs()
    for h in range(2):
        for c in range(NC):
            row = (h * NC + c) * BZ
            m, g = mine[row : row + BZ, :], got[row : row + BZ, :]
            a, b = m + rs(m, 4), g + rs(g, 4)
            s = m + g
            ab = a + b
            x0, x1 = jnp.where(x_first, a, b), jnp.where(x_first, b, a)
            y0, y1 = jnp.where(y_first, rs(s, 1), rs(s, 5)), jnp.where(y_first, rs(s, 5), rs(s, 1))
            t = jnp.where(sub == 0, x0, jnp.where(sub == 1, rs(x1, 1), rs(ab, 2)))
            t = jnp.where(sub == 2, y0, jnp.where(sub == 3, rs(y1, 1), t))
            out[0, 0, c, :, h * L : h * L + L] = t[:6]


def smooth_kernel(shape, moved, rates, first, x_core, x_link, y_near, y_far, out, held):
    x_first, y_first, _, _ = ends(shape)
    lane, sub = lanes(), subs()
    swap = swap_index(lane)
    low_lane, high_lane = lane < E, lane >= L - E
    for c in range(NC):
        rate = rates[c * BZ : c * BZ + BZ, :]
        scale = 1.0 / (1.0 + 6.0 * rate)

        def ghosts(a_ref, b_ref, a_first):
            a, b = (tuple(ref[(h * NC + c) * BZ : (h * NC + c + 1) * BZ, :] for h in range(2)) for ref in (a_ref, b_ref))
            low = [jnp.where(a_first, q, p) for p, q in zip(a, b)]
            high = [jnp.where(a_first, p, q) for p, q in zip(a, b)]
            return low, high

        low, high = ghosts(x_core, x_link, x_first)
        low_y, high_y = ghosts(y_near, y_far, y_first)
        for x in range(E):
            here = tile_at(first, c, x)
            before = low if x == 0 else tile_at(first, c, x - 1)
            after = high if x == E - 1 else tile_at(first, c, x + 1)
            sums = inner(here, lane, sub, swap)
            shift = E * (x % 8)
            edge = (
                jnp.where(low_lane, rl(low_y[x // 8], -shift), 0.0),
                jnp.where(high_lane, rl(high_y[x // 8], L - E - shift), 0.0),
            )
            start = tile_at(moved, c, x)
            row = (c * E + x) * BZ
            for h in range(2):
                held[h, row : row + BZ, :] = (start[h] + rate * (sums[h] + before[h] + after[h] + edge[h])) * scale
        for s in range(BZ):
            for h in range(2):
                out[0, 0, s, c, :, h * L : h * L + L] = held[h, pl.ds(c * E * BZ + s, E, stride=BZ), :]


def body(shape, fields_old, coeff_old, new_place, cf_mask):
    rows, columns = shape
    count = rows * columns
    both = ("gx", "gy")

    def swap(array, pairs):
        return lax.ppermute(array, both, pairs)

    even_pairs = [(i, i ^ 1) for i in range(count)]
    odd_pairs = [(i, (i + 1) % count if i % 2 else (i - 1) % count) for i in range(count)]
    at = lambda a, b: a * columns + b
    core_pairs = [(at(a, b), at(a ^ 1, b)) for a in range(rows) for b in range(columns)]
    link_pairs = [
        (at(a, b), at((a + 1) % rows if a % 2 else (a - 1) % rows, b)) for a in range(rows) for b in range(columns)
    ]
    far_pairs = [
        (at(a, b), at(a ^ 1, b) if b in (0, columns - 1) else at(a, b + 1 if b % 2 else b - 1))
        for a in range(rows)
        for b in range(columns)
    ]
    k = lambda f: functools.partial(f, shape)
    big = (2, NC * E * BZ, L)

    boxes, even, odd = call(
        k(pack_kernel),
        [(new_place, "any"), (coeff_old, "any"), (fields_old, "any")],
        [((BZ, NC, E, 2 * L), "vmem"), ((PARCEL, 2 * L), "vmem"), ((PARCEL, 2 * L), "vmem")],
        [SM((1, 1, BZ), I32), SM((1, 1, BZ, NC), F32), pltpu.SemaphoreType.DMA((3,))],
    )
    odd_got = swap(odd, odd_pairs)
    even_got = swap(even, even_pairs)
    stayed, rates, masks = call(
        k(stay_kernel),
        [(new_place, "smem"), (coeff_old, "smem"), (cf_mask, "smem"), (boxes, "vmem")],
        [(big, "vmem"), ((PLANE, L), "vmem"), ((3 * BZ, L), "vmem")],
    )
    core, link, rates = call(
        k(xsend_kernel),
        [(even_got, "vmem"), (odd_got, "vmem"), (stayed, "vmem"), (rates, "vmem")],
        [((FACE + PLANE, L), "vmem"), ((FACE + PLANE, L), "vmem"), ((PLANE, L), "vmem")],
    )
    link_got = swap(link, link_pairs)
    core_got = swap(core, core_pairs)
    moved, near, far = call(
        k(merge_kernel),
        [(even_got, "vmem"), (odd_got, "vmem"), (stayed, "vmem")],
        [(big, "vmem"), ((FACE, L), "vmem"), ((FACE, L), "vmem")],
    )
    near, far = call(
        k(ysend_kernel),
        [(core_got, "vmem"), (link_got, "vmem"), (rates, "vmem"), (near, "vmem"), (far, "vmem")],
        [((FACE + PLANE, L), "vmem"), ((FACE + PLANE, L), "vmem")],
    )
    far_got = swap(far, far_pairs)
    near_got = swap(near, even_pairs)
    part, core_first, link_first = call(
        k(sweep_kernel_with_rates),
        [(a, "vmem") for a in (moved, rates, core_got, link_got, core, link)],
        [(big, "vmem"), ((3 * PLANE, L), "vmem"), ((3 * PLANE, L), "vmem")],
    )
    plane = ((2 * PLANE, L), "vmem")
    first, x_core, x_link, y_near, y_far, kept, sent = call(
        k(flux_kernel),
        [(a, "vmem") for a in (part, rates, masks, core_first, link_first, near_got, far_got, near, far)],
        [(big, "vmem"), plane, plane, plane, plane, plane, plane],
    )
    got = swap(sent, even_pairs)
    (smoothed,) = call(
        k(smooth_kernel),
        [(a, "vmem") for a in (moved, rates, first, x_core, x_link, y_near, y_far)],
        [((1, 1, BZ, NC, E, 2 * L), "out")],
        [VM(big, F32)],
    )
    mine, sent = call(k(half_kernel), [(kept, "vmem"), (got, "vmem")], [plane, plane])
    got = swap(sent, core_pairs)
    (registers,) = call(k(register_kernel), [(mine, "vmem"), (got, "vmem")], [((1, 1, NC, 6, 2 * L), "out")])
    return smoothed, registers


def sweep_kernel_with_rates(shape, moved, rates, core, link, core_sent, link_sent, out, core_first, link_first):
    sweep_kernel(shape, moved, rates, core, link, core_sent, link_sent, out, core_first, link_first)
    _, _, link_ok, _ = ends(shape)
    core_first[2 * PLANE :, :] = core[FACE:, :]
    link_first[2 * PLANE :, :] = jnp.where(link_ok, link[FACE:, :], 0.0)


def solution(mesh):
    shape = (mesh.shape["gx"], mesh.shape["gy"])
    return jax.shard_map(
        functools.partial(body, shape),
        mesh=mesh,
        in_specs=(
            P("gx", "gy", None, None, None, None),
            P("gx", "gy", None, None),
            P("gx", "gy", None),
            P("gx", "gy", None, None),
        ),
        out_specs=(P("gx", "gy", None, None, None, None), P("gx", "gy", None, None, None)),
        check_vma=False,
    )
```

time: 116 us -> 38.5 us (0.33)
  the two profiles are of different devices: /device:TPU:25 before, /device:TPU:0 now
where the time goes in v1:
time: 38.5 us; the launch traced here: 38.3 us
  waiting for transfers between devices  14.5 us (38%)
  starting transfers between devices  11.2 us (29%)
  Pallas kernels  9.37 us (24%)
  local copies, waits for them, and re-layouts  2.51 us (7%)
  between operations  0.75 us (2%)
    ppermute x8, waiting for transfers between devices, swap(): return lax.ppermute(array, both, pairs)  14.5 us
    ppermute x8, starting transfers between devices, swap(): return lax.ppermute(array, both, pairs)  11.2 us
    pallas_call x10, Pallas kernels, call(): pl.pallas_call(kernel, out_shape=shapes, in_specs=in_specs, out_specs=out...  9.37 us
    unnamed x9, local copies, waits for them, and re-layouts  2.51 us
  transfers between devices with their start and end apart: 8, of which 5 were waited for; matrix products, arithmetic and copies ran while one was open for 0% of the time, Pallas kernels for 11%

profile of v1, /device:TPU:0, one launch (start us, length us, event | category | flops | bytes accessed | tf_op | source)
XLA Modules:
  0.0 38.3 jit_solution(15831191521937613712)
XLA Ops:
  0.6 0.8 %copy.6.coeff_hbm.coeff = f32[1,1,8,5]{3,2,1,0:T(8,128)S(1)} copy(f32[1,1,8,5]{2,1,3,0:T(1,128)} %param.5) | data formatting | bytes 320 | tf_op args[1]
  1.4 1.1 %copy-done = f32[1,1,8,5,16,256]{5,4,3,2,1,0:T(8,128)S(1)} copy-done((f32[1,1,8,5,16,256]{5,4,3,2,1,0:T(8,128)S(1)}, f32[1,1,8,5,16,256]{5,4,3,2,1,0:T(8,128)}, u32[]{:S(2)}) %copy-start) | copy-done | bytes 655384
  2.5 1.0 %shard_map.59 = (f32[8,5,16,256]{3,2,1,0:T(8,128)S(1)}, f32[176,256]{1,0:T(8,128)S(1)}, f32[176,256]{1,0:T(8,128)S(1)}) custom-call(s32[1,1,8]{2,1,0:T(1,128)S(1)} %copy-done.1, f32[1,1,8,5]{3,2,1,0:T(8,128)S(1)} %copy.6.coeff_hbm.coeff, f32[1,1,8,5,16,256]{5,4,3,2,1,0:T(8,128)S(1)} %copy-done), custom_call_target="tpu_custom_call" | custom-call | flops 1000 | tf_op jit(solution)/shard_map/pallas_call | solution.py:48
  3.5 3.0 %collective-permute-start = (f32[176,256]{1,0:T(8,128)S(1)}, f32[176,256]{1,0:T(8,128)S(1)}, u32[]{:S(2)}, u32[]{:S(2)}) collective-permute-start(f32[176,256]{1,0:T(8,128)S(1)} %get-tuple-element.28), channel_id=1, source_target_pairs={{0,1},{1,0},{2,3},{3,2},{4,5},{5,4},{6,7},{7,6},{8,9},{9,8},{10,11... | collective-permute-start | bytes 540680 | tf_op jit(solution)/shard_map/ppermute | solution.py:512
  6.5 3.6 %collective-permute-start.1 = (f32[176,256]{1,0:T(8,128)S(1)}, f32[176,256]{1,0:T(8,128)S(1)}, u32[]{:S(2)}, u32[]{:S(2)}) collective-permute-start(f32[176,256]{1,0:T(8,128)S(1)} %get-tuple-element.29), channel_id=1, source_target_pairs={{0,31},{1,2},{2,1},{3,4},{4,3},{5,6},{6,5},{7,8},{8,7},{9,10},{10,... | collective-permute-start | bytes 540680 | tf_op jit(solution)/shard_map/ppermute | solution.py:512
  10.2 0.8 %shard_map.60 = (f32[2,640,128]{2,1,0:T(8,128)S(1)}, f32[40,128]{1,0:T(8,128)S(1)}, f32[24,128]{1,0:T(8,128)S(1)}) custom-call(s32[1,1,8]{2,1,0:T(1,128)S(1)} %copy-done.1, f32[1,1,8,5]{3,2,1,0:T(8,128)S(1)} %copy.6.coeff_hbm.coeff, s32[1,1,3,8]{3,2,1,0:T(4,128)S(1)} %copy.8.mask, f32[8,5,16,256]{3,2,1,0:T(8,128)S(1)} %get-tuple-element.30.boxes), custom_call_target="tpu_custom_call" | custom-call | flops 1000 | tf_op jit(solution)/shard_map/pallas_call | solution.py:48
  11.0 3.2 %collective-permute-done.even = f32[176,256]{1,0:T(8,128)S(1)} collective-permute-done((f32[176,256]{1,0:T(8,128)S(1)}, f32[176,256]{1,0:T(8,128)S(1)}, u32[]{:S(2)}, u32[]{:S(2)}) %collective-permute-start) | collective-permute-done | bytes 180256 | tf_op jit(solution)/shard_map/ppermute | solution.py:512
  14.2 2.5 %collective-permute-done.1.odd = f32[176,256]{1,0:T(8,128)S(1)} collective-permute-done((f32[176,256]{1,0:T(8,128)S(1)}, f32[176,256]{1,0:T(8,128)S(1)}, u32[]{:S(2)}, u32[]{:S(2)}) %collective-permute-start.1) | collective-permute-done | bytes 180256 | tf_op jit(solution)/shard_map/ppermute | solution.py:512
  16.7 0.1 shard_map.62
  16.8 0.1 collective-permute-start.2
  16.9 1.2 %collective-permute-start.3 = (f32[200,128]{1,0:T(8,128)S(1)}, f32[200,128]{1,0:T(8,128)S(1)}, u32[]{:S(2)}, u32[]{:S(2)}) collective-permute-start(f32[200,128]{1,0:T(8,128)S(1)} %get-tuple-element.36.link_sent), channel_id=1, source_target_pairs={{0,24},{1,25},{2,26},{3,27},{4,28},{5,29},{6,30},{7,31},{8,16},{9,... | collective-permute-start | bytes 307208 | tf_op jit(solution)/shard_map/ppermute | solution.py:512
  18.0 0.4 %shard_map.61 = (f32[2,640,128]{2,1,0:T(8,128)S(1)}, f32[160,128]{1,0:T(8,128)S(1)}, f32[160,128]{1,0:T(8,128)S(1)}) custom-call(f32[176,256]{1,0:T(8,128)S(1)} %collective-permute-done.even, f32[176,256]{1,0:T(8,128)S(1)} %collective-permute-done.1.odd, f32[2,640,128]{2,1,0:T(8,128)S(1)} %get-tuple-element.31.moved), custom_call_target="tpu_custom_call" | custom-call | flops 1000 | tf_op jit(solution)/shard_map/pallas_call | solution.py:48
  18.5 3.1 %collective-permute-done.3.link = f32[200,128]{1,0:T(8,128)S(1)} collective-permute-done((f32[200,128]{1,0:T(8,128)S(1)}, f32[200,128]{1,0:T(8,128)S(1)}, u32[]{:S(2)}, u32[]{:S(2)}) %collective-permute-start.3) | collective-permute-done | bytes 102432 | tf_op jit(solution)/shard_map/ppermute | solution.py:512
  21.5 0.1 shard_map.64
  21.6 0.1 collective-permute-start.4
  21.7 0.5 %collective-permute-start.5 = (f32[200,128]{1,0:T(8,128)S(1)}, f32[200,128]{1,0:T(8,128)S(1)}, u32[]{:S(2)}, u32[]{:S(2)}) collective-permute-start(f32[200,128]{1,0:T(8,128)S(1)} %get-tuple-element.44.far_sent), channel_id=1, source_target_pairs={{0,8},{1,2},{2,1},{3,4},{4,3},{5,6},{6,5},{7,15},{8,0},{9,10},{10,... | collective-permute-start | bytes 307208 | tf_op jit(solution)/shard_map/ppermute | solution.py:512
  22.2 1.0 %shard_map.63 = (f32[2,640,128]{2,1,0:T(8,128)S(1)}, f32[120,128]{1,0:T(8,128)S(1)}, f32[120,128]{1,0:T(8,128)S(1)}) custom-call(f32[2,640,128]{2,1,0:T(8,128)S(1)} %get-tuple-element.32.moved, f32[40,128]{1,0:T(8,128)S(1)} %get-tuple-element.34.rates.moved_rates, f32[200,128]{1,0:T(8,128)S(1)} %collective-permute-done.2.core, ...), custom_call_target="tpu_custom_call" | custom-call | flops 1000 | tf_op jit(solution)/shard_map/pallas_call | solution.py:48
  23.2 3.7 %collective-permute-done.4.near = f32[200,128]{1,0:T(8,128)S(1)} collective-permute-done((f32[200,128]{1,0:T(8,128)S(1)}, f32[200,128]{1,0:T(8,128)S(1)}, u32[]{:S(2)}, u32[]{:S(2)}) %collective-permute-start.4) | collective-permute-done | bytes 102432 | tf_op jit(solution)/shard_map/ppermute | solution.py:512
  26.9 4.0 %shard_map.65 = (f32[2,640,128]{2,1,0:T(8,128)S(1)}, f32[80,128]{1,0:T(8,128)S(1)}, f32[80,128]{1,0:T(8,128)S(1)}, f32[80,128]{1,0:T(8,128)S(1)}, f32[80,128]{1,...) custom-call(f32[2,640,128]{2,1,0:T(8,128)S(1)} %get-tuple-element.37.partial, ...), custom_call_target="tpu_custom_call" | custom-call | flops 1000 | tf_op jit(solution)/shard_map/pallas_call | solution.py:48
  30.9 2.7 %collective-permute-start.6 = (f32[80,128]{1,0:T(8,128)S(1)}, f32[80,128]{1,0:T(8,128)S(1)}, u32[]{:S(2)}, u32[]{:S(2)}) collective-permute-start(f32[80,128]{1,0:T(8,128)S(1)} %get-tuple-element.51), channel_id=1, source_target_pairs={{0,1},{1,0},{2,3},{3,2},{4,5},{5,4},{6,7},{7,6},{8,9},{9,8},{10,11... | collective-permute-start | bytes 122888 | tf_op jit(solution)/shard_map/ppermute | solution.py:512
  33.6 2.0 %collective-permute-done.6.got = f32[80,128]{1,0:T(8,128)S(1)} collective-permute-done((f32[80,128]{1,0:T(8,128)S(1)}, f32[80,128]{1,0:T(8,128)S(1)}, u32[]{:S(2)}, u32[]{:S(2)}) %collective-permute-start.6) | collective-permute-done | bytes 40992 | tf_op jit(solution)/shard_map/ppermute | solution.py:512
  35.6 0.1 collective-permute-start.7
  35.7 1.9 %shard_map.66 = f32[1,1,8,5,16,256]{5,4,3,2,1,0:T(8,128)} custom-call(f32[2,640,128]{2,1,0:T(8,128)S(1)} %get-tuple-element.32.moved, f32[40,128]{1,0:T(8,128)S(1)} %get-tuple-element.34.rates.moved_rates, f32[2,640,128]{2,1,0:T(8,128)S(1)} %get-tuple-element.45.first, f32[80,128]{1,0:T(8,128)S(1)} %get-tuple-element.46.x_core, ...), custom_call_target="tpu_custom_call" | custom-call | flops 1000 | tf_op jit(solution)/shard_map/pallas_call | solution.py:48
  37.7 0.6 %copy.9 = f32[1,1,5,6,256]{4,1,3,2,0:T(1,128)} copy(f32[1,1,5,6,256]{4,3,2,1,0:T(8,128)S(1)} %shard_map.68) | data formatting | bytes 61440
  (11 shorter events, 0.1 us)
Async XLA Ops:
  0.6 0.8 %copy-start.1 = (s32[1,1,8]{2,1,0:T(1,128)S(1)}, s32[1,1,8]{2,1,0:T(1,128)}, u32[]{:S(2)}) copy-start(s32[1,1,8]{2,1,0:T(1,128)} %place.1) | copy-start | bytes 100
  1.4 1.1 %copy-start = (f32[1,1,8,5,16,256]{5,4,3,2,1,0:T(8,128)S(1)}, f32[1,1,8,5,16,256]{5,4,3,2,1,0:T(8,128)}, u32[]{:S(2)}) copy-start(f32[1,1,8,5,16,256]{5,4,3,2,1,0:T(8,128)} %fields_hbm.1) | copy-start | bytes 1966084
  3.5 6.7 %copy-start.2 = (s32[1,1,3,8]{3,1,2,0:T(1,128)S(1)}, s32[1,1,3,8]{3,1,2,0:T(1,128)}, u32[]{:S(2)}) copy-start(s32[1,1,3,8]{3,1,2,0:T(1,128)} %param.7) | copy-start | bytes 292
  3.5 10.7 %collective-permute-start = (f32[176,256]{1,0:T(8,128)S(1)}, f32[176,256]{1,0:T(8,128)S(1)}, u32[]{:S(2)}, u32[]{:S(2)}) collective-permute-start(f32[176,256]{1,0:T(8,128)S(1)} %get-tuple-element.28), channel_id=1, source_target_pairs={{0,1},{1,0},{2,3},{3,2},{4,5},{5,4},{6,7},{7,6},{8,9},{9,8},{10,11... | collective-permute-start | bytes 540680 | tf_op jit(solution)/shard_map/ppermute | solution.py:512
  6.5 10.2 %collective-permute-start.1 = (f32[176,256]{1,0:T(8,128)S(1)}, f32[176,256]{1,0:T(8,128)S(1)}, u32[]{:S(2)}, u32[]{:S(2)}) collective-permute-start(f32[176,256]{1,0:T(8,128)S(1)} %get-tuple-element.29), channel_id=1, source_target_pairs={{0,31},{1,2},{2,1},{3,4},{4,3},{5,6},{6,5},{7,8},{8,7},{9,10},{10,... | collective-permute-start | bytes 540680 | tf_op jit(solution)/shard_map/ppermute | solution.py:512
  16.8 1.7 %collective-permute-start.2 = (f32[200,128]{1,0:T(8,128)S(1)}, f32[200,128]{1,0:T(8,128)S(1)}, u32[]{:S(2)}, u32[]{:S(2)}) collective-permute-start(f32[200,128]{1,0:T(8,128)S(1)} %get-tuple-element.35.core_sent), channel_id=1, source_target_pairs={{0,8},{1,9},{2,10},{3,11},{4,12},{5,13},{6,14},{7,15},{8,0},{9,1},... | collective-permute-start | bytes 307208 | tf_op jit(solution)/shard_map/ppermute | solution.py:512
  16.9 4.7 %collective-permute-start.3 = (f32[200,128]{1,0:T(8,128)S(1)}, f32[200,128]{1,0:T(8,128)S(1)}, u32[]{:S(2)}, u32[]{:S(2)}) collective-permute-start(f32[200,128]{1,0:T(8,128)S(1)} %get-tuple-element.36.link_sent), channel_id=1, source_target_pairs={{0,24},{1,25},{2,26},{3,27},{4,28},{5,29},{6,30},{7,31},{8,16},{9,... | collective-permute-start | bytes 307208 | tf_op jit(solution)/shard_map/ppermute | solution.py:512
  21.6 5.2 %collective-permute-start.4 = (f32[200,128]{1,0:T(8,128)S(1)}, f32[200,128]{1,0:T(8,128)S(1)}, u32[]{:S(2)}, u32[]{:S(2)}) collective-permute-start(f32[200,128]{1,0:T(8,128)S(1)} %get-tuple-element.43.near_sent), channel_id=1, source_target_pairs={{0,1},{1,0},{2,3},{3,2},{4,5},{5,4},{6,7},{7,6},{8,9},{9,8},{10,11... | collective-permute-start | bytes 307208 | tf_op jit(solution)/shard_map/ppermute | solution.py:512
  21.7 5.2 %collective-permute-start.5 = (f32[200,128]{1,0:T(8,128)S(1)}, f32[200,128]{1,0:T(8,128)S(1)}, u32[]{:S(2)}, u32[]{:S(2)}) collective-permute-start(f32[200,128]{1,0:T(8,128)S(1)} %get-tuple-element.44.far_sent), channel_id=1, source_target_pairs={{0,8},{1,2},{2,1},{3,4},{4,3},{5,6},{6,5},{7,15},{8,0},{9,10},{10,... | collective-permute-start | bytes 307208 | tf_op jit(solution)/shard_map/ppermute | solution.py:512
  30.9 4.7 %collective-permute-start.6 = (f32[80,128]{1,0:T(8,128)S(1)}, f32[80,128]{1,0:T(8,128)S(1)}, u32[]{:S(2)}, u32[]{:S(2)}) collective-permute-start(f32[80,128]{1,0:T(8,128)S(1)} %get-tuple-element.51), channel_id=1, source_target_pairs={{0,1},{1,0},{2,3},{3,2},{4,5},{5,4},{6,7},{7,6},{8,9},{9,8},{10,11... | collective-permute-start | bytes 122888 | tf_op jit(solution)/shard_map/ppermute | solution.py:512
  35.6 2.0 %collective-permute-start.7 = (f32[80,128]{1,0:T(8,128)S(1)}, f32[80,128]{1,0:T(8,128)S(1)}, u32[]{:S(2)}, u32[]{:S(2)}) collective-permute-start(f32[80,128]{1,0:T(8,128)S(1)} %get-tuple-element.53), channel_id=1, source_target_pairs={{0,8},{1,9},{2,10},{3,11},{4,12},{5,13},{6,14},{7,15},{8,0},{9,1},... | collective-permute-start | bytes 122888 | tf_op jit(solution)/shard_map/ppermute | solution.py:512

commit v2 on v1

--- a/solution.py
+++ b/solution.py
@@ -35,8 +35,8 @@
             given.append(array)
             in_specs.append(pl.BlockSpec(memory_space=SM))
         else:
-            given.append(array)
-            in_specs.append(pl.BlockSpec(memory_space=pl.ANY))
+            given.append(pltpu.with_memory_space_constraint(array, pltpu.HBM))
+            in_specs.append(pl.BlockSpec(memory_space=pltpu.HBM))
     shapes, out_specs = [], []
     for shape, space in outs:
         if space == "vmem":
@@ -116,7 +116,7 @@
             out[LABELS + k : LABELS + k + 1, :] = jnp.full((1, 2 * L), labels[k].astype(F32), F32)
             for c in range(NC):
                 row = MOVE * BOXROWS + k * NC + c
-                out[row : row + 1, :] = jnp.full((1, 2 * L), coeff[0, 0, sources[k], c], F32)
+                out[row : row + 1, :] = jnp.full((1, 2 * L), coeff[0, c, 0, sources[k]], F32)
     big.wait()
     for out, sources in zip((even, odd), chosen):
         for k in range(MOVE):
@@ -136,11 +136,11 @@
             for c in range(NC):
                 for h in range(2):
                     moved[h, pl.ds(c * E * BZ + slot, E, stride=BZ), :] = boxes[s, c, :, h * L : h * L + L]
-                rates[pl.ds(c * BZ + slot, 1), :] = jnp.full((1, L), coeff[0, 0, s, c], F32)
+                rates[pl.ds(c * BZ + slot, 1), :] = jnp.full((1, L), coeff[0, c, 0, s], F32)
 
     for d in range(3):
         for s in range(BZ):
-            masks[d * BZ + s : d * BZ + s + 1, :] = jnp.full((1, L), mask[0, 0, d, s].astype(F32), F32)
+            masks[d * BZ + s : d * BZ + s + 1, :] = jnp.full((1, L), mask[0, d, 0, s].astype(F32), F32)
 
 
 def arrivals(even, odd):
@@ -276,10 +276,22 @@
     return tuple(ref[h, row : row + BZ, :] for h in range(2))
 
 
-def sweep_kernel(shape, moved, rates, core, link, core_sent, link_sent, out, core_first, link_first):
+def z_differences(tiles, sub, upper):
+    down = [jnp.where(sub == 0, 0.0, t) for t in [rs(t, 1) for t in tiles]]
+    up = [jnp.where(sub == BZ - 1, 0.0, t) for t in [rs(t, -1) for t in tiles]]
+    high = [rl(t, 1 - E) for t in [jnp.where(upper, t, d) for t, d in zip(tiles, down)]]
+    return [jnp.where(upper, u - g, g - t) for g, u, t in zip(high, up, tiles)]
+
+
+def sweep_kernel(shape, moved, rates, core, link, core_sent, link_sent, out, core_first, link_first, tops):
     x_first, _, link_ok, _ = ends(shape)
+    _, gy, _ = place_of(shape)
     lane, sub = lanes(), subs()
     swap = swap_index(lane)
+    upper = sub % 2 == 1
+    z = lane % E
+    core_first[2 * PLANE :, :] = core[FACE:, :]
+    link_first[2 * PLANE :, :] = jnp.where(link_ok, link[FACE:, :], 0.0)
     for c in range(NC):
         rate = rates[c * BZ : c * BZ + BZ, :]
         scale = 1.0 / (1.0 + 6.0 * rate)
@@ -309,6 +321,23 @@
             row = (c * E + x) * BZ
             for h in range(2):
                 out[h, row : row + BZ, :] = (here[h] + rate * (sums[h] + before[h] + after[h])) * scale
+    every = [(h, c, k) for c in range(NC) for h in range(2) for k in range(E // 2)]
+    d = []
+    for h, c, k in every:
+        row = (c * E + 2 * k) * BZ
+        d.append(out[h, row : row + BZ, :] + out[h, row + BZ : row + 2 * BZ, :])
+    d = z_differences(d, sub, upper)
+    d = [t + r for t, r in zip(d, [rl(t, -E) for t in d])]
+    d = [rl(t, k) for t, (_, _, k) in zip(d, every)]
+    faces = {}
+    for t, (h, c, k) in zip(d, every):
+        faces[h, c] = t if k == 0 else jnp.where(z == k, t, faces[h, c])
+    y8 = lane % 8
+    source = (y8 % 4) * (2 * E) + lane // E
+    picked = {key: pick_lanes(t, source) for key, t in faces.items()}
+    for c in range(NC):
+        top = jnp.where(y8 < 4, picked[0, c], picked[1, c])
+        tops[c * BZ : c * BZ + BZ, :] = jnp.where(z // 8 == gy % 2, top, 0.0)
 
 
 def coarse_plane(pair, parity, lane, sub):
@@ -321,9 +350,17 @@
     return jnp.where(lane % E // 8 == sub % 2, 0.25 * out, 0.0)
 
 
+def strips(low, high, x, low_lane, high_lane):
+    shift = E * (x % 8)
+    return (
+        jnp.where(low_lane, rl(low[x // 8], -shift), 0.0),
+        jnp.where(high_lane, rl(high[x // 8], L - E - shift), 0.0),
+    )
+
+
 def flux_kernel(
-    shape, partial, moved_rates, masks, core_first, link_first, near, far, near_sent, far_sent,
-    first, x_core, x_link, y_near, y_far, kept, sent,
+    shape, partial, moved_rates, masks, tops, core_first, link_first, near, far, near_sent, far_sent,
+    x_core, x_link, y_near, y_far, kept, sent,
 ):
     x_first, y_first, link_ok, far_ok = ends(shape)
     gx, gy, _ = place_of(shape)
@@ -333,52 +370,61 @@
     upper = sub % 2 == 1
     z = lane % E
     low_lane, high_lane = lane < E, lane >= L - E
-    for c in range(NC):
-        rate = moved_rates[c * BZ : c * BZ + BZ, :]
-        scale = 1.0 / (1.0 + 6.0 * rate)
-        weight = rate * scale
-        lines, ghost_r, ghost_f = [], [], []
-        for got, sent_, kept_, ok in ((near, near_sent, y_near, None), (far, far_sent, y_far, far_ok)):
+    each = range(NC)
+    rate = [moved_rates[c * BZ : c * BZ + BZ, :] for c in each]
+    scale = [1.0 / (1.0 + 6.0 * r) for r in rate]
+    weight = [r * q for r, q in zip(rate, scale)]
+
+    def extra_at(ref, c):
+        return ref[FACE + c * BZ : FACE + c * BZ + BZ, :]
+
+    def corner(extra):
+        return jnp.where(low_lane, extra, 0.0), jnp.where(high_lane, rl(extra, L - 2 * E), 0.0)
+
+    sides = []
+    for got, sent_, kept_, ok in ((near, near_sent, y_near, None), (far, far_sent, y_far, far_ok)):
+        planes, extras, firsts = [], [], []
+        for c in each:
             g0, g1, own = pair_at(got, 0, c), pair_at(got, 1, c), pair_at(sent_, 0, c)
-            extra = got[FACE + c * BZ : FACE + c * BZ + BZ, :]
+            extra = extra_at(got, c)
             if ok is not None:
                 g0, g1 = (tuple(jnp.where(ok, t, 0.0) for t in g) for g in (g0, g1))
                 extra = jnp.where(ok, extra, 0.0)
             g_rate = jnp.where(lane < L // 2, rl(extra, L // 2), extra)
             g_scale = 1.0 / (1.0 + 6.0 * g_rate)
-            sums = inner(g0, lane, sub, swap)
-            line = (jnp.where(low_lane, extra, 0.0), jnp.where(high_lane, rl(extra, L - 2 * E), 0.0))
-            first_g = []
+            sums, line = inner(g0, lane, sub, swap), corner(extra)
+            first = []
             for h in range(2):
                 value = (g0[h] + g_rate * (sums[h] + line[h] + g1[h] + own[h])) * g_scale
                 if ok is not None:
                     value = jnp.where(ok, value, 0.0)
                 row = (h * NC + c) * BZ
                 kept_[row : row + BZ, :] = value
-                first_g.append(value)
-            lines.append(extra)
-            ghost_r.append(g0)
-            ghost_f.append(first_g)
+                first.append(value)
+            planes.append(g0)
+            extras.append(extra)
+            firsts.append(first)
+        sides.append((planes, extras, firsts))
+    far_r, far_f = sides[1][0], sides[1][2]
+
+    def by_side(which, c):
+        a, b = sides[0][which][c], sides[1][which][c]
+        if which == 1:
+            return jnp.where(y_first, b, a), jnp.where(y_first, a, b)
+        return [jnp.where(y_first, q, p) for p, q in zip(a, b)], [jnp.where(y_first, p, q) for p, q in zip(a, b)]
+
+    faces_y = []
+    for c in each:
         own, own1 = pair_at(far_sent, 0, c), pair_at(far_sent, 1, c)
-        extra = far_sent[FACE + c * BZ : FACE + c * BZ + BZ, :]
-        sums = inner(own, lane, sub, swap)
-        line = (jnp.where(low_lane, extra, 0.0), jnp.where(high_lane, rl(extra, L - 2 * E), 0.0))
-        flux_y = []
-        for h in range(2):
-            value = (own[h] + rate * (sums[h] + line[h] + own1[h] + ghost_r[1][h])) * scale
-            flux_y.append(ghost_f[1][h] - value)
-        low_r = [jnp.where(y_first, b, a) for a, b in zip(*ghost_r)]
-        high_r = [jnp.where(y_first, a, b) for a, b in zip(*ghost_r)]
-        low_line = jnp.where(y_first, lines[1], lines[0])
-        high_line = jnp.where(y_first, lines[0], lines[1])
-        for x in range(E):
-            a, b = tile_at(partial, c, x)
-            shift = E * (x % 8)
-            a = a + weight * jnp.where(low_lane, rl(low_r[x // 8], -shift), 0.0)
-            b = b + weight * jnp.where(high_lane, rl(high_r[x // 8], L - E - shift), 0.0)
-            row = (c * E + x) * BZ
-            first[0, row : row + BZ, :] = a
-            first[1, row : row + BZ, :] = b
+        sums, line = inner(own, lane, sub, swap), corner(extra_at(far_sent, c))
+        flux = [
+            far_f[c][h] - (own[h] + rate[c] * (sums[h] + line[h] + own1[h] + far_r[c][h])) * scale[c] for h in range(2)
+        ]
+        face = coarse_plane(flux, par_x, lane, sub) * (rate[c] * masks[BZ : 2 * BZ, :])
+        faces_y.append(face + rs(face, 1))
+    faces_x = []
+    for c in each:
+        low_line, high_line = by_side(1, c)
         planes = []
         for part, kept_, at_low, ok in ((core_first, x_core, ~x_first, None), (link_first, x_link, x_first, link_ok)):
             g_rate = kept_rate(part, c)
@@ -386,50 +432,49 @@
             bottom = jnp.where(at_low, low_line, rl(low_line, -E))
             top = jnp.where(at_low, rl(high_line, L - E), rl(high_line, L - 2 * E))
             plane = []
-            for h, (line_, there) in enumerate(((bottom, low_lane), (top, high_lane))):
+            for h, (line, there) in enumerate(((bottom, low_lane), (top, high_lane))):
                 row = (h * NC + c) * BZ
-                value = part[row : row + BZ, :] + g_weight * jnp.where(there, line_, 0.0)
+                value = part[row : row + BZ, :] + g_weight * jnp.where(there, line, 0.0)
                 if ok is not None:
                     value = jnp.where(ok, value, 0.0)
                 kept_[row : row + BZ, :] = value
                 plane.append(value)
             planes.append(plane)
-        flux_x = []
+        low_r, high_r = by_side(0, c)
+        at_0, at_15 = (strips(low_r, high_r, x, low_lane, high_lane) for x in (0, E - 1))
+        cells_0, cells_15 = tile_at(partial, c, 0), tile_at(partial, c, E - 1)
+        flux = []
         for h in range(2):
-            low = first[h, c * E * BZ : c * E * BZ + BZ, :]
-            row = (c * E + E - 1) * BZ
-            high = first[h, row : row + BZ, :]
-            flux_x.append(planes[1][h] - jnp.where(x_first, low, high))
-        faces_z = []
+            cell = jnp.where(x_first, cells_0[h], cells_15[h])
+            cell = cell + weight[c] * jnp.where(x_first, at_0[h], at_15[h])
+            flux.append(planes[1][h] - cell)
+        face = coarse_plane(flux, par_y, lane, sub) * (rate[c] * masks[0:BZ, :])
+        faces_x.append(face + rs(face, -1))
+    faces_z = []
+    source = (lane // E % 4) * (2 * E) + jnp.where(lane % 8 == 7, 7, 0)
+    d = []
+    for c in each:
+        for side in by_side(0, c):
+            d += [weight[c] * t for t in side]
+    d = [t + r for t, r in zip(d, [rl(t, -E) for t in d])]
+    d = z_differences(d, sub, upper)
+    halves = []
+    for c in each:
         for h in range(2):
-            face = None
-            for k in range(E // 2):
-                row = (c * E + 2 * k) * BZ
-                t = first[h, row : row + BZ, :] + first[h, row + BZ : row + 2 * BZ, :]
-                down = jnp.where(sub == 0, 0.0, rs(t, 1))
-                up = jnp.where(sub == BZ - 1, 0.0, rs(t, -1))
-                high = rl(jnp.where(upper, t, down), 1 - E)
-                d = high - jnp.where(upper, up, t)
-                d = jnp.where(upper, -d, d)
-                d = rl(d + rl(d, -E), k)
-                face = d if face is None else jnp.where(z == k, d, face)
-            faces_z.append(face)
-        face_x = coarse_plane(flux_x, par_y, lane, sub) * (rate * masks[0:BZ, :])
-        face_y = coarse_plane(flux_y, par_x, lane, sub) * (rate * masks[BZ : 2 * BZ, :])
-        y8 = lane % 8
-        source = (y8 % 4) * (2 * E) + lane // E
-        face_z = jnp.where(y8 < 4, pick_lanes(faces_z[0], source), pick_lanes(faces_z[1], source))
-        face_z = jnp.where(z // 8 == par_y, face_z, 0.0) * (0.25 * rate * masks[2 * BZ :, :])
-        face_x = face_x + rs(face_x, -1)
-        face_y = face_y + rs(face_y, 1)
+            halves.append(jnp.where(z == 7, rl(d[4 * c + 2 + h], 7), d[4 * c + h]))
+    halves = [pick_lanes(t, source) for t in halves]
+    for c in each:
+        add = jnp.where(lane < L // 2, halves[2 * c], halves[2 * c + 1])
+        add = jnp.where((z == 8 * par_y) | (z == 8 * par_y + 7), add, 0.0)
+        faces_z.append((tops[c * BZ : c * BZ + BZ, :] + add) * (0.25 * rate[c] * masks[2 * BZ :, :]))
+    left = sub % 4 < 2
+    for c in each:
         for h in range(2):
-            sides = jnp.where(upper, jnp.where(par_x == h, face_y, 0.0), jnp.where(par_y == h, face_x, 0.0))
-            tops = jnp.where(par_x == h, face_z, 0.0)
-            left = sub % 4 < 2
-            columns = (
-                jnp.where(left, sides, rs(tops, 2)),
-                jnp.where(left, rs(sides, -2), tops),
+            outer = jnp.where(
+                upper, jnp.where(par_x == h, faces_y[c], 0.0), jnp.where(par_y == h, faces_x[c], 0.0)
             )
+            top = jnp.where(par_x == h, faces_z[c], 0.0)
+            columns = (jnp.where(left, outer, rs(top, 2)), jnp.where(left, rs(outer, -2), top))
             row = (h * NC + c) * BZ
             kept[row : row + BZ, :] = jnp.where(y_first, columns[0], columns[1])
             sent[row : row + BZ, :] = jnp.where(y_first, columns[1], columns[0])
@@ -467,33 +512,37 @@
             out[0, 0, c, :, h * L : h * L + L] = t[:6]
 
 
-def smooth_kernel(shape, moved, rates, first, x_core, x_link, y_near, y_far, out, held):
-    x_first, y_first, _, _ = ends(shape)
+def smooth_kernel(shape, moved, rates, partial, near, far, x_core, x_link, y_near, y_far, out, first, held):
+    x_first, y_first, _, far_ok = ends(shape)
     lane, sub = lanes(), subs()
     swap = swap_index(lane)
     low_lane, high_lane = lane < E, lane >= L - E
     for c in range(NC):
         rate = rates[c * BZ : c * BZ + BZ, :]
         scale = 1.0 / (1.0 + 6.0 * rate)
-
-        def ghosts(a_ref, b_ref, a_first):
-            a, b = (tuple(ref[(h * NC + c) * BZ : (h * NC + c + 1) * BZ, :] for h in range(2)) for ref in (a_ref, b_ref))
+        weight = rate * scale
+
+        def ghosts(a, b, a_first):
             low = [jnp.where(a_first, q, p) for p, q in zip(a, b)]
             high = [jnp.where(a_first, p, q) for p, q in zip(a, b)]
             return low, high
 
-        low, high = ghosts(x_core, x_link, x_first)
-        low_y, high_y = ghosts(y_near, y_far, y_first)
+        low, high = ghosts(pair_at(x_core, 0, c), pair_at(x_link, 0, c), x_first)
+        low_y, high_y = ghosts(pair_at(y_near, 0, c), pair_at(y_far, 0, c), y_first)
+        far_r = [jnp.where(far_ok, t, 0.0) for t in pair_at(far, 0, c)]
+        low_r, high_r = ghosts(pair_at(near, 0, c), far_r, y_first)
+
+        for x in range(E):
+            edge = strips(low_r, high_r, x, low_lane, high_lane)
+            row = (c * E + x) * BZ
+            for h in range(2):
+                first[h, row : row + BZ, :] = partial[h, row : row + BZ, :] + weight * edge[h]
         for x in range(E):
             here = tile_at(first, c, x)
             before = low if x == 0 else tile_at(first, c, x - 1)
             after = high if x == E - 1 else tile_at(first, c, x + 1)
             sums = inner(here, lane, sub, swap)
-            shift = E * (x % 8)
-            edge = (
-                jnp.where(low_lane, rl(low_y[x // 8], -shift), 0.0),
-                jnp.where(high_lane, rl(high_y[x // 8], L - E - shift), 0.0),
-            )
+            edge = strips(low_y, high_y, x, low_lane, high_lane)
             start = tile_at(moved, c, x)
             row = (c * E + x) * BZ
             for h in range(2):
@@ -524,13 +573,15 @@
         for b in range(columns)
     ]
     k = lambda f: functools.partial(f, shape)
+    coeff_old = coeff_old.transpose(0, 3, 1, 2)
+    cf_mask = cf_mask.transpose(0, 2, 1, 3)
     big = (2, NC * E * BZ, L)
 
     boxes, even, odd = call(
         k(pack_kernel),
         [(new_place, "any"), (coeff_old, "any"), (fields_old, "any")],
         [((BZ, NC, E, 2 * L), "vmem"), ((PARCEL, 2 * L), "vmem"), ((PARCEL, 2 * L), "vmem")],
-        [SM((1, 1, BZ), I32), SM((1, 1, BZ, NC), F32), pltpu.SemaphoreType.DMA((3,))],
+        [SM((1, 1, BZ), I32), SM((1, NC, 1, BZ), F32), pltpu.SemaphoreType.DMA((3,))],
     )
     odd_got = swap(odd, odd_pairs)
     even_got = swap(even, even_pairs)
@@ -558,35 +609,28 @@
     )
     far_got = swap(far, far_pairs)
     near_got = swap(near, even_pairs)
-    part, core_first, link_first = call(
-        k(sweep_kernel_with_rates),
+    part, core_first, link_first, tops = call(
+        k(sweep_kernel),
         [(a, "vmem") for a in (moved, rates, core_got, link_got, core, link)],
-        [(big, "vmem"), ((3 * PLANE, L), "vmem"), ((3 * PLANE, L), "vmem")],
+        [(big, "vmem"), ((3 * PLANE, L), "vmem"), ((3 * PLANE, L), "vmem"), ((PLANE, L), "vmem")],
     )
     plane = ((2 * PLANE, L), "vmem")
-    first, x_core, x_link, y_near, y_far, kept, sent = call(
+    x_core, x_link, y_near, y_far, kept, sent = call(
         k(flux_kernel),
-        [(a, "vmem") for a in (part, rates, masks, core_first, link_first, near_got, far_got, near, far)],
-        [(big, "vmem"), plane, plane, plane, plane, plane, plane],
+        [(a, "vmem") for a in (part, rates, masks, tops, core_first, link_first, near_got, far_got, near, far)],
+        [plane] * 6,
     )
     got = swap(sent, even_pairs)
     (smoothed,) = call(
         k(smooth_kernel),
-        [(a, "vmem") for a in (moved, rates, first, x_core, x_link, y_near, y_far)],
+        [(a, "vmem") for a in (moved, rates, part, near_got, far_got, x_core, x_link, y_near, y_far)],
         [((1, 1, BZ, NC, E, 2 * L), "out")],
-        [VM(big, F32)],
+        [VM(big, F32), VM(big, F32)],
     )
     mine, sent = call(k(half_kernel), [(kept, "vmem"), (got, "vmem")], [plane, plane])
     got = swap(sent, core_pairs)
     (registers,) = call(k(register_kernel), [(mine, "vmem"), (got, "vmem")], [((1, 1, NC, 6, 2 * L), "out")])
     return smoothed, registers
-
-
-def sweep_kernel_with_rates(shape, moved, rates, core, link, core_sent, link_sent, out, core_first, link_first):
-    sweep_kernel(shape, moved, rates, core, link, core_sent, link_sent, out, core_first, link_first)
-    _, _, link_ok, _ = ends(shape)
-    core_first[2 * PLANE :, :] = core[FACE:, :]
-    link_first[2 * PLANE :, :] = jnp.where(link_ok, link[FACE:, :], 0.0)
 
 
 def solution(mesh):

time: 38.5 us -> 34.2 us (0.89)
  Pallas kernels: 9.37 us -> 7.23 us
  local copies, waits for them, and re-layouts: 2.51 us -> 1.3 us
  waiting for transfers between devices: 14.5 us -> 13.5 us
    pallas_call x10, Pallas kernels: 9.37 us -> 7.23 us  [call(): pl.pallas_call(kernel, out_shape=shapes, in_specs=in_specs, out_specs=out...]
    unnamed x9 -> x7, local copies, waits for them, and re-layouts: 2.51 us -> 1.3 us
    ppermute x8, waiting for transfers between devices: 14.5 us -> 13.5 us  [swap(): return lax.ppermute(array, both, pairs)]
  transfers between devices with their start and end apart: 8 -> 8, of which waited for: 5 -> 5; matrix products, arithmetic and copies ran while one was open for 0% -> 0% of each run, Pallas kernels for 11% -> 14%
where the time goes in v2:
time: 34.2 us; the launch traced here: 34 us
  waiting for transfers between devices  13.5 us (39%)
  starting transfers between devices  11.2 us (33%)
  Pallas kernels  7.23 us (21%)
  local copies, waits for them, and re-layouts  1.3 us (4%)
  between operations  0.74 us (2%)
    ppermute x8, waiting for transfers between devices, swap(): return lax.ppermute(array, both, pairs)  13.5 us
    ppermute x8, starting transfers between devices, swap(): return lax.ppermute(array, both, pairs)  11.2 us
    pallas_call x10, Pallas kernels, call(): pl.pallas_call(kernel, out_shape=shapes, in_specs=in_specs, out_specs=out...  7.23 us
    unnamed x7, local copies, waits for them, and re-layouts  1.3 us
  transfers between devices with their start and end apart: 8, of which 5 were waited for; matrix products, arithmetic and copies ran while one was open for 0% of the time, Pallas kernels for 14%

profile of v2, /device:TPU:0, one launch (start us, length us, event | category | flops | bytes accessed | tf_op | source)
XLA Modules:
  0.0 34.0 jit_solution(10149644664945110633)
XLA Ops:
  0.6 1.1 %shard_map.59 = (f32[8,5,16,256]{3,2,1,0:T(8,128)S(1)}, f32[176,256]{1,0:T(8,128)S(1)}, f32[176,256]{1,0:T(8,128)S(1)}) custom-call(s32[1,1,8]{2,1,0:T(1,128)} %place.1, f32[1,5,1,8]{3,2,1,0:T(1,128)} %bitcast.2, f32[1,1,8,5,16,256]{5,4,3,2,1,0:T(8,128)} %fields_hbm.1), custom_call_target="tpu_custom_call" | custom-call | flops 1000 | tf_op jit(solution)/shard_map/pallas_call | solution.py:48
  1.8 0.0 copy-start
  1.8 3.0 %collective-permute-start = (f32[176,256]{1,0:T(8,128)S(1)}, f32[176,256]{1,0:T(8,128)S(1)}, u32[]{:S(2)}, u32[]{:S(2)}) collective-permute-start(f32[176,256]{1,0:T(8,128)S(1)} %get-tuple-element.28), channel_id=1, source_target_pairs={{0,1},{1,0},{2,3},{3,2},{4,5},{5,4},{6,7},{7,6},{8,9},{9,8},{10,11... | collective-permute-start | bytes 540680 | tf_op jit(solution)/shard_map/ppermute | solution.py:561
  4.8 3.6 %collective-permute-start.1 = (f32[176,256]{1,0:T(8,128)S(1)}, f32[176,256]{1,0:T(8,128)S(1)}, u32[]{:S(2)}, u32[]{:S(2)}) collective-permute-start(f32[176,256]{1,0:T(8,128)S(1)} %get-tuple-element.29), channel_id=1, source_target_pairs={{0,31},{1,2},{2,1},{3,4},{4,3},{5,6},{6,5},{7,8},{8,7},{9,10},{10,... | collective-permute-start | bytes 540680 | tf_op jit(solution)/shard_map/ppermute | solution.py:561
  8.5 0.6 %copy-done.1 = s32[1,1,8]{2,1,0:T(1,128)S(1)} copy-done((s32[1,1,8]{2,1,0:T(1,128)S(1)}, s32[1,1,8]{2,1,0:T(1,128)}, u32[]{:S(2)}) %copy-start.1) | copy-done | bytes 56
  9.1 0.8 %shard_map.60 = (f32[2,640,128]{2,1,0:T(8,128)S(1)}, f32[40,128]{1,0:T(8,128)S(1)}, f32[24,128]{1,0:T(8,128)S(1)}) custom-call(s32[1,1,8]{2,1,0:T(1,128)S(1)} %copy-done.1, f32[1,5,1,8]{3,2,1,0:T(1,128)S(1)} %bitcast.3, s32[1,3,1,8]{3,2,1,0:T(1,128)S(1)} %bitcast.4, f32[8,5,16,256]{3,2,1,0:T(8,128)S(1)} %get-tuple-element.30.boxes), custom_call_target="tpu_custom_call" | custom-call | flops 1000 | tf_op jit(solution)/shard_map/pallas_call | solution.py:48
  9.9 2.6 %collective-permute-done.even = f32[176,256]{1,0:T(8,128)S(1)} collective-permute-done((f32[176,256]{1,0:T(8,128)S(1)}, f32[176,256]{1,0:T(8,128)S(1)}, u32[]{:S(2)}, u32[]{:S(2)}) %collective-permute-start) | collective-permute-done | bytes 180256 | tf_op jit(solution)/shard_map/ppermute | solution.py:561
  12.5 2.5 %collective-permute-done.1.odd = f32[176,256]{1,0:T(8,128)S(1)} collective-permute-done((f32[176,256]{1,0:T(8,128)S(1)}, f32[176,256]{1,0:T(8,128)S(1)}, u32[]{:S(2)}, u32[]{:S(2)}) %collective-permute-start.1) | collective-permute-done | bytes 180256 | tf_op jit(solution)/shard_map/ppermute | solution.py:561
  15.0 0.1 shard_map.62
  15.1 0.1 collective-permute-start.2
  15.2 1.2 %collective-permute-start.3 = (f32[200,128]{1,0:T(8,128)S(1)}, f32[200,128]{1,0:T(8,128)S(1)}, u32[]{:S(2)}, u32[]{:S(2)}) collective-permute-start(f32[200,128]{1,0:T(8,128)S(1)} %get-tuple-element.36.link_sent), channel_id=1, source_target_pairs={{0,24},{1,25},{2,26},{3,27},{4,28},{5,29},{6,30},{7,31},{8,16},{9,... | collective-permute-start | bytes 307208 | tf_op jit(solution)/shard_map/ppermute | solution.py:561
  16.3 0.4 %shard_map.61 = (f32[2,640,128]{2,1,0:T(8,128)S(1)}, f32[160,128]{1,0:T(8,128)S(1)}, f32[160,128]{1,0:T(8,128)S(1)}) custom-call(f32[176,256]{1,0:T(8,128)S(1)} %collective-permute-done.even, f32[176,256]{1,0:T(8,128)S(1)} %collective-permute-done.1.odd, f32[2,640,128]{2,1,0:T(8,128)S(1)} %get-tuple-element.31.moved), custom_call_target="tpu_custom_call" | custom-call | flops 1000 | tf_op jit(solution)/shard_map/pallas_call | solution.py:48
  16.8 3.1 %collective-permute-done.3.link = f32[200,128]{1,0:T(8,128)S(1)} collective-permute-done((f32[200,128]{1,0:T(8,128)S(1)}, f32[200,128]{1,0:T(8,128)S(1)}, u32[]{:S(2)}, u32[]{:S(2)}) %collective-permute-start.3) | collective-permute-done | bytes 102432 | tf_op jit(solution)/shard_map/ppermute | solution.py:561
  19.9 0.1 shard_map.64
  20.0 0.1 collective-permute-start.4
  20.0 0.5 %collective-permute-start.5 = (f32[200,128]{1,0:T(8,128)S(1)}, f32[200,128]{1,0:T(8,128)S(1)}, u32[]{:S(2)}, u32[]{:S(2)}) collective-permute-start(f32[200,128]{1,0:T(8,128)S(1)} %get-tuple-element.41.far_sent), channel_id=1, source_target_pairs={{0,8},{1,2},{2,1},{3,4},{4,3},{5,6},{6,5},{7,15},{8,0},{9,10},{10,... | collective-permute-start | bytes 307208 | tf_op jit(solution)/shard_map/ppermute | solution.py:561
  20.5 1.4 %shard_map.63 = (f32[2,640,128]{2,1,0:T(8,128)S(1)}, f32[120,128]{1,0:T(8,128)S(1)}, f32[120,128]{1,0:T(8,128)S(1)}, f32[40,128]{1,0:T(8,128)S(1)}) custom-call(f32[2,640,128]{2,1,0:T(8,128)S(1)} %get-tuple-element.32.moved, f32[40,128]{1,0:T(8,128)S(1)} %get-tuple-element.34.rates.moved_rates, f32[200,128]{1,0:T(8,128)S(1)} %collective-permute-done.2.core, ...), custom_call_target="tpu_custom_call" | custom-call | flops 1000 | tf_op jit(solution)/shard_map/pallas_call | solution.py:48
  21.8 3.3 %collective-permute-done.4.near = f32[200,128]{1,0:T(8,128)S(1)} collective-permute-done((f32[200,128]{1,0:T(8,128)S(1)}, f32[200,128]{1,0:T(8,128)S(1)}, u32[]{:S(2)}, u32[]{:S(2)}) %collective-permute-start.4) | collective-permute-done | bytes 102432 | tf_op jit(solution)/shard_map/ppermute | solution.py:561
  25.2 1.1 %shard_map.65 = (f32[80,128]{1,0:T(8,128)S(1)}, f32[80,128]{1,0:T(8,128)S(1)}, f32[80,128]{1,0:T(8,128)S(1)}, f32[80,128]{1,0:T(8,128)S(1)}, f32[80,128]{1,0:T(8,128)S(1)}, /*index=5*/f32[80,128]{1,0:T(8,128)S(1)}) custom-call(f32[2,640,128]{2,1,0:T(8,128)S(1)} %get-tuple-element.37.partial, f32[40,128]{1,0:T(8,128)S(1)} %get-tuple-element.34.rates.moved_rates, ...), custom_call_target="tpu_custom_call" | custom-call | flops 1000 | tf_op jit(solution)/shard_map/pallas_call | solution.py:48
  26.3 2.7 %collective-permute-start.6 = (f32[80,128]{1,0:T(8,128)S(1)}, f32[80,128]{1,0:T(8,128)S(1)}, u32[]{:S(2)}, u32[]{:S(2)}) collective-permute-start(f32[80,128]{1,0:T(8,128)S(1)} %get-tuple-element.51), channel_id=1, source_target_pairs={{0,1},{1,0},{2,3},{3,2},{4,5},{5,4},{6,7},{7,6},{8,9},{9,8},{10,11... | collective-permute-start | bytes 122888 | tf_op jit(solution)/shard_map/ppermute | solution.py:561
  29.0 2.0 %collective-permute-done.6.got = f32[80,128]{1,0:T(8,128)S(1)} collective-permute-done((f32[80,128]{1,0:T(8,128)S(1)}, f32[80,128]{1,0:T(8,128)S(1)}, u32[]{:S(2)}, u32[]{:S(2)}) %collective-permute-start.6) | collective-permute-done | bytes 40992 | tf_op jit(solution)/shard_map/ppermute | solution.py:561
  31.0 0.1 collective-permute-start.7
  31.1 2.3 %shard_map.66 = f32[1,1,8,5,16,256]{5,4,3,2,1,0:T(8,128)} custom-call(f32[2,640,128]{2,1,0:T(8,128)S(1)} %get-tuple-element.32.moved, f32[40,128]{1,0:T(8,128)S(1)} %get-tuple-element.34.rates.moved_rates, f32[2,640,128]{2,1,0:T(8,128)S(1)} %get-tuple-element.37.partial, f32[200,128]{1,0:T(8,128)S(1)} %collective-permute-done.4.near, ...), custom_call_target="tpu_custom_call" | custom-call | flops 1000 | tf_op jit(solution)/shard_map/pallas_call | solution.py:48
  33.4 0.6 %copy.6 = f32[1,1,5,6,256]{4,1,3,2,0:T(1,128)} copy(f32[1,1,5,6,256]{4,3,2,1,0:T(8,128)S(1)} %shard_map.68) | data formatting | bytes 61440
  (9 shorter events, 0.1 us)
Async XLA Ops:
  1.8 6.7 %copy-start = (f32[1,1,8,5]{2,1,3,0:T(1,128)S(1)}, f32[1,1,8,5]{2,1,3,0:T(1,128)}, u32[]{:S(2)}) copy-start(f32[1,1,8,5]{2,1,3,0:T(1,128)} %param.5) | copy-start | bytes 484
  1.8 10.7 %collective-permute-start = (f32[176,256]{1,0:T(8,128)S(1)}, f32[176,256]{1,0:T(8,128)S(1)}, u32[]{:S(2)}, u32[]{:S(2)}) collective-permute-start(f32[176,256]{1,0:T(8,128)S(1)} %get-tuple-element.28), channel_id=1, source_target_pairs={{0,1},{1,0},{2,3},{3,2},{4,5},{5,4},{6,7},{7,6},{8,9},{9,8},{10,11... | collective-permute-start | bytes 540680 | tf_op jit(solution)/shard_map/ppermute | solution.py:561
  4.8 3.6 %copy-start.2 = (s32[1,1,3,8]{3,1,2,0:T(1,128)S(1)}, s32[1,1,3,8]{3,1,2,0:T(1,128)}, u32[]{:S(2)}) copy-start(s32[1,1,3,8]{3,1,2,0:T(1,128)} %param.7) | copy-start | bytes 292
  4.8 10.2 %collective-permute-start.1 = (f32[176,256]{1,0:T(8,128)S(1)}, f32[176,256]{1,0:T(8,128)S(1)}, u32[]{:S(2)}, u32[]{:S(2)}) collective-permute-start(f32[176,256]{1,0:T(8,128)S(1)} %get-tuple-element.29), channel_id=1, source_target_pairs={{0,31},{1,2},{2,1},{3,4},{4,3},{5,6},{6,5},{7,8},{8,7},{9,10},{10,... | collective-permute-start | bytes 540680 | tf_op jit(solution)/shard_map/ppermute | solution.py:561
  8.5 0.7 %copy-start.1 = (s32[1,1,8]{2,1,0:T(1,128)S(1)}, s32[1,1,8]{2,1,0:T(1,128)}, u32[]{:S(2)}) copy-start(s32[1,1,8]{2,1,0:T(1,128)} %place.1) | copy-start | bytes 100
  15.1 1.7 %collective-permute-start.2 = (f32[200,128]{1,0:T(8,128)S(1)}, f32[200,128]{1,0:T(8,128)S(1)}, u32[]{:S(2)}, u32[]{:S(2)}) collective-permute-start(f32[200,128]{1,0:T(8,128)S(1)} %get-tuple-element.35.core_sent), channel_id=1, source_target_pairs={{0,8},{1,9},{2,10},{3,11},{4,12},{5,13},{6,14},{7,15},{8,0},{9,1},... | collective-permute-start | bytes 307208 | tf_op jit(solution)/shard_map/ppermute | solution.py:561
  15.2 4.7 %collective-permute-start.3 = (f32[200,128]{1,0:T(8,128)S(1)}, f32[200,128]{1,0:T(8,128)S(1)}, u32[]{:S(2)}, u32[]{:S(2)}) collective-permute-start(f32[200,128]{1,0:T(8,128)S(1)} %get-tuple-element.36.link_sent), channel_id=1, source_target_pairs={{0,24},{1,25},{2,26},{3,27},{4,28},{5,29},{6,30},{7,31},{8,16},{9,... | collective-permute-start | bytes 307208 | tf_op jit(solution)/shard_map/ppermute | solution.py:561
  20.0 5.2 %collective-permute-start.4 = (f32[200,128]{1,0:T(8,128)S(1)}, f32[200,128]{1,0:T(8,128)S(1)}, u32[]{:S(2)}, u32[]{:S(2)}) collective-permute-start(f32[200,128]{1,0:T(8,128)S(1)} %get-tuple-element.40.near_sent), channel_id=1, source_target_pairs={{0,1},{1,0},{2,3},{3,2},{4,5},{5,4},{6,7},{7,6},{8,9},{9,8},{10,11... | collective-permute-start | bytes 307208 | tf_op jit(solution)/shard_map/ppermute | solution.py:561
  20.0 5.2 %collective-permute-start.5 = (f32[200,128]{1,0:T(8,128)S(1)}, f32[200,128]{1,0:T(8,128)S(1)}, u32[]{:S(2)}, u32[]{:S(2)}) collective-permute-start(f32[200,128]{1,0:T(8,128)S(1)} %get-tuple-element.41.far_sent), channel_id=1, source_target_pairs={{0,8},{1,2},{2,1},{3,4},{4,3},{5,6},{6,5},{7,15},{8,0},{9,10},{10,... | collective-permute-start | bytes 307208 | tf_op jit(solution)/shard_map/ppermute | solution.py:561
  26.3 4.7 %collective-permute-start.6 = (f32[80,128]{1,0:T(8,128)S(1)}, f32[80,128]{1,0:T(8,128)S(1)}, u32[]{:S(2)}, u32[]{:S(2)}) collective-permute-start(f32[80,128]{1,0:T(8,128)S(1)} %get-tuple-element.51), channel_id=1, source_target_pairs={{0,1},{1,0},{2,3},{3,2},{4,5},{5,4},{6,7},{7,6},{8,9},{9,8},{10,11... | collective-permute-start | bytes 122888 | tf_op jit(solution)/shard_map/ppermute | solution.py:561
  31.0 2.3 %collective-permute-start.7 = (f32[80,128]{1,0:T(8,128)S(1)}, f32[80,128]{1,0:T(8,128)S(1)}, u32[]{:S(2)}, u32[]{:S(2)}) collective-permute-start(f32[80,128]{1,0:T(8,128)S(1)} %get-tuple-element.53), channel_id=1, source_target_pairs={{0,8},{1,9},{2,10},{3,11},{4,12},{5,13},{6,14},{7,15},{8,0},{9,1},... | collective-permute-start | bytes 122888 | tf_op jit(solution)/shard_map/ppermute | solution.py:561

commit v3 on v2

--- a/solution.py
+++ b/solution.py
@@ -17,9 +17,13 @@
 
 PLANE = NC * BZ
 FACE = 4 * PLANE
-BOXROWS = NC * E
-LABELS = MOVE * BOXROWS + MOVE * NC
-PARCEL = 176
+EDGES = (0, 1, E - 2, E - 1)
+AHEAD = MOVE * NC * 4
+LABELS = AHEAD + MOVE * NC
+PARCEL = 56
+REST = MOVE * NC * 12
+XFACE = FACE + BZ
+YFACE = FACE + 2 * BZ
 
 VM = pltpu.VMEM
 SM = pltpu.SMEM
@@ -44,7 +48,7 @@
             out_specs.append(pl.BlockSpec(memory_space=VM))
         else:
             shapes.append(jax.ShapeDtypeStruct(shape, F32))
-            out_specs.append(pl.BlockSpec(memory_space=VM))
+            out_specs.append(pl.BlockSpec(memory_space=pltpu.HBM if space == "hbm" else VM))
     return pl.pallas_call(
         kernel,
         out_shape=shapes,
@@ -86,17 +90,18 @@
     return gx, gy, gx * mesh_shape[1] + gy
 
 
-def pack_kernel(shape, place_hbm, coeff_hbm, fields_hbm, boxes, even, odd, place, coeff, sem):
-    big = pltpu.make_async_copy(fields_hbm.at[0, 0], boxes, sem.at[0])
-    small = pltpu.make_async_copy(place_hbm, place, sem.at[1])
-    other = pltpu.make_async_copy(coeff_hbm, coeff, sem.at[2])
-    big.start()
-    small.start()
-    other.start()
+def pack_kernel(
+    shape, place_hbm, coeff_hbm, mask_hbm, fields_hbm, even, odd, even_rest, odd_rest, boxes, slots, rates, masks,
+    place, coeff, mask, sem,
+):
+    pairs = ((fields_hbm.at[0, 0], boxes), (place_hbm, place), (coeff_hbm, coeff), (mask_hbm, mask))
+    copies = [pltpu.make_async_copy(a, b, sem.at[i]) for i, (a, b) in enumerate(pairs)]
+    for copy in copies:
+        copy.start()
     _, _, me = place_of(shape)
     ahead = 1 - 2 * (me % 2)
-    small.wait()
-    other.wait()
+    for copy in copies[1:]:
+        copy.wait()
     chosen = []
     for out, owner in ((even, me + ahead), (odd, me - ahead)):
         count = jnp.int32(0)
@@ -115,32 +120,41 @@
         for k in range(MOVE):
             out[LABELS + k : LABELS + k + 1, :] = jnp.full((1, 2 * L), labels[k].astype(F32), F32)
             for c in range(NC):
-                row = MOVE * BOXROWS + k * NC + c
+                row = AHEAD + k * NC + c
                 out[row : row + 1, :] = jnp.full((1, 2 * L), coeff[0, c, 0, sources[k]], F32)
-    big.wait()
-    for out, sources in zip((even, odd), chosen):
+    for s in range(BZ):
+        value = place[0, 0, s]
+        label = jnp.where(value // BZ == me, value % BZ + 1, 0)
+        slots[s : s + 1, :] = jnp.full((1, L), label.astype(F32), F32)
+        for c in range(NC):
+            rates[s * NC + c : s * NC + c + 1, :] = jnp.full((1, L), coeff[0, c, 0, s], F32)
+        for d in range(3):
+            masks[d * BZ + s : d * BZ + s + 1, :] = jnp.full((1, L), mask[0, d, 0, s].astype(F32), F32)
+    copies[0].wait()
+    for out, rest, sources in ((even, even_rest, chosen[0]), (odd, odd_rest, chosen[1])):
         for k in range(MOVE):
             for c in range(NC):
-                row = (k * NC + c) * E
-                out[row : row + E, :] = boxes[sources[k], c]
-
-
-def stay_kernel(shape, place, coeff, mask, boxes, moved, rates, masks):
-    _, _, me = place_of(shape)
-    for s in range(BZ):
-        value = place[0, 0, s]
-        slot = value % BZ
-
-        @pl.when(value // BZ == me)
-        def _():
-            for c in range(NC):
-                for h in range(2):
-                    moved[h, pl.ds(c * E * BZ + slot, E, stride=BZ), :] = boxes[s, c, :, h * L : h * L + L]
-                rates[pl.ds(c * BZ + slot, 1), :] = jnp.full((1, L), coeff[0, c, 0, s], F32)
-
-    for d in range(3):
+                box = k * NC + c
+                out[4 * box : 4 * box + 2, :] = boxes[sources[k], c, :2]
+                out[4 * box + 2 : 4 * box + 4, :] = boxes[sources[k], c, E - 2 :]
+                rest[12 * box : 12 * box + 12, :] = boxes[sources[k], c, 2 : E - 2]
+
+
+def stay_kernel(shape, boxes, slots, old_rates, moved, rates):
+    label = (subs() + 1).astype(F32)
+    found = [slots[s : s + 1, :] == label for s in range(BZ)]
+    for c in range(NC):
+        tile = jnp.zeros((BZ, L), F32)
         for s in range(BZ):
-            masks[d * BZ + s : d * BZ + s + 1, :] = jnp.full((1, L), mask[0, d, 0, s].astype(F32), F32)
+            tile = jnp.where(found[s], old_rates[s * NC + c : s * NC + c + 1, :], tile)
+        rates[c * BZ : c * BZ + BZ, :] = tile
+        for x in range(E):
+            row = (c * E + x) * BZ
+            for h in range(2):
+                tile = jnp.zeros((BZ, L), F32)
+                for s in range(BZ):
+                    tile = jnp.where(found[s], boxes[s, c, x : x + 1, h * L : h * L + L], tile)
+                moved[h, row : row + BZ, :] = tile
 
 
 def arrivals(even, odd):
@@ -153,13 +167,20 @@
     return found
 
 
-def merged(found, moved, c, x, h):
+def merged(found, moved, c, x, h, rests=None):
     row = (c * E + x) * BZ
     tile = moved[h, row : row + BZ, :]
-    for parcel, k, hit in found:
-        at = (k * NC + c) * E + x
-        tile = jnp.where(hit, parcel[at : at + 1, h * L : h * L + L], tile)
+    for i, (parcel, k, hit) in enumerate(found):
+        if x in EDGES:
+            source, at = parcel, (k * NC + c) * 4 + EDGES.index(x)
+        else:
+            source, at = rests[i // MOVE], (k * NC + c) * 12 + x - 2
+        tile = jnp.where(hit, source[at : at + 1, h * L : h * L + L], tile)
     return tile
+
+
+def spread(tile, lane):
+    return pick_lanes(tile, jnp.full((BZ, L), lane, I32))
 
 
 def plane_row(layer, h, c):
@@ -170,14 +191,15 @@
     gx, _, _ = place_of(shape)
     first = gx % 2 == 0
     found = arrivals(even, odd)
+    lane = lanes()
+    together = jnp.zeros((BZ, L), F32)
     for c in range(NC):
         tile = rates[c * BZ : c * BZ + BZ, :]
         for parcel, k, hit in found:
-            at = MOVE * BOXROWS + k * NC + c
+            at = AHEAD + k * NC + c
             tile = jnp.where(hit, parcel[at : at + 1, :L], tile)
         all_rates[c * BZ : c * BZ + BZ, :] = tile
-        core[FACE + c * BZ : FACE + c * BZ + BZ, :] = tile
-        link[FACE + c * BZ : FACE + c * BZ + BZ, :] = tile
+        together = jnp.where(lane % L == c, tile, together)
         for layer in range(2):
             for h in range(2):
                 low = merged(found, moved, c, layer, h)
@@ -185,9 +207,11 @@
                 at = plane_row(layer, h, c)
                 core[at : at + BZ, :] = jnp.where(first, high, low)
                 link[at : at + BZ, :] = jnp.where(first, low, high)
-
-
-def merge_kernel(shape, even, odd, moved, out, near, far):
+    core[FACE:, :] = together
+    link[FACE:, :] = together
+
+
+def merge_kernel(shape, odd, even, odd_rest, even_rest, moved, out, near, far):
     _, gy, _ = place_of(shape)
     first = gy % 2 == 0
     found = arrivals(even, odd)
@@ -201,7 +225,7 @@
             here = lane // E == x % 8
             half = x // 8
             for h in range(2):
-                tile = merged(found, moved, c, x, h)
+                tile = merged(found, moved, c, x, h, (even_rest, odd_rest))
                 out[h, row : row + BZ, :] = tile
                 for layer in range(2):
                     keep, start = ((low, E * layer) if h == 0 else (high, L - E - E * layer))
@@ -223,11 +247,13 @@
     return x_first, y_first, link_ok, far_ok
 
 
-def ysend_kernel(shape, core, link, rates, near, far, near_out, far_out):
+def ysend_kernel(shape, link, core, rates, near, far, near_out, far_out):
     x_first, y_first, link_ok, _ = ends(shape)
     lane = lanes()
     near_out[:FACE, :] = near[...]
     far_out[:FACE, :] = far[...]
+    bottoms = [jnp.zeros((BZ, L), F32)] * 2
+    tops = [jnp.zeros((BZ, L), F32)] * 2
     for c in range(NC):
         lines = []
         for h in range(2):
@@ -235,14 +261,28 @@
             a = core[at : at + BZ, :]
             b = jnp.where(link_ok, link[at : at + BZ, :], 0.0)
             lines.append((jnp.where(x_first, b, a), jnp.where(x_first, a, b)))
+        i, at = divmod(c, 4)
+        at *= 2 * E
+        low = (lane >= at) & (lane < at + E)
+        high = (lane >= at + E) & (lane < at + 2 * E)
+        bottoms[i] = jnp.where(low, rl(lines[0][0], at), jnp.where(high, rl(lines[0][1], at + E), bottoms[i]))
+        tops[i] = jnp.where(low, rl(lines[1][0], at + E), jnp.where(high, rl(lines[1][1], at + 2 * E), tops[i]))
         rate = rates[c * BZ : c * BZ + BZ, :]
-        bottom = jnp.where(lane < E, lines[0][0], rl(lines[0][1], E))
-        top = jnp.where(lane < E, rl(lines[1][0], E), rl(lines[1][1], 2 * E))
-        bottom = jnp.where(lane < 2 * E, bottom, rate)
-        top = jnp.where(lane < 2 * E, top, rate)
-        at = FACE + c * BZ
-        near_out[at : at + BZ, :] = jnp.where(y_first, top, bottom)
-        far_out[at : at + BZ, :] = jnp.where(y_first, bottom, top)
+        bottoms[1] = jnp.where(lane == L // 2 + c, rate, bottoms[1])
+        tops[1] = jnp.where(lane == L // 2 + c, rate, tops[1])
+    for i in range(2):
+        at = FACE + i * BZ
+        near_out[at : at + BZ, :] = jnp.where(y_first, tops[i], bottoms[i])
+        far_out[at : at + BZ, :] = jnp.where(y_first, bottoms[i], tops[i])
+
+
+def extra_at(ref, c):
+    i, at = divmod(c, 4)
+    return rl(ref[FACE + i * BZ : FACE + i * BZ + BZ, :], -2 * E * at)
+
+
+def y_rate(ref, c):
+    return spread(ref[FACE + BZ : FACE + 2 * BZ, :], L // 2 + c)
 
 
 def z_parts(x, lane, sub, swap):
@@ -283,25 +323,24 @@
     return [jnp.where(upper, u - g, g - t) for g, u, t in zip(high, up, tiles)]
 
 
-def sweep_kernel(shape, moved, rates, core, link, core_sent, link_sent, out, core_first, link_first, tops):
+def sweep_kernel(shape, moved, rates, link, core, core_sent, link_sent, out, core_first, link_first, tops):
     x_first, _, link_ok, _ = ends(shape)
     _, gy, _ = place_of(shape)
     lane, sub = lanes(), subs()
     swap = swap_index(lane)
     upper = sub % 2 == 1
     z = lane % E
-    core_first[2 * PLANE :, :] = core[FACE:, :]
-    link_first[2 * PLANE :, :] = jnp.where(link_ok, link[FACE:, :], 0.0)
     for c in range(NC):
         rate = rates[c * BZ : c * BZ + BZ, :]
         scale = 1.0 / (1.0 + 6.0 * rate)
         ghost = []
         for got, sent, kept, ok in ((core, core_sent, core_first, None), (link, link_sent, link_first, link_ok)):
             g0, g1, own = pair_at(got, 0, c), pair_at(got, 1, c), pair_at(sent, 0, c)
-            g_rate = got[FACE + c * BZ : FACE + c * BZ + BZ, :]
+            g_rate = spread(got[FACE:, :], c)
             if ok is not None:
                 g0, g1 = (tuple(jnp.where(ok, t, 0.0) for t in g) for g in (g0, g1))
                 g_rate = jnp.where(ok, g_rate, 0.0)
+            kept[2 * PLANE + c * BZ : 2 * PLANE + c * BZ + BZ, :] = g_rate
             ghost.append(g0)
             g_scale = 1.0 / (1.0 + 6.0 * g_rate)
             sums = inner(g0, lane, sub, swap)
@@ -358,9 +397,44 @@
     )
 
 
+def corner(extra, low_lane, high_lane):
+    return jnp.where(low_lane, extra, 0.0), jnp.where(high_lane, rl(extra, L - 2 * E), 0.0)
+
+
+def y_ghosts(got, ok, c):
+    g0, g1, extra = pair_at(got, 0, c), pair_at(got, 1, c), extra_at(got, c)
+    if ok is not None:
+        g0, g1 = (tuple(jnp.where(ok, t, 0.0) for t in g) for g in (g0, g1))
+        extra = jnp.where(ok, extra, 0.0)
+    return g0, g1, extra
+
+
+def y_first_sweep(got, sent, ok, ghost, c, lane, sub, swap):
+    g0, g1, extra = ghost
+    own = pair_at(sent, 0, c)
+    g_rate = y_rate(got, c)
+    if ok is not None:
+        g_rate = jnp.where(ok, g_rate, 0.0)
+    g_scale = 1.0 / (1.0 + 6.0 * g_rate)
+    sums, line = inner(g0, lane, sub, swap), corner(extra, lane < E, lane >= L - E)
+    values = [(g0[h] + g_rate * (sums[h] + line[h] + g1[h] + own[h])) * g_scale for h in range(2)]
+    return values if ok is None else [jnp.where(ok, t, 0.0) for t in values]
+
+
+def x_first_sweep(part, ok, at_low, low_line, high_line, c, low_lane, high_lane):
+    g_rate = part[2 * PLANE + c * BZ : 2 * PLANE + c * BZ + BZ, :]
+    g_weight = g_rate / (1.0 + 6.0 * g_rate)
+    bottom = jnp.where(at_low, low_line, rl(low_line, -E))
+    top = jnp.where(at_low, rl(high_line, L - E), rl(high_line, L - 2 * E))
+    values = []
+    for h, (line, there) in enumerate(((bottom, low_lane), (top, high_lane))):
+        row = (h * NC + c) * BZ
+        values.append(part[row : row + BZ, :] + g_weight * jnp.where(there, line, 0.0))
+    return values if ok is None else [jnp.where(ok, t, 0.0) for t in values]
+
+
 def flux_kernel(
-    shape, partial, moved_rates, masks, tops, core_first, link_first, near, far, near_sent, far_sent,
-    x_core, x_link, y_near, y_far, kept, sent,
+    shape, partial, moved_rates, masks, tops, link_first, near, far, far_sent, x_link, y_far, kept, sent
 ):
     x_first, y_first, link_ok, far_ok = ends(shape)
     gx, gy, _ = place_of(shape)
@@ -374,49 +448,27 @@
     rate = [moved_rates[c * BZ : c * BZ + BZ, :] for c in each]
     scale = [1.0 / (1.0 + 6.0 * r) for r in rate]
     weight = [r * q for r, q in zip(rate, scale)]
-
-    def extra_at(ref, c):
-        return ref[FACE + c * BZ : FACE + c * BZ + BZ, :]
-
-    def corner(extra):
-        return jnp.where(low_lane, extra, 0.0), jnp.where(high_lane, rl(extra, L - 2 * E), 0.0)
-
-    sides = []
-    for got, sent_, kept_, ok in ((near, near_sent, y_near, None), (far, far_sent, y_far, far_ok)):
-        planes, extras, firsts = [], [], []
-        for c in each:
-            g0, g1, own = pair_at(got, 0, c), pair_at(got, 1, c), pair_at(sent_, 0, c)
-            extra = extra_at(got, c)
-            if ok is not None:
-                g0, g1 = (tuple(jnp.where(ok, t, 0.0) for t in g) for g in (g0, g1))
-                extra = jnp.where(ok, extra, 0.0)
-            g_rate = jnp.where(lane < L // 2, rl(extra, L // 2), extra)
-            g_scale = 1.0 / (1.0 + 6.0 * g_rate)
-            sums, line = inner(g0, lane, sub, swap), corner(extra)
-            first = []
-            for h in range(2):
-                value = (g0[h] + g_rate * (sums[h] + line[h] + g1[h] + own[h])) * g_scale
-                if ok is not None:
-                    value = jnp.where(ok, value, 0.0)
-                row = (h * NC + c) * BZ
-                kept_[row : row + BZ, :] = value
-                first.append(value)
-            planes.append(g0)
-            extras.append(extra)
-            firsts.append(first)
-        sides.append((planes, extras, firsts))
-    far_r, far_f = sides[1][0], sides[1][2]
+    near_g = [y_ghosts(near, None, c) for c in each]
+    far_g = [y_ghosts(far, far_ok, c) for c in each]
+    far_f = []
+    for c in each:
+        values = y_first_sweep(far, far_sent, far_ok, far_g[c], c, lane, sub, swap)
+        for h in range(2):
+            row = (h * NC + c) * BZ
+            y_far[row : row + BZ, :] = values[h]
+        far_f.append(values)
+    far_r = [g[0] for g in far_g]
 
     def by_side(which, c):
-        a, b = sides[0][which][c], sides[1][which][c]
-        if which == 1:
+        a, b = near_g[c][which], far_g[c][which]
+        if which == 2:
             return jnp.where(y_first, b, a), jnp.where(y_first, a, b)
         return [jnp.where(y_first, q, p) for p, q in zip(a, b)], [jnp.where(y_first, p, q) for p, q in zip(a, b)]
 
     faces_y = []
     for c in each:
         own, own1 = pair_at(far_sent, 0, c), pair_at(far_sent, 1, c)
-        sums, line = inner(own, lane, sub, swap), corner(extra_at(far_sent, c))
+        sums, line = inner(own, lane, sub, swap), corner(extra_at(far_sent, c), low_lane, high_lane)
         flux = [
             far_f[c][h] - (own[h] + rate[c] * (sums[h] + line[h] + own1[h] + far_r[c][h])) * scale[c] for h in range(2)
         ]
@@ -424,22 +476,10 @@
         faces_y.append(face + rs(face, 1))
     faces_x = []
     for c in each:
-        low_line, high_line = by_side(1, c)
-        planes = []
-        for part, kept_, at_low, ok in ((core_first, x_core, ~x_first, None), (link_first, x_link, x_first, link_ok)):
-            g_rate = kept_rate(part, c)
-            g_weight = g_rate / (1.0 + 6.0 * g_rate)
-            bottom = jnp.where(at_low, low_line, rl(low_line, -E))
-            top = jnp.where(at_low, rl(high_line, L - E), rl(high_line, L - 2 * E))
-            plane = []
-            for h, (line, there) in enumerate(((bottom, low_lane), (top, high_lane))):
-                row = (h * NC + c) * BZ
-                value = part[row : row + BZ, :] + g_weight * jnp.where(there, line, 0.0)
-                if ok is not None:
-                    value = jnp.where(ok, value, 0.0)
-                kept_[row : row + BZ, :] = value
-                plane.append(value)
-            planes.append(plane)
+        ghost = x_first_sweep(link_first, link_ok, x_first, *by_side(2, c), c, low_lane, high_lane)
+        for h in range(2):
+            row = (h * NC + c) * BZ
+            x_link[row : row + BZ, :] = ghost[h]
         low_r, high_r = by_side(0, c)
         at_0, at_15 = (strips(low_r, high_r, x, low_lane, high_lane) for x in (0, E - 1))
         cells_0, cells_15 = tile_at(partial, c, 0), tile_at(partial, c, E - 1)
@@ -447,7 +487,7 @@
         for h in range(2):
             cell = jnp.where(x_first, cells_0[h], cells_15[h])
             cell = cell + weight[c] * jnp.where(x_first, at_0[h], at_15[h])
-            flux.append(planes[1][h] - cell)
+            flux.append(ghost[h] - cell)
         face = coarse_plane(flux, par_y, lane, sub) * (rate[c] * masks[0:BZ, :])
         faces_x.append(face + rs(face, -1))
     faces_z = []
@@ -480,11 +520,7 @@
             sent[row : row + BZ, :] = jnp.where(y_first, columns[1], columns[0])
 
 
-def kept_rate(part, c):
-    return part[2 * PLANE + c * BZ : 2 * PLANE + c * BZ + BZ, :]
-
-
-def half_kernel(shape, kept, got, mine, sent):
+def half_kernel(shape, kept, got, _, mine, sent):
     gx, _, _ = place_of(shape)
     first = gx % 2 == 0
     top = subs() < 4
@@ -495,7 +531,7 @@
         sent[i * BZ : i * BZ + BZ, :] = jnp.where(first, rows[1], rows[0])
 
 
-def register_kernel(shape, mine, got, out):
+def register_kernel(shape, mine, got, _, out):
     x_first, y_first, _, _ = ends(shape)
     sub = subs()
     for h in range(2):
@@ -512,26 +548,33 @@
             out[0, 0, c, :, h * L : h * L + L] = t[:6]
 
 
-def smooth_kernel(shape, moved, rates, partial, near, far, x_core, x_link, y_near, y_far, out, first, held):
+def smooth_kernel(
+    comps, shape, moved, rates, partial, core_first, near, far, near_sent, x_link, y_far, _, out, done,
+    first, held, boxes, sem,
+):
+    done[...] = jnp.zeros((BZ, L), F32)
     x_first, y_first, _, far_ok = ends(shape)
     lane, sub = lanes(), subs()
     swap = swap_index(lane)
     low_lane, high_lane = lane < E, lane >= L - E
-    for c in range(NC):
+    copies = []
+    for c in comps:
         rate = rates[c * BZ : c * BZ + BZ, :]
         scale = 1.0 / (1.0 + 6.0 * rate)
         weight = rate * scale
 
-        def ghosts(a, b, a_first):
+        def by_side(a, b, a_first):
             low = [jnp.where(a_first, q, p) for p, q in zip(a, b)]
             high = [jnp.where(a_first, p, q) for p, q in zip(a, b)]
             return low, high
 
-        low, high = ghosts(pair_at(x_core, 0, c), pair_at(x_link, 0, c), x_first)
-        low_y, high_y = ghosts(pair_at(y_near, 0, c), pair_at(y_far, 0, c), y_first)
-        far_r = [jnp.where(far_ok, t, 0.0) for t in pair_at(far, 0, c)]
-        low_r, high_r = ghosts(pair_at(near, 0, c), far_r, y_first)
-
+        near_g, far_g = y_ghosts(near, None, c), y_ghosts(far, far_ok, c)
+        (low_line,), (high_line,) = by_side(near_g[2:], far_g[2:], y_first)
+        core = x_first_sweep(core_first, None, ~x_first, low_line, high_line, c, low_lane, high_lane)
+        low, high = by_side(core, pair_at(x_link, 0, c), x_first)
+        near_f = y_first_sweep(near, near_sent, None, near_g, c, lane, sub, swap)
+        low_y, high_y = by_side(near_f, pair_at(y_far, 0, c), y_first)
+        low_r, high_r = by_side(near_g[0], far_g[0], y_first)
         for x in range(E):
             edge = strips(low_r, high_r, x, low_lane, high_lane)
             row = (c * E + x) * BZ
@@ -549,7 +592,11 @@
                 held[h, row : row + BZ, :] = (start[h] + rate * (sums[h] + before[h] + after[h] + edge[h])) * scale
         for s in range(BZ):
             for h in range(2):
-                out[0, 0, s, c, :, h * L : h * L + L] = held[h, pl.ds(c * E * BZ + s, E, stride=BZ), :]
+                boxes[c, s, :, h * L : h * L + L] = held[h, pl.ds(c * E * BZ + s, E, stride=BZ), :]
+        copies.append(pltpu.make_async_copy(boxes.at[c], out.at[0, 0, :, c], sem.at[c]))
+        copies[-1].start()
+    for copy in copies:
+        copy.wait()
 
 
 def body(shape, fields_old, coeff_old, new_place, cf_mask):
@@ -577,59 +624,84 @@
     cf_mask = cf_mask.transpose(0, 2, 1, 3)
     big = (2, NC * E * BZ, L)
 
-    boxes, even, odd = call(
+    plane = ((2 * PLANE, L), "vmem")
+    even, odd, even_rest, odd_rest, boxes, slots, rates, masks = call(
         k(pack_kernel),
-        [(new_place, "any"), (coeff_old, "any"), (fields_old, "any")],
-        [((BZ, NC, E, 2 * L), "vmem"), ((PARCEL, 2 * L), "vmem"), ((PARCEL, 2 * L), "vmem")],
-        [SM((1, 1, BZ), I32), SM((1, NC, 1, BZ), F32), pltpu.SemaphoreType.DMA((3,))],
-    )
+        [(a, "hbm") for a in (new_place, coeff_old, cf_mask, fields_old)],
+        [
+            ((PARCEL, 2 * L), "vmem"),
+            ((PARCEL, 2 * L), "vmem"),
+            ((REST, 2 * L), "vmem"),
+            ((REST, 2 * L), "vmem"),
+            ((BZ, NC, E, 2 * L), "vmem"),
+            ((BZ, L), "vmem"),
+            ((PLANE, L), "vmem"),
+            ((3 * BZ, L), "vmem"),
+        ],
+        [
+            SM((1, 1, BZ), I32),
+            SM((1, NC, 1, BZ), F32),
+            SM((1, 3, 1, BZ), I32),
+            pltpu.SemaphoreType.DMA((4,)),
+        ],
+    )
+    even_got = swap(even, even_pairs)
     odd_got = swap(odd, odd_pairs)
-    even_got = swap(even, even_pairs)
-    stayed, rates, masks = call(
+    even_rest_got = swap(even_rest, even_pairs)
+    odd_rest_got = swap(odd_rest, odd_pairs)
+    stayed, rates = call(
         k(stay_kernel),
-        [(new_place, "smem"), (coeff_old, "smem"), (cf_mask, "smem"), (boxes, "vmem")],
-        [(big, "vmem"), ((PLANE, L), "vmem"), ((3 * BZ, L), "vmem")],
+        [(a, "vmem") for a in (boxes, slots, rates)],
+        [(big, "vmem"), ((PLANE, L), "vmem")],
     )
     core, link, rates = call(
         k(xsend_kernel),
-        [(even_got, "vmem"), (odd_got, "vmem"), (stayed, "vmem"), (rates, "vmem")],
-        [((FACE + PLANE, L), "vmem"), ((FACE + PLANE, L), "vmem"), ((PLANE, L), "vmem")],
-    )
+        [(a, "vmem") for a in (even_got, odd_got, stayed, rates)],
+        [((XFACE, L), "vmem"), ((XFACE, L), "vmem"), ((PLANE, L), "vmem")],
+    )
+    core_got = swap(core, core_pairs)
     link_got = swap(link, link_pairs)
-    core_got = swap(core, core_pairs)
     moved, near, far = call(
         k(merge_kernel),
-        [(even_got, "vmem"), (odd_got, "vmem"), (stayed, "vmem")],
+        [(a, "vmem") for a in (odd_got, even_got, odd_rest_got, even_rest_got, stayed)],
         [(big, "vmem"), ((FACE, L), "vmem"), ((FACE, L), "vmem")],
     )
     near, far = call(
         k(ysend_kernel),
-        [(core_got, "vmem"), (link_got, "vmem"), (rates, "vmem"), (near, "vmem"), (far, "vmem")],
-        [((FACE + PLANE, L), "vmem"), ((FACE + PLANE, L), "vmem")],
-    )
+        [(a, "vmem") for a in (link_got, core_got, rates, near, far)],
+        [((YFACE, L), "vmem"), ((YFACE, L), "vmem")],
+    )
+    near_got = swap(near, even_pairs)
     far_got = swap(far, far_pairs)
-    near_got = swap(near, even_pairs)
     part, core_first, link_first, tops = call(
         k(sweep_kernel),
-        [(a, "vmem") for a in (moved, rates, core_got, link_got, core, link)],
+        [(a, "vmem") for a in (moved, rates, link_got, core_got, core, link)],
         [(big, "vmem"), ((3 * PLANE, L), "vmem"), ((3 * PLANE, L), "vmem"), ((PLANE, L), "vmem")],
     )
-    plane = ((2 * PLANE, L), "vmem")
-    x_core, x_link, y_near, y_far, kept, sent = call(
+    x_link, y_far, kept, sent = call(
         k(flux_kernel),
-        [(a, "vmem") for a in (part, rates, masks, tops, core_first, link_first, near_got, far_got, near, far)],
-        [plane] * 6,
+        [(a, "vmem") for a in (part, rates, masks, tops, link_first, near_got, far_got, far)],
+        [plane] * 4,
     )
     got = swap(sent, even_pairs)
-    (smoothed,) = call(
-        k(smooth_kernel),
-        [(a, "vmem") for a in (moved, rates, part, near_got, far_got, x_core, x_link, y_near, y_far)],
-        [((1, 1, BZ, NC, E, 2 * L), "out")],
-        [VM(big, F32), VM(big, F32)],
-    )
-    mine, sent = call(k(half_kernel), [(kept, "vmem"), (got, "vmem")], [plane, plane])
+
+    def smooth(comps, before, aliases):
+        ins = (moved, rates, part, core_first, near_got, far_got, near, x_link, y_far)
+        return call(
+            functools.partial(smooth_kernel, comps, shape),
+            [(a, "vmem") for a in ins] + [before],
+            [((1, 1, BZ, NC, E, 2 * L), "hbm"), ((BZ, L), "vmem")],
+            [VM(big, F32), VM(big, F32), VM((NC, BZ, E, 2 * L), F32), pltpu.SemaphoreType.DMA((NC,))],
+            aliases,
+        )
+
+    smoothed, done = smooth((0, 1, 2), (masks, "vmem"), None)
+    mine, sent = call(k(half_kernel), [(kept, "vmem"), (got, "vmem"), (done, "vmem")], [plane, plane])
     got = swap(sent, core_pairs)
-    (registers,) = call(k(register_kernel), [(mine, "vmem"), (got, "vmem")], [((1, 1, NC, 6, 2 * L), "out")])
+    smoothed, done = smooth((3, 4), (smoothed, "hbm"), {9: 0})
+    (registers,) = call(
+        k(register_kernel), [(mine, "vmem"), (got, "vmem"), (done, "vmem")], [((1, 1, NC, 6, 2 * L), "out")]
+    )
     return smoothed, registers
 
 

time: 34.2 us -> 31.1 us (0.909)
  waiting for transfers between devices: 13.5 us -> 9.03 us
  starting transfers between devices: 11.2 us -> 13 us
  local copies, waits for them, and re-layouts: 1.3 us -> 0.64 us
    ppermute x8 -> x10, waiting for transfers between devices: 13.5 us -> 9.03 us  [swap(): return lax.ppermute(array, both, pairs)]
    ppermute x8 -> x10, starting transfers between devices: 11.2 us -> 13 us  [swap(): return lax.ppermute(array, both, pairs)]
    unnamed x7 -> x1, local copies, waits for them, and re-layouts: 1.3 us -> 0.64 us
    pallas_call x10 -> x11, Pallas kernels: 7.23 us -> 7.49 us  [call(): pl.pallas_call(kernel, out_shape=shapes, in_specs=in_specs, out_specs=out...]
  transfers between devices with their start and end apart: 8 -> 10, of which waited for: 5 -> 6; matrix products, arithmetic and copies ran while one was open for 0% -> 0% of each run, Pallas kernels for 14% -> 17%
where the time goes in v3:
time: 31.1 us; the launch traced here: 30.9 us
  starting transfers between devices  13 us (42%)
  waiting for transfers between devices  9.03 us (29%)
  Pallas kernels  7.49 us (24%)
  between operations  0.73 us (2%)
  local copies, waits for them, and re-layouts  0.64 us (2%)
    ppermute x10, starting transfers between devices, swap(): return lax.ppermute(array, both, pairs)  13 us
    ppermute x10, waiting for transfers between devices, swap(): return lax.ppermute(array, both, pairs)  9.03 us
    pallas_call x11, Pallas kernels, call(): pl.pallas_call(kernel, out_shape=shapes, in_specs=in_specs, out_specs=out...  7.49 us
    unnamed x1, local copies, waits for them, and re-layouts  0.64 us
  transfers between devices with their start and end apart: 10, of which 6 were waited for; matrix products, arithmetic and copies ran while one was open for 0% of the time, Pallas kernels for 17%

profile of v3, /device:TPU:0, one launch (start us, length us, event | category | flops | bytes accessed | tf_op | source)
XLA Modules:
  0.0 30.9 jit_solution(1875532065614696464)
XLA Ops:
  0.6 1.2 %shard_map.59 = (f32[56,256]{1,0:T(8,128)S(1)}, f32[56,256]{1,0:T(8,128)S(1)}, f32[120,256]{1,0:T(8,128)S(1)}, f32[120,256]{1,0:T(8,128)S(1)}, f32[8,5,16,256]{3...) custom-call(s32[1,1,8]{2,1,0:T(1,128)} %place_hbm.1, ...), custom_call_target="tpu_custom_call" | custom-call | flops 1000 | tf_op jit(solution)/shard_map/pallas_call | solution.py:52
  1.8 6.4 %collective-permute-start = (f32[56,256]{1,0:T(8,128)S(1)}, f32[56,256]{1,0:T(8,128)S(1)}, u32[]{:S(2)}, u32[]{:S(2)}) collective-permute-start(f32[56,256]{1,0:T(8,128)S(1)} %get-tuple-element.34), channel_id=1, source_target_pairs={{0,31},{1,2},{2,1},{3,4},{4,3},{5,6},{6,5},{7,8},{8,7},{9,10},{10,... | collective-permute-start | bytes 172040 | tf_op jit(solution)/shard_map/ppermute | solution.py:608
  8.3 1.3 %collective-permute-start.2 = (f32[120,256]{1,0:T(8,128)S(1)}, f32[120,256]{1,0:T(8,128)S(1)}, u32[]{:S(2)}, u32[]{:S(2)}) collective-permute-start(f32[120,256]{1,0:T(8,128)S(1)} %get-tuple-element.36), channel_id=1, source_target_pairs={{0,31},{1,2},{2,1},{3,4},{4,3},{5,6},{6,5},{7,8},{8,7},{9,10},{10,... | collective-permute-start | bytes 368648 | tf_op jit(solution)/shard_map/ppermute | solution.py:608
  9.6 0.7 %collective-permute-start.3 = (f32[120,256]{1,0:T(8,128)S(1)}, f32[120,256]{1,0:T(8,128)S(1)}, u32[]{:S(2)}, u32[]{:S(2)}) collective-permute-start(f32[120,256]{1,0:T(8,128)S(1)} %get-tuple-element.37), channel_id=1, source_target_pairs={{0,1},{1,0},{2,3},{3,2},{4,5},{5,4},{6,7},{7,6},{8,9},{9,8},{10,11... | collective-permute-start | bytes 368648 | tf_op jit(solution)/shard_map/ppermute | solution.py:608
  10.3 0.3 shard_map.60
  10.6 0.1 collective-permute-done.odd
  10.6 1.8 %collective-permute-done.1.even = f32[56,256]{1,0:T(8,128)S(1)} collective-permute-done((f32[56,256]{1,0:T(8,128)S(1)}, f32[56,256]{1,0:T(8,128)S(1)}, u32[]{:S(2)}, u32[]{:S(2)}) %collective-permute-start.1) | collective-permute-done | bytes 57376 | tf_op jit(solution)/shard_map/ppermute | solution.py:608
  12.5 0.1 shard_map.62
  12.5 0.5 %collective-permute-start.4 = (f32[168,128]{1,0:T(8,128)S(1)}, f32[168,128]{1,0:T(8,128)S(1)}, u32[]{:S(2)}, u32[]{:S(2)}) collective-permute-start(f32[168,128]{1,0:T(8,128)S(1)} %get-tuple-element.45.link_sent), channel_id=1, source_target_pairs={{0,24},{1,25},{2,26},{3,27},{4,28},{5,29},{6,30},{7,31},{8,16},{9,... | collective-permute-start | bytes 258056 | tf_op jit(solution)/shard_map/ppermute | solution.py:608
  13.0 0.6 %collective-permute-start.5 = (f32[168,128]{1,0:T(8,128)S(1)}, f32[168,128]{1,0:T(8,128)S(1)}, u32[]{:S(2)}, u32[]{:S(2)}) collective-permute-start(f32[168,128]{1,0:T(8,128)S(1)} %get-tuple-element.46.core_sent), channel_id=1, source_target_pairs={{0,8},{1,9},{2,10},{3,11},{4,12},{5,13},{6,14},{7,15},{8,0},{9,1},... | collective-permute-start | bytes 258056 | tf_op jit(solution)/shard_map/ppermute | solution.py:608
  13.6 3.9 %collective-permute-done.2.odd_rest = f32[120,256]{1,0:T(8,128)S(1)} collective-permute-done((f32[120,256]{1,0:T(8,128)S(1)}, f32[120,256]{1,0:T(8,128)S(1)}, u32[]{:S(2)}, u32[]{:S(2)}) %collective-permute-start.2) | collective-permute-done | bytes 122912 | tf_op jit(solution)/shard_map/ppermute | solution.py:608
  17.6 0.2 collective-permute-done.3.even_rest
  17.8 0.4 %shard_map.61 = (f32[2,640,128]{2,1,0:T(8,128)S(1)}, f32[160,128]{1,0:T(8,128)S(1)}, f32[160,128]{1,0:T(8,128)S(1)}) custom-call(f32[56,256]{1,0:T(8,128)S(1)} %collective-permute-done.odd, f32[56,256]{1,0:T(8,128)S(1)} %collective-permute-done.1.even, f32[120,256]{1,0:T(8,128)S(1)} %collective-permute-done.2.odd_rest, ...), custom_call_target="tpu_custom_call" | custom-call | flops 1000 | tf_op jit(solution)/shard_map/pallas_call | solution.py:52
  18.2 0.1 shard_map.64
  18.3 0.3 %collective-permute-start.6 = (f32[176,128]{1,0:T(8,128)S(1)}, f32[176,128]{1,0:T(8,128)S(1)}, u32[]{:S(2)}, u32[]{:S(2)}) collective-permute-start(f32[176,128]{1,0:T(8,128)S(1)} %get-tuple-element.51.near_sent), channel_id=1, source_target_pairs={{0,1},{1,0},{2,3},{3,2},{4,5},{5,4},{6,7},{7,6},{8,9},{9,8},{10,11... | collective-permute-start | bytes 270344 | tf_op jit(solution)/shard_map/ppermute | solution.py:608
  18.7 1.4 %shard_map.63 = (f32[2,640,128]{2,1,0:T(8,128)S(1)}, f32[120,128]{1,0:T(8,128)S(1)}, f32[120,128]{1,0:T(8,128)S(1)}, f32[40,128]{1,0:T(8,128)S(1)}) custom-call(f32[2,640,128]{2,1,0:T(8,128)S(1)} %get-tuple-element.42.moved, f32[40,128]{1,0:T(8,128)S(1)} %get-tuple-element.44.rates.moved_rates, f32[168,128]{1,0:T(8,128)S(1)} %collective-permute-done.4.link, ...), custom_call_target="tpu_custom_call" | custom-call | flops 1000 | tf_op jit(solution)/shard_map/pallas_call | solution.py:52
  20.1 2.8 %collective-permute-done.6.near = f32[176,128]{1,0:T(8,128)S(1)} collective-permute-done((f32[176,128]{1,0:T(8,128)S(1)}, f32[176,128]{1,0:T(8,128)S(1)}, u32[]{:S(2)}, u32[]{:S(2)}) %collective-permute-start.6) | collective-permute-done | bytes 90144 | tf_op jit(solution)/shard_map/ppermute | solution.py:608
  22.9 0.8 %shard_map.65 = (f32[80,128]{1,0:T(8,128)S(1)}, f32[80,128]{1,0:T(8,128)S(1)}, f32[80,128]{1,0:T(8,128)S(1)}, f32[80,128]{1,0:T(8,128)S(1)}) custom-call(f32[2,640,128]{2,1,0:T(8,128)S(1)} %get-tuple-element.47.partial, f32[40,128]{1,0:T(8,128)S(1)} %get-tuple-element.44.rates.moved_rates, f32[24,128]{1,0:T(8,128)S(1)} %get-tuple-element.53.masks._, ...), custom_call_target="tpu_custom_call" | custom-call | flops 1000 | tf_op jit(solution)/shard_map/pallas_call | solution.py:52
  23.7 3.0 %collective-permute-start.8 = (f32[80,128]{1,0:T(8,128)S(1)}, f32[80,128]{1,0:T(8,128)S(1)}, u32[]{:S(2)}, u32[]{:S(2)}) collective-permute-start(f32[80,128]{1,0:T(8,128)S(1)} %get-tuple-element.61), channel_id=1, source_target_pairs={{0,1},{1,0},{2,3},{3,2},{4,5},{5,4},{6,7},{7,6},{8,9},{9,8},{10,11... | collective-permute-start | bytes 122888 | tf_op jit(solution)/shard_map/ppermute | solution.py:608
  26.7 1.8 %shard_map.66 = (f32[1,1,8,5,16,256]{5,4,3,2,1,0:T(8,128)}, f32[8,128]{1,0:T(8,128)S(1)}) custom-call(f32[2,640,128]{2,1,0:T(8,128)S(1)} %get-tuple-element.42.moved, f32[40,128]{1,0:T(8,128)S(1)} %get-tuple-element.44.rates.moved_rates, f32[2,640,128]{2,1,0:T(8,128)S(1)} %get-tuple-element.47.partial, f32[120,128]{1,0:T(8,128)S(1)} %get-tuple-element.48.core_first, ...), custom_call_target="tpu_custom_call" | custom-call | flops 1000 | tf_op jit(solution)/shard_map/pallas_call | solution.py:52
  28.6 0.2 collective-permute-done.8.got
  28.7 0.1 collective-permute-start.9
  28.8 1.4 %shard_map.67 = (f32[1,1,8,5,16,256]{5,4,3,2,1,0:T(8,128)}, f32[8,128]{1,0:T(8,128)S(1)}) custom-call(f32[2,640,128]{2,1,0:T(8,128)S(1)} %get-tuple-element.42.moved, f32[40,128]{1,0:T(8,128)S(1)} %get-tuple-element.44.rates.moved_rates, f32[2,640,128]{2,1,0:T(8,128)S(1)} %get-tuple-element.47.partial, ...), custom_call_target="tpu_custom_call", output_to_operand_aliasing={{0}: (9, {})} | custom-call | flops 1000 | tf_op jit(solution)/shard_map/pallas_call | solution.py:52
  30.3 0.6 %copy.7 = f32[1,1,5,6,256]{4,1,3,2,0:T(1,128)} copy(f32[1,1,5,6,256]{4,3,2,1,0:T(8,128)S(1)} %shard_map.69) | data formatting | bytes 61440
  (8 shorter events, 0.1 us)
Async XLA Ops:
  1.8 8.8 %collective-permute-start = (f32[56,256]{1,0:T(8,128)S(1)}, f32[56,256]{1,0:T(8,128)S(1)}, u32[]{:S(2)}, u32[]{:S(2)}) collective-permute-start(f32[56,256]{1,0:T(8,128)S(1)} %get-tuple-element.34), channel_id=1, source_target_pairs={{0,31},{1,2},{2,1},{3,4},{4,3},{5,6},{6,5},{7,8},{8,7},{9,10},{10,... | collective-permute-start | bytes 172040 | tf_op jit(solution)/shard_map/ppermute | solution.py:608
  8.3 4.2 %collective-permute-start.1 = (f32[56,256]{1,0:T(8,128)S(1)}, f32[56,256]{1,0:T(8,128)S(1)}, u32[]{:S(2)}, u32[]{:S(2)}) collective-permute-start(f32[56,256]{1,0:T(8,128)S(1)} %get-tuple-element.35), channel_id=1, source_target_pairs={{0,1},{1,0},{2,3},{3,2},{4,5},{5,4},{6,7},{7,6},{8,9},{9,8},{10,11... | collective-permute-start | bytes 172040 | tf_op jit(solution)/shard_map/ppermute | solution.py:608
  8.3 9.3 %collective-permute-start.2 = (f32[120,256]{1,0:T(8,128)S(1)}, f32[120,256]{1,0:T(8,128)S(1)}, u32[]{:S(2)}, u32[]{:S(2)}) collective-permute-start(f32[120,256]{1,0:T(8,128)S(1)} %get-tuple-element.36), channel_id=1, source_target_pairs={{0,31},{1,2},{2,1},{3,4},{4,3},{5,6},{6,5},{7,8},{8,7},{9,10},{10,... | collective-permute-start | bytes 368648 | tf_op jit(solution)/shard_map/ppermute | solution.py:608
  9.6 8.2 %collective-permute-start.3 = (f32[120,256]{1,0:T(8,128)S(1)}, f32[120,256]{1,0:T(8,128)S(1)}, u32[]{:S(2)}, u32[]{:S(2)}) collective-permute-start(f32[120,256]{1,0:T(8,128)S(1)} %get-tuple-element.37), channel_id=1, source_target_pairs={{0,1},{1,0},{2,3},{3,2},{4,5},{5,4},{6,7},{7,6},{8,9},{9,8},{10,11... | collective-permute-start | bytes 368648 | tf_op jit(solution)/shard_map/ppermute | solution.py:608
  12.5 5.7 %collective-permute-start.4 = (f32[168,128]{1,0:T(8,128)S(1)}, f32[168,128]{1,0:T(8,128)S(1)}, u32[]{:S(2)}, u32[]{:S(2)}) collective-permute-start(f32[168,128]{1,0:T(8,128)S(1)} %get-tuple-element.45.link_sent), channel_id=1, source_target_pairs={{0,24},{1,25},{2,26},{3,27},{4,28},{5,29},{6,30},{7,31},{8,16},{9,... | collective-permute-start | bytes 258056 | tf_op jit(solution)/shard_map/ppermute | solution.py:608
  13.0 5.2 %collective-permute-start.5 = (f32[168,128]{1,0:T(8,128)S(1)}, f32[168,128]{1,0:T(8,128)S(1)}, u32[]{:S(2)}, u32[]{:S(2)}) collective-permute-start(f32[168,128]{1,0:T(8,128)S(1)} %get-tuple-element.46.core_sent), channel_id=1, source_target_pairs={{0,8},{1,9},{2,10},{3,11},{4,12},{5,13},{6,14},{7,15},{8,0},{9,1},... | collective-permute-start | bytes 258056 | tf_op jit(solution)/shard_map/ppermute | solution.py:608
  18.3 4.6 %collective-permute-start.6 = (f32[176,128]{1,0:T(8,128)S(1)}, f32[176,128]{1,0:T(8,128)S(1)}, u32[]{:S(2)}, u32[]{:S(2)}) collective-permute-start(f32[176,128]{1,0:T(8,128)S(1)} %get-tuple-element.51.near_sent), channel_id=1, source_target_pairs={{0,1},{1,0},{2,3},{3,2},{4,5},{5,4},{6,7},{7,6},{8,9},{9,8},{10,11... | collective-permute-start | bytes 270344 | tf_op jit(solution)/shard_map/ppermute | solution.py:608
  18.7 4.2 %collective-permute-start.7 = (f32[176,128]{1,0:T(8,128)S(1)}, f32[176,128]{1,0:T(8,128)S(1)}, u32[]{:S(2)}, u32[]{:S(2)}) collective-permute-start(f32[176,128]{1,0:T(8,128)S(1)} %get-tuple-element.52.far_sent), channel_id=1, source_target_pairs={{0,8},{1,2},{2,1},{3,4},{4,3},{5,6},{6,5},{7,15},{8,0},{9,10},{10,... | collective-permute-start | bytes 270344 | tf_op jit(solution)/shard_map/ppermute | solution.py:608
  23.7 5.0 %collective-permute-start.8 = (f32[80,128]{1,0:T(8,128)S(1)}, f32[80,128]{1,0:T(8,128)S(1)}, u32[]{:S(2)}, u32[]{:S(2)}) collective-permute-start(f32[80,128]{1,0:T(8,128)S(1)} %get-tuple-element.61), channel_id=1, source_target_pairs={{0,1},{1,0},{2,3},{3,2},{4,5},{5,4},{6,7},{7,6},{8,9},{9,8},{10,11... | collective-permute-start | bytes 122888 | tf_op jit(solution)/shard_map/ppermute | solution.py:608
  28.7 1.5 %collective-permute-start.9 = (f32[80,128]{1,0:T(8,128)S(1)}, f32[80,128]{1,0:T(8,128)S(1)}, u32[]{:S(2)}, u32[]{:S(2)}) collective-permute-start(f32[80,128]{1,0:T(8,128)S(1)} %get-tuple-element.64), channel_id=1, source_target_pairs={{0,8},{1,9},{2,10},{3,11},{4,12},{5,13},{6,14},{7,15},{8,0},{9,1},... | collective-permute-start | bytes 122888 | tf_op jit(solution)/shard_map/ppermute | solution.py:608

commit v4 on v3

--- a/solution.py
+++ b/solution.py
@@ -19,8 +19,7 @@
 FACE = 4 * PLANE
 EDGES = (0, 1, E - 2, E - 1)
 AHEAD = MOVE * NC * 4
-LABELS = AHEAD + MOVE * NC
-PARCEL = 56
+PARCEL = 48
 REST = MOVE * NC * 12
 XFACE = FACE + BZ
 YFACE = FACE + 2 * BZ
@@ -35,9 +34,6 @@
         if space == "vmem":
             given.append(pltpu.with_memory_space_constraint(array, VM))
             in_specs.append(pl.BlockSpec(memory_space=VM))
-        elif space == "smem":
-            given.append(array)
-            in_specs.append(pl.BlockSpec(memory_space=SM))
         else:
             given.append(pltpu.with_memory_space_constraint(array, pltpu.HBM))
             in_specs.append(pl.BlockSpec(memory_space=pltpu.HBM))
@@ -90,48 +86,60 @@
     return gx, gy, gx * mesh_shape[1] + gy
 
 
+def sources_of(place, owner):
+    count = jnp.int32(0)
+    sources = [jnp.int32(0)] * MOVE
+    labels = [jnp.int32(0)] * MOVE
+    for s in range(BZ):
+        value = place[s]
+        hit = value // BZ == owner
+        for k in range(MOVE):
+            taken = hit & (count == k)
+            sources[k] = jnp.where(taken, s, sources[k])
+            labels[k] = jnp.where(taken, value % BZ + 1, labels[k])
+        count = count + hit.astype(I32)
+    return sources, labels
+
+
+def fill_rest(rest, boxes, sources):
+    for k in range(MOVE):
+        for c in range(NC):
+            box = k * NC + c
+            rest[12 * box : 12 * box + 12, :] = boxes[sources[k], c, 2 : E - 2]
+
+
 def pack_kernel(
     shape, place_hbm, coeff_hbm, mask_hbm, fields_hbm, even, odd, even_rest, odd_rest, boxes, slots, rates, masks,
-    place, coeff, mask, sem,
+    place_s, coeff, mask, sem,
 ):
-    pairs = ((fields_hbm.at[0, 0], boxes), (place_hbm, place), (coeff_hbm, coeff), (mask_hbm, mask))
+    pairs = ((fields_hbm.at[0, 0], boxes), (place_hbm, place_s), (coeff_hbm, coeff), (mask_hbm, mask))
     copies = [pltpu.make_async_copy(a, b, sem.at[i]) for i, (a, b) in enumerate(pairs)]
     for copy in copies:
         copy.start()
     _, _, me = place_of(shape)
     ahead = 1 - 2 * (me % 2)
+    lane = lax.broadcasted_iota(I32, (1, L), 1)
     for copy in copies[1:]:
         copy.wait()
-    chosen = []
-    for out, owner in ((even, me + ahead), (odd, me - ahead)):
-        count = jnp.int32(0)
-        sources = [jnp.int32(0)] * MOVE
-        labels = [jnp.int32(0)] * MOVE
-        for s in range(BZ):
-            value = place[0, 0, s]
-            hit = value // BZ == owner
-            for k in range(MOVE):
-                taken = hit & (count == k)
-                sources[k] = jnp.where(taken, s, sources[k])
-                labels[k] = jnp.where(taken, value % BZ + 1, labels[k])
-            count = count + hit.astype(I32)
-        chosen.append(sources)
-        out[LABELS + MOVE : PARCEL, :] = jnp.zeros((PARCEL - LABELS - MOVE, 2 * L), F32)
+    place = [place_s[0, 0, s] for s in range(BZ)]
+    chosen = [sources_of(place, me + ahead), sources_of(place, me - ahead)]
+    for out, (sources, labels) in zip((even, odd), chosen):
+        out[AHEAD:PARCEL, :] = jnp.zeros((PARCEL - AHEAD, 2 * L), F32)
         for k in range(MOVE):
-            out[LABELS + k : LABELS + k + 1, :] = jnp.full((1, 2 * L), labels[k].astype(F32), F32)
+            out[AHEAD + k : AHEAD + k + 1, L:] = jnp.full((1, L), labels[k].astype(F32), F32)
+            line = jnp.zeros((1, L), F32)
             for c in range(NC):
-                row = AHEAD + k * NC + c
-                out[row : row + 1, :] = jnp.full((1, 2 * L), coeff[0, c, 0, sources[k]], F32)
+                line = jnp.where(lane == c, coeff[0, c, 0, sources[k]], line)
+            out[AHEAD + k : AHEAD + k + 1, :L] = line
     for s in range(BZ):
-        value = place[0, 0, s]
-        label = jnp.where(value // BZ == me, value % BZ + 1, 0)
+        label = jnp.where(place[s] // BZ == me, place[s] % BZ + 1, 0)
         slots[s : s + 1, :] = jnp.full((1, L), label.astype(F32), F32)
         for c in range(NC):
             rates[s * NC + c : s * NC + c + 1, :] = jnp.full((1, L), coeff[0, c, 0, s], F32)
         for d in range(3):
             masks[d * BZ + s : d * BZ + s + 1, :] = jnp.full((1, L), mask[0, d, 0, s].astype(F32), F32)
     copies[0].wait()
-    for out, rest, sources in ((even, even_rest, chosen[0]), (odd, odd_rest, chosen[1])):
+    for out, rest, (sources, _) in zip((even, odd), (even_rest, odd_rest), chosen):
         for k in range(MOVE):
             for c in range(NC):
                 box = k * NC + c
@@ -162,7 +170,7 @@
     found = []
     for parcel in (even, odd):
         for k in range(MOVE):
-            label = parcel[LABELS + k : LABELS + k + 1, :L]
+            label = parcel[AHEAD + k : AHEAD + k + 1, L:]
             found.append((parcel, k, label == (sub + 1).astype(F32)))
     return found
 
@@ -196,8 +204,8 @@
     for c in range(NC):
         tile = rates[c * BZ : c * BZ + BZ, :]
         for parcel, k, hit in found:
-            at = AHEAD + k * NC + c
-            tile = jnp.where(hit, parcel[at : at + 1, :L], tile)
+            line = jnp.broadcast_to(parcel[AHEAD + k : AHEAD + k + 1, :L], (BZ, L))
+            tile = jnp.where(hit, spread(line, c), tile)
         all_rates[c * BZ : c * BZ + BZ, :] = tile
         together = jnp.where(lane % L == c, tile, together)
         for layer in range(2):
@@ -211,7 +219,7 @@
     link[FACE:, :] = together
 
 
-def merge_kernel(shape, odd, even, odd_rest, even_rest, moved, out, near, far):
+def merge_kernel(shape, even, odd, even_rest, odd_rest, moved, out, near, far):
     _, gy, _ = place_of(shape)
     first = gy % 2 == 0
     found = arrivals(even, odd)
@@ -434,7 +442,7 @@
 
 
 def flux_kernel(
-    shape, partial, moved_rates, masks, tops, link_first, near, far, far_sent, x_link, y_far, kept, sent
+    shape, partial, moved_rates, masks, tops, link_first, far, near, far_sent, _, y_far, kept, sent
 ):
     x_first, y_first, link_ok, far_ok = ends(shape)
     gx, gy, _ = place_of(shape)
@@ -477,9 +485,6 @@
     faces_x = []
     for c in each:
         ghost = x_first_sweep(link_first, link_ok, x_first, *by_side(2, c), c, low_lane, high_lane)
-        for h in range(2):
-            row = (h * NC + c) * BZ
-            x_link[row : row + BZ, :] = ghost[h]
         low_r, high_r = by_side(0, c)
         at_0, at_15 = (strips(low_r, high_r, x, low_lane, high_lane) for x in (0, E - 1))
         cells_0, cells_15 = tile_at(partial, c, 0), tile_at(partial, c, E - 1)
@@ -531,7 +536,7 @@
         sent[i * BZ : i * BZ + BZ, :] = jnp.where(first, rows[1], rows[0])
 
 
-def register_kernel(shape, mine, got, _, out):
+def register_kernel(shape, mine, got, out):
     x_first, y_first, _, _ = ends(shape)
     sub = subs()
     for h in range(2):
@@ -548,48 +553,75 @@
             out[0, 0, c, :, h * L : h * L + L] = t[:6]
 
 
+def second_kernel(shape, moved, rates, partial, core_first, link_first, out):
+    x_first, _, _, _ = ends(shape)
+    lane, sub = lanes(), subs()
+    swap = swap_index(lane)
+    for c in range(NC):
+        rate = rates[c * BZ : c * BZ + BZ, :]
+        core, link = pair_at(core_first, 0, c), pair_at(link_first, 0, c)
+        low = [jnp.where(x_first, b, a) for a, b in zip(core, link)]
+        high = [jnp.where(x_first, a, b) for a, b in zip(core, link)]
+        for x in range(E):
+            here = tile_at(partial, c, x)
+            before = low if x == 0 else tile_at(partial, c, x - 1)
+            after = high if x == E - 1 else tile_at(partial, c, x + 1)
+            sums = inner(here, lane, sub, swap)
+            start = tile_at(moved, c, x)
+            row = (c * E + x) * BZ
+            for h in range(2):
+                out[h, row : row + BZ, :] = start[h] + rate * (sums[h] + before[h] + after[h])
+
+
 def smooth_kernel(
-    comps, shape, moved, rates, partial, core_first, near, far, near_sent, x_link, y_far, _, out, done,
-    first, held, boxes, sem,
+    shape, rates, partial, core_first, link_first, far, near, near_sent, y_far, out, done, planes, held, boxes, sem
 ):
     done[...] = jnp.zeros((BZ, L), F32)
     x_first, y_first, _, far_ok = ends(shape)
     lane, sub = lanes(), subs()
     swap = swap_index(lane)
     low_lane, high_lane = lane < E, lane >= L - E
+
+    def by_side(a, b, a_first):
+        low = [jnp.where(a_first, q, p) for p, q in zip(a, b)]
+        high = [jnp.where(a_first, p, q) for p, q in zip(a, b)]
+        return low, high
+
+    for c in range(NC):
+        rate = rates[c * BZ : c * BZ + BZ, :]
+        weight = rate / (1.0 + 6.0 * rate)
+        near_g, far_g = y_ghosts(near, None, c), y_ghosts(far, far_ok, c)
+        near_f = y_first_sweep(near, near_sent, None, near_g, c, lane, sub, swap)
+        ghosts_f = by_side(near_f, pair_at(y_far, 0, c), y_first)
+        ghosts_r = by_side(near_g[0], far_g[0], y_first)
+        lines = by_side(near_g[2:], far_g[2:], y_first)
+        x_rates = [ref[2 * PLANE + c * BZ : 2 * PLANE + c * BZ + BZ, :] for ref in (core_first, link_first)]
+        x_weights = [t / (1.0 + 6.0 * t) for t in x_rates]
+        (low_w,), (high_w,) = by_side(x_weights[:1], x_weights[1:], x_first)
+        for side in range(2):
+            added = [weight * t for t in ghosts_r[side]]
+            (line,) = lines[side]
+            sums = inner(added, lane, sub, swap)
+            ends_ = (jnp.where(low_lane, low_w * line, 0.0), jnp.where(high_lane, high_w * rl(line, L - 2 * E), 0.0))
+            for h in range(2):
+                row = ((side * 2 + h) * NC + c) * BZ
+                planes[0, row : row + BZ, :] = rate * (sums[h] + ends_[h] + ghosts_f[side][h])
+                planes[1, row : row + BZ, :] = rate * added[h]
+    next_low = (lane >= E) & (lane < 2 * E)
+    next_high = (lane >= L - 2 * E) & (lane < L - E)
     copies = []
-    for c in comps:
+    for c in range(NC):
         rate = rates[c * BZ : c * BZ + BZ, :]
         scale = 1.0 / (1.0 + 6.0 * rate)
-        weight = rate * scale
-
-        def by_side(a, b, a_first):
-            low = [jnp.where(a_first, q, p) for p, q in zip(a, b)]
-            high = [jnp.where(a_first, p, q) for p, q in zip(a, b)]
-            return low, high
-
-        near_g, far_g = y_ghosts(near, None, c), y_ghosts(far, far_ok, c)
-        (low_line,), (high_line,) = by_side(near_g[2:], far_g[2:], y_first)
-        core = x_first_sweep(core_first, None, ~x_first, low_line, high_line, c, low_lane, high_lane)
-        low, high = by_side(core, pair_at(x_link, 0, c), x_first)
-        near_f = y_first_sweep(near, near_sent, None, near_g, c, lane, sub, swap)
-        low_y, high_y = by_side(near_f, pair_at(y_far, 0, c), y_first)
-        low_r, high_r = by_side(near_g[0], far_g[0], y_first)
         for x in range(E):
-            edge = strips(low_r, high_r, x, low_lane, high_lane)
             row = (c * E + x) * BZ
-            for h in range(2):
-                first[h, row : row + BZ, :] = partial[h, row : row + BZ, :] + weight * edge[h]
-        for x in range(E):
-            here = tile_at(first, c, x)
-            before = low if x == 0 else tile_at(first, c, x - 1)
-            after = high if x == E - 1 else tile_at(first, c, x + 1)
-            sums = inner(here, lane, sub, swap)
-            edge = strips(low_y, high_y, x, low_lane, high_lane)
-            start = tile_at(moved, c, x)
-            row = (c * E + x) * BZ
-            for h in range(2):
-                held[h, row : row + BZ, :] = (start[h] + rate * (sums[h] + before[h] + after[h] + edge[h])) * scale
+            shift = E * (x % 8)
+            for h, (here, there, at) in enumerate(((low_lane, next_low, 0), (high_lane, next_high, L - E))):
+                plane = ((h * 2 + x // 8) * NC + c) * BZ
+                first = rl(planes[0, plane : plane + BZ, :], at - shift)
+                second = rl(planes[1, plane : plane + BZ, :], (at - E if h else E) - shift)
+                add = jnp.where(here, first, jnp.where(there, second, 0.0))
+                held[h, row : row + BZ, :] = (partial[h, row : row + BZ, :] + add) * scale
         for s in range(BZ):
             for h in range(2):
                 boxes[c, s, :, h * L : h * L + L] = held[h, pl.ds(c * E * BZ + s, E, stride=BZ), :]
@@ -663,7 +695,7 @@
     link_got = swap(link, link_pairs)
     moved, near, far = call(
         k(merge_kernel),
-        [(a, "vmem") for a in (odd_got, even_got, odd_rest_got, even_rest_got, stayed)],
+        [(a, "vmem") for a in (even_got, odd_got, even_rest_got, odd_rest_got, stayed)],
         [(big, "vmem"), ((FACE, L), "vmem"), ((FACE, L), "vmem")],
     )
     near, far = call(
@@ -678,29 +710,33 @@
         [(a, "vmem") for a in (moved, rates, link_got, core_got, core, link)],
         [(big, "vmem"), ((3 * PLANE, L), "vmem"), ((3 * PLANE, L), "vmem"), ((PLANE, L), "vmem")],
     )
-    x_link, y_far, kept, sent = call(
+    (second,) = call(
+        k(second_kernel),
+        [(a, "vmem") for a in (moved, rates, part, core_first, link_first)],
+        [(big, "vmem")],
+    )
+    y_far, kept, sent = call(
         k(flux_kernel),
-        [(a, "vmem") for a in (part, rates, masks, tops, link_first, near_got, far_got, far)],
-        [plane] * 4,
+        [(a, "vmem") for a in (part, rates, masks, tops, link_first, far_got, near_got, far, second)],
+        [plane] * 3,
     )
     got = swap(sent, even_pairs)
 
-    def smooth(comps, before, aliases):
-        ins = (moved, rates, part, core_first, near_got, far_got, near, x_link, y_far)
-        return call(
-            functools.partial(smooth_kernel, comps, shape),
-            [(a, "vmem") for a in ins] + [before],
-            [((1, 1, BZ, NC, E, 2 * L), "hbm"), ((BZ, L), "vmem")],
-            [VM(big, F32), VM(big, F32), VM((NC, BZ, E, 2 * L), F32), pltpu.SemaphoreType.DMA((NC,))],
-            aliases,
-        )
-
-    smoothed, done = smooth((0, 1, 2), (masks, "vmem"), None)
+    smoothed, done = call(
+        k(smooth_kernel),
+        [(a, "vmem") for a in (rates, second, core_first, link_first, far_got, near_got, near, y_far)],
+        [((1, 1, BZ, NC, E, 2 * L), "hbm"), ((BZ, L), "vmem")],
+        [
+            VM((2, 4 * PLANE, L), F32),
+            VM(big, F32),
+            VM((NC, BZ, E, 2 * L), F32),
+            pltpu.SemaphoreType.DMA((NC,)),
+        ],
+    )
     mine, sent = call(k(half_kernel), [(kept, "vmem"), (got, "vmem"), (done, "vmem")], [plane, plane])
     got = swap(sent, core_pairs)
-    smoothed, done = smooth((3, 4), (smoothed, "hbm"), {9: 0})
     (registers,) = call(
-        k(register_kernel), [(mine, "vmem"), (got, "vmem"), (done, "vmem")], [((1, 1, NC, 6, 2 * L), "out")]
+        k(register_kernel), [(mine, "vmem"), (got, "vmem")], [((1, 1, NC, 6, 2 * L), "out")]
     )
     return smoothed, registers
 

time: 31.1 us -> 30.2 us (0.971)
  starting transfers between devices: 13 us -> 11.9 us
  waiting for transfers between devices: 9.03 us -> 10 us
  Pallas kernels: 7.49 us -> 6.71 us
    ppermute x10, starting transfers between devices: 13 us -> 11.9 us  [swap(): return lax.ppermute(array, both, pairs)]
    ppermute x10, waiting for transfers between devices: 9.03 us -> 10 us  [swap(): return lax.ppermute(array, both, pairs)]
    pallas_call x11, Pallas kernels: 7.49 us -> 6.71 us  [call(): pl.pallas_call(kernel, out_shape=shapes, in_specs=in_specs, out_specs=out...]
  transfers between devices with their start and end apart: 10 -> 10, of which waited for: 6 -> 6; matrix products, arithmetic and copies ran while one was open for 0% -> 0% of each run, Pallas kernels for 17% -> 15%
where the time goes in v4:
time: 30.2 us; the launch traced here: 30 us
  starting transfers between devices  11.9 us (39%)
  waiting for transfers between devices  10 us (33%)
  Pallas kernels  6.71 us (22%)
  between operations  0.75 us (2%)
  local copies, waits for them, and re-layouts  0.64 us (2%)
    ppermute x10, starting transfers between devices, swap(): return lax.ppermute(array, both, pairs)  11.9 us
    ppermute x10, waiting for transfers between devices, swap(): return lax.ppermute(array, both, pairs)  10 us
    pallas_call x11, Pallas kernels, call(): pl.pallas_call(kernel, out_shape=shapes, in_specs=in_specs, out_specs=out...  6.71 us
    unnamed x1, local copies, waits for them, and re-layouts  0.64 us
  transfers between devices with their start and end apart: 10, of which 6 were waited for; matrix products, arithmetic and copies ran while one was open for 0% of the time, Pallas kernels for 15%

profile of v4, /device:TPU:0, one launch (start us, length us, event | category | flops | bytes accessed | tf_op | source)
XLA Modules:
  0.0 30.0 jit_solution(4325625548274739909)
XLA Ops:
  0.6 1.2 %shard_map.59 = (f32[48,256]{1,0:T(8,128)S(1)}, f32[48,256]{1,0:T(8,128)S(1)}, f32[120,256]{1,0:T(8,128)S(1)}, f32[120,256]{1,0:T(8,128)S(1)}, f32[8,5,16,256]{3...) custom-call(s32[1,1,8]{2,1,0:T(1,128)} %place_hbm.1, ...), custom_call_target="tpu_custom_call" | custom-call | flops 1000 | tf_op jit(solution)/shard_map/pallas_call | solution.py:48
  1.8 3.0 %collective-permute-start = (f32[48,256]{1,0:T(8,128)S(1)}, f32[48,256]{1,0:T(8,128)S(1)}, u32[]{:S(2)}, u32[]{:S(2)}) collective-permute-start(f32[48,256]{1,0:T(8,128)S(1)} %get-tuple-element.31), channel_id=1, source_target_pairs={{0,1},{1,0},{2,3},{3,2},{4,5},{5,4},{6,7},{7,6},{8,9},{9,8},{10,11... | collective-permute-start | bytes 147464 | tf_op jit(solution)/shard_map/ppermute | solution.py:640
  4.9 3.6 %collective-permute-start.1 = (f32[48,256]{1,0:T(8,128)S(1)}, f32[48,256]{1,0:T(8,128)S(1)}, u32[]{:S(2)}, u32[]{:S(2)}) collective-permute-start(f32[48,256]{1,0:T(8,128)S(1)} %get-tuple-element.32), channel_id=1, source_target_pairs={{0,31},{1,2},{2,1},{3,4},{4,3},{5,6},{6,5},{7,8},{8,7},{9,10},{10,... | collective-permute-start | bytes 147464 | tf_op jit(solution)/shard_map/ppermute | solution.py:640
  8.5 1.7 %collective-permute-start.3 = (f32[120,256]{1,0:T(8,128)S(1)}, f32[120,256]{1,0:T(8,128)S(1)}, u32[]{:S(2)}, u32[]{:S(2)}) collective-permute-start(f32[120,256]{1,0:T(8,128)S(1)} %get-tuple-element.40), channel_id=1, source_target_pairs={{0,31},{1,2},{2,1},{3,4},{4,3},{5,6},{6,5},{7,8},{8,7},{9,10},{10,... | collective-permute-start | bytes 368648 | tf_op jit(solution)/shard_map/ppermute | solution.py:640
  10.2 0.3 shard_map.60
  10.5 1.9 %collective-permute-done.1.odd = f32[48,256]{1,0:T(8,128)S(1)} collective-permute-done((f32[48,256]{1,0:T(8,128)S(1)}, f32[48,256]{1,0:T(8,128)S(1)}, u32[]{:S(2)}, u32[]{:S(2)}) %collective-permute-start.1) | collective-permute-done | bytes 49184 | tf_op jit(solution)/shard_map/ppermute | solution.py:640
  12.4 0.1 shard_map.61
  12.5 0.1 collective-permute-start.4
  12.6 1.3 %collective-permute-start.5 = (f32[168,128]{1,0:T(8,128)S(1)}, f32[168,128]{1,0:T(8,128)S(1)}, u32[]{:S(2)}, u32[]{:S(2)}) collective-permute-start(f32[168,128]{1,0:T(8,128)S(1)} %get-tuple-element.43.core_sent), channel_id=1, source_target_pairs={{0,8},{1,9},{2,10},{3,11},{4,12},{5,13},{6,14},{7,15},{8,0},{9,1},... | collective-permute-start | bytes 258056 | tf_op jit(solution)/shard_map/ppermute | solution.py:640
  13.9 0.4 %collective-permute-done.2.even_rest = f32[120,256]{1,0:T(8,128)S(1)} collective-permute-done((f32[120,256]{1,0:T(8,128)S(1)}, f32[120,256]{1,0:T(8,128)S(1)}, u32[]{:S(2)}, u32[]{:S(2)}) %collective-permute-start.2) | collective-permute-done | bytes 122912 | tf_op jit(solution)/shard_map/ppermute | solution.py:640
  14.3 3.2 %collective-permute-done.3.odd_rest = f32[120,256]{1,0:T(8,128)S(1)} collective-permute-done((f32[120,256]{1,0:T(8,128)S(1)}, f32[120,256]{1,0:T(8,128)S(1)}, u32[]{:S(2)}, u32[]{:S(2)}) %collective-permute-start.3) | collective-permute-done | bytes 122912 | tf_op jit(solution)/shard_map/ppermute | solution.py:640
  17.5 0.4 %shard_map.62 = (f32[2,640,128]{2,1,0:T(8,128)S(1)}, f32[160,128]{1,0:T(8,128)S(1)}, f32[160,128]{1,0:T(8,128)S(1)}) custom-call(f32[48,256]{1,0:T(8,128)S(1)} %collective-permute-done.even, f32[48,256]{1,0:T(8,128)S(1)} %collective-permute-done.1.odd, f32[120,256]{1,0:T(8,128)S(1)} %collective-permute-done.2.even_rest, ...), custom_call_target="tpu_custom_call" | custom-call | flops 1000 | tf_op jit(solution)/shard_map/pallas_call | solution.py:48
  17.9 0.1 shard_map.65
  18.1 0.5 %collective-permute-start.7 = (f32[176,128]{1,0:T(8,128)S(1)}, f32[176,128]{1,0:T(8,128)S(1)}, u32[]{:S(2)}, u32[]{:S(2)}) collective-permute-start(f32[176,128]{1,0:T(8,128)S(1)} %get-tuple-element.50.near_sent), channel_id=1, source_target_pairs={{0,1},{1,0},{2,3},{3,2},{4,5},{5,4},{6,7},{7,6},{8,9},{9,8},{10,11... | collective-permute-start | bytes 270344 | tf_op jit(solution)/shard_map/ppermute | solution.py:640
  18.6 1.4 %shard_map.63 = (f32[2,640,128]{2,1,0:T(8,128)S(1)}, f32[120,128]{1,0:T(8,128)S(1)}, f32[120,128]{1,0:T(8,128)S(1)}, f32[40,128]{1,0:T(8,128)S(1)}) custom-call(f32[2,640,128]{2,1,0:T(8,128)S(1)} %get-tuple-element.41.moved, f32[40,128]{1,0:T(8,128)S(1)} %get-tuple-element.38.rates.moved_rates, f32[168,128]{1,0:T(8,128)S(1)} %collective-permute-done.4.link, ...), custom_call_target="tpu_custom_call" | custom-call | flops 1000 | tf_op jit(solution)/shard_map/pallas_call | solution.py:48
  20.0 0.9 %shard_map.64._.partial = f32[2,640,128]{2,1,0:T(8,128)S(1)} custom-call(f32[2,640,128]{2,1,0:T(8,128)S(1)} %get-tuple-element.41.moved, f32[40,128]{1,0:T(8,128)S(1)} %get-tuple-element.38.rates.moved_rates, f32[2,640,128]{2,1,0:T(8,128)S(1)} %get-tuple-element.44.partial, f32[120,128]{1,0:T(8,128)S(1)} %get-tuple-element.45.core_first, ...), custom_call_target="tpu_custom_call" | custom-call | flops 1000 | tf_op jit(solution)/shard_map/pallas_call | solution.py:48
  20.9 2.2 %collective-permute-done.7.near = f32[176,128]{1,0:T(8,128)S(1)} collective-permute-done((f32[176,128]{1,0:T(8,128)S(1)}, f32[176,128]{1,0:T(8,128)S(1)}, u32[]{:S(2)}, u32[]{:S(2)}) %collective-permute-start.7) | collective-permute-done | bytes 90144 | tf_op jit(solution)/shard_map/ppermute | solution.py:640
  23.1 0.8 %shard_map.66 = (f32[80,128]{1,0:T(8,128)S(1)}, f32[80,128]{1,0:T(8,128)S(1)}, f32[80,128]{1,0:T(8,128)S(1)}) custom-call(f32[2,640,128]{2,1,0:T(8,128)S(1)} %get-tuple-element.44.partial, f32[40,128]{1,0:T(8,128)S(1)} %get-tuple-element.38.rates.moved_rates, f32[24,128]{1,0:T(8,128)S(1)} %get-tuple-element.51.masks, f32[40,128]{1,0:T(8,128)S(1)} %get-tuple-element.52.tops, ...), custom_call_target="tpu_custom_call" | custom-call | flops 1000 | tf_op jit(solution)/shard_map/pallas_call | solution.py:48
  24.0 1.5 %collective-permute-start.8 = (f32[80,128]{1,0:T(8,128)S(1)}, f32[80,128]{1,0:T(8,128)S(1)}, u32[]{:S(2)}, u32[]{:S(2)}) collective-permute-start(f32[80,128]{1,0:T(8,128)S(1)} %get-tuple-element.56), channel_id=1, source_target_pairs={{0,1},{1,0},{2,3},{3,2},{4,5},{5,4},{6,7},{7,6},{8,9},{9,8},{10,11... | collective-permute-start | bytes 122888 | tf_op jit(solution)/shard_map/ppermute | solution.py:640
  25.5 1.4 %shard_map.67 = (f32[1,1,8,5,16,256]{5,4,3,2,1,0:T(8,128)}, f32[8,128]{1,0:T(8,128)S(1)}) custom-call(f32[40,128]{1,0:T(8,128)S(1)} %get-tuple-element.38.rates.moved_rates, f32[2,640,128]{2,1,0:T(8,128)S(1)} %shard_map.64._.partial, f32[120,128]{1,0:T(8,128)S(1)} %get-tuple-element.45.core_first, f32[120,128]{1,0:T(8,128)S(1)} %get-tuple-element.46.link_first, ...), custom_call_target="tpu_custom_call" | custom-call | flops 1000 | tf_op jit(solution)/shard_map/pallas_call | solution.py:48
  26.9 1.1 %collective-permute-done.8.got = f32[80,128]{1,0:T(8,128)S(1)} collective-permute-done((f32[80,128]{1,0:T(8,128)S(1)}, f32[80,128]{1,0:T(8,128)S(1)}, u32[]{:S(2)}, u32[]{:S(2)}) %collective-permute-start.8) | collective-permute-done | bytes 40992 | tf_op jit(solution)/shard_map/ppermute | solution.py:640
  28.1 0.1 collective-permute-start.9
  28.1 1.2 %collective-permute-done.9.got = f32[80,128]{1,0:T(8,128)S(1)} collective-permute-done((f32[80,128]{1,0:T(8,128)S(1)}, f32[80,128]{1,0:T(8,128)S(1)}, u32[]{:S(2)}, u32[]{:S(2)}) %collective-permute-start.9) | collective-permute-done | bytes 40992 | tf_op jit(solution)/shard_map/ppermute | solution.py:640
  29.4 0.6 %copy.6 = f32[1,1,5,6,256]{4,1,3,2,0:T(1,128)} copy(f32[1,1,5,6,256]{4,3,2,1,0:T(8,128)S(1)} %shard_map.69) | data formatting | bytes 61440
  (8 shorter events, 0.1 us)
Async XLA Ops:
  1.8 8.7 %collective-permute-start = (f32[48,256]{1,0:T(8,128)S(1)}, f32[48,256]{1,0:T(8,128)S(1)}, u32[]{:S(2)}, u32[]{:S(2)}) collective-permute-start(f32[48,256]{1,0:T(8,128)S(1)} %get-tuple-element.31), channel_id=1, source_target_pairs={{0,1},{1,0},{2,3},{3,2},{4,5},{5,4},{6,7},{7,6},{8,9},{9,8},{10,11... | collective-permute-start | bytes 147464 | tf_op jit(solution)/shard_map/ppermute | solution.py:640
  4.9 7.5 %collective-permute-start.1 = (f32[48,256]{1,0:T(8,128)S(1)}, f32[48,256]{1,0:T(8,128)S(1)}, u32[]{:S(2)}, u32[]{:S(2)}) collective-permute-start(f32[48,256]{1,0:T(8,128)S(1)} %get-tuple-element.32), channel_id=1, source_target_pairs={{0,31},{1,2},{2,1},{3,4},{4,3},{5,6},{6,5},{7,8},{8,7},{9,10},{10,... | collective-permute-start | bytes 147464 | tf_op jit(solution)/shard_map/ppermute | solution.py:640
  8.5 5.8 %collective-permute-start.2 = (f32[120,256]{1,0:T(8,128)S(1)}, f32[120,256]{1,0:T(8,128)S(1)}, u32[]{:S(2)}, u32[]{:S(2)}) collective-permute-start(f32[120,256]{1,0:T(8,128)S(1)} %get-tuple-element.39), channel_id=1, source_target_pairs={{0,1},{1,0},{2,3},{3,2},{4,5},{5,4},{6,7},{7,6},{8,9},{9,8},{10,11... | collective-permute-start | bytes 368648 | tf_op jit(solution)/shard_map/ppermute | solution.py:640
  8.5 9.0 %collective-permute-start.3 = (f32[120,256]{1,0:T(8,128)S(1)}, f32[120,256]{1,0:T(8,128)S(1)}, u32[]{:S(2)}, u32[]{:S(2)}) collective-permute-start(f32[120,256]{1,0:T(8,128)S(1)} %get-tuple-element.40), channel_id=1, source_target_pairs={{0,31},{1,2},{2,1},{3,4},{4,3},{5,6},{6,5},{7,8},{8,7},{9,10},{10,... | collective-permute-start | bytes 368648 | tf_op jit(solution)/shard_map/ppermute | solution.py:640
  12.5 5.4 %collective-permute-start.4 = (f32[168,128]{1,0:T(8,128)S(1)}, f32[168,128]{1,0:T(8,128)S(1)}, u32[]{:S(2)}, u32[]{:S(2)}) collective-permute-start(f32[168,128]{1,0:T(8,128)S(1)} %get-tuple-element.42.link_sent), channel_id=1, source_target_pairs={{0,24},{1,25},{2,26},{3,27},{4,28},{5,29},{6,30},{7,31},{8,16},{9,... | collective-permute-start | bytes 258056 | tf_op jit(solution)/shard_map/ppermute | solution.py:640
  12.6 5.3 %collective-permute-start.5 = (f32[168,128]{1,0:T(8,128)S(1)}, f32[168,128]{1,0:T(8,128)S(1)}, u32[]{:S(2)}, u32[]{:S(2)}) collective-permute-start(f32[168,128]{1,0:T(8,128)S(1)} %get-tuple-element.43.core_sent), channel_id=1, source_target_pairs={{0,8},{1,9},{2,10},{3,11},{4,12},{5,13},{6,14},{7,15},{8,0},{9,1},... | collective-permute-start | bytes 258056 | tf_op jit(solution)/shard_map/ppermute | solution.py:640
  18.0 2.9 %collective-permute-start.6 = (f32[176,128]{1,0:T(8,128)S(1)}, f32[176,128]{1,0:T(8,128)S(1)}, u32[]{:S(2)}, u32[]{:S(2)}) collective-permute-start(f32[176,128]{1,0:T(8,128)S(1)} %get-tuple-element.49.far_sent), channel_id=1, source_target_pairs={{0,8},{1,2},{2,1},{3,4},{4,3},{5,6},{6,5},{7,15},{8,0},{9,10},{10,... | collective-permute-start | bytes 270344 | tf_op jit(solution)/shard_map/ppermute | solution.py:640
  18.1 5.0 %collective-permute-start.7 = (f32[176,128]{1,0:T(8,128)S(1)}, f32[176,128]{1,0:T(8,128)S(1)}, u32[]{:S(2)}, u32[]{:S(2)}) collective-permute-start(f32[176,128]{1,0:T(8,128)S(1)} %get-tuple-element.50.near_sent), channel_id=1, source_target_pairs={{0,1},{1,0},{2,3},{3,2},{4,5},{5,4},{6,7},{7,6},{8,9},{9,8},{10,11... | collective-permute-start | bytes 270344 | tf_op jit(solution)/shard_map/ppermute | solution.py:640
  24.0 4.1 %collective-permute-start.8 = (f32[80,128]{1,0:T(8,128)S(1)}, f32[80,128]{1,0:T(8,128)S(1)}, u32[]{:S(2)}, u32[]{:S(2)}) collective-permute-start(f32[80,128]{1,0:T(8,128)S(1)} %get-tuple-element.56), channel_id=1, source_target_pairs={{0,1},{1,0},{2,3},{3,2},{4,5},{5,4},{6,7},{7,6},{8,9},{9,8},{10,11... | collective-permute-start | bytes 122888 | tf_op jit(solution)/shard_map/ppermute | solution.py:640
  28.1 1.3 %collective-permute-start.9 = (f32[80,128]{1,0:T(8,128)S(1)}, f32[80,128]{1,0:T(8,128)S(1)}, u32[]{:S(2)}, u32[]{:S(2)}) collective-permute-start(f32[80,128]{1,0:T(8,128)S(1)} %get-tuple-element.59), channel_id=1, source_target_pairs={{0,8},{1,9},{2,10},{3,11},{4,12},{5,13},{6,14},{7,15},{8,0},{9,1},... | collective-permute-start | bytes 122888 | tf_op jit(solution)/shard_map/ppermute | solution.py:640

commit v5 on v4

--- a/solution.py
+++ b/solution.py
@@ -148,21 +148,25 @@
                 rest[12 * box : 12 * box + 12, :] = boxes[sources[k], c, 2 : E - 2]
 
 
-def stay_kernel(shape, boxes, slots, old_rates, moved, rates):
+def stays(slots):
     label = (subs() + 1).astype(F32)
-    found = [slots[s : s + 1, :] == label for s in range(BZ)]
-    for c in range(NC):
-        tile = jnp.zeros((BZ, L), F32)
-        for s in range(BZ):
-            tile = jnp.where(found[s], old_rates[s * NC + c : s * NC + c + 1, :], tile)
-        rates[c * BZ : c * BZ + BZ, :] = tile
+    return [slots[s : s + 1, :] == label for s in range(BZ)]
+
+
+def stayed_tile(found, boxes, c, x, h):
+    tile = jnp.zeros((BZ, L), F32)
+    for s in range(BZ):
+        tile = jnp.where(found[s], boxes[s, c, x : x + 1, h * L : h * L + L], tile)
+    return tile
+
+
+def stay_kernel(shape, boxes, slots, moved):
+    found = stays(slots)
+    for c in range(NC):
         for x in range(E):
             row = (c * E + x) * BZ
             for h in range(2):
-                tile = jnp.zeros((BZ, L), F32)
-                for s in range(BZ):
-                    tile = jnp.where(found[s], boxes[s, c, x : x + 1, h * L : h * L + L], tile)
-                moved[h, row : row + BZ, :] = tile
+                moved[h, row : row + BZ, :] = stayed_tile(found, boxes, c, x, h)
 
 
 def arrivals(even, odd):
@@ -175,9 +179,7 @@
     return found
 
 
-def merged(found, moved, c, x, h, rests=None):
-    row = (c * E + x) * BZ
-    tile = moved[h, row : row + BZ, :]
+def merged(found, tile, c, x, h, rests=None):
     for i, (parcel, k, hit) in enumerate(found):
         if x in EDGES:
             source, at = parcel, (k * NC + c) * 4 + EDGES.index(x)
@@ -195,26 +197,27 @@
     return ((layer * 2 + h) * NC + c) * BZ
 
 
-def xsend_kernel(shape, even, odd, moved, rates, core, link, all_rates):
+def xsend_kernel(shape, even, odd, boxes, slots, old_rates, core, link, rates):
     gx, _, _ = place_of(shape)
     first = gx % 2 == 0
-    found = arrivals(even, odd)
+    kept, found = stays(slots), arrivals(even, odd)
     lane = lanes()
     together = jnp.zeros((BZ, L), F32)
     for c in range(NC):
-        tile = rates[c * BZ : c * BZ + BZ, :]
+        tile = jnp.zeros((BZ, L), F32)
+        for s in range(BZ):
+            tile = jnp.where(kept[s], old_rates[s * NC + c : s * NC + c + 1, :], tile)
         for parcel, k, hit in found:
             line = jnp.broadcast_to(parcel[AHEAD + k : AHEAD + k + 1, :L], (BZ, L))
             tile = jnp.where(hit, spread(line, c), tile)
-        all_rates[c * BZ : c * BZ + BZ, :] = tile
-        together = jnp.where(lane % L == c, tile, together)
+        rates[c * BZ : c * BZ + BZ, :] = tile
+        together = jnp.where(lane == c, tile, together)
         for layer in range(2):
             for h in range(2):
-                low = merged(found, moved, c, layer, h)
-                high = merged(found, moved, c, E - 1 - layer, h)
+                sides = [merged(found, stayed_tile(kept, boxes, c, x, h), c, x, h) for x in (layer, E - 1 - layer)]
                 at = plane_row(layer, h, c)
-                core[at : at + BZ, :] = jnp.where(first, high, low)
-                link[at : at + BZ, :] = jnp.where(first, low, high)
+                core[at : at + BZ, :] = jnp.where(first, sides[1], sides[0])
+                link[at : at + BZ, :] = jnp.where(first, sides[0], sides[1])
     core[FACE:, :] = together
     link[FACE:, :] = together
 
@@ -233,7 +236,7 @@
             here = lane // E == x % 8
             half = x // 8
             for h in range(2):
-                tile = merged(found, moved, c, x, h, (even_rest, odd_rest))
+                tile = merged(found, moved[h, row : row + BZ, :], c, x, h, (even_rest, odd_rest))
                 out[h, row : row + BZ, :] = tile
                 for layer in range(2):
                     keep, start = ((low, E * layer) if h == 0 else (high, L - E - E * layer))
@@ -442,7 +445,7 @@
 
 
 def flux_kernel(
-    shape, partial, moved_rates, masks, tops, link_first, far, near, far_sent, _, y_far, kept, sent
+    shape, partial, moved_rates, masks, tops, link_first, far, near, far_sent, own_far, y_far, kept, sent
 ):
     x_first, y_first, link_ok, far_ok = ends(shape)
     gx, gy, _ = place_of(shape)
@@ -475,11 +478,8 @@
 
     faces_y = []
     for c in each:
-        own, own1 = pair_at(far_sent, 0, c), pair_at(far_sent, 1, c)
-        sums, line = inner(own, lane, sub, swap), corner(extra_at(far_sent, c), low_lane, high_lane)
-        flux = [
-            far_f[c][h] - (own[h] + rate[c] * (sums[h] + line[h] + own1[h] + far_r[c][h])) * scale[c] for h in range(2)
-        ]
+        own = pair_at(own_far, 0, c)
+        flux = [far_f[c][h] - own[h] - weight[c] * far_r[c][h] for h in range(2)]
         face = coarse_plane(flux, par_x, lane, sub) * (rate[c] * masks[BZ : 2 * BZ, :])
         faces_y.append(face + rs(face, 1))
     faces_x = []
@@ -514,22 +514,18 @@
         faces_z.append((tops[c * BZ : c * BZ + BZ, :] + add) * (0.25 * rate[c] * masks[2 * BZ :, :]))
     left = sub % 4 < 2
     for c in each:
-        for h in range(2):
-            outer = jnp.where(
-                upper, jnp.where(par_x == h, faces_y[c], 0.0), jnp.where(par_y == h, faces_x[c], 0.0)
-            )
-            top = jnp.where(par_x == h, faces_z[c], 0.0)
-            columns = (jnp.where(left, outer, rs(top, 2)), jnp.where(left, rs(outer, -2), top))
-            row = (h * NC + c) * BZ
-            kept[row : row + BZ, :] = jnp.where(y_first, columns[0], columns[1])
-            sent[row : row + BZ, :] = jnp.where(y_first, columns[1], columns[0])
+        outer = jnp.where(upper, faces_y[c], faces_x[c])
+        columns = (jnp.where(left, outer, rs(faces_z[c], 2)), jnp.where(left, rs(outer, -2), faces_z[c]))
+        row = c * BZ
+        kept[row : row + BZ, :] = jnp.where(y_first, columns[0], columns[1])
+        sent[row : row + BZ, :] = jnp.where(y_first, columns[1], columns[0])
 
 
 def half_kernel(shape, kept, got, _, mine, sent):
     gx, _, _ = place_of(shape)
     first = gx % 2 == 0
     top = subs() < 4
-    for i in range(2 * NC):
+    for i in range(NC):
         a, b = kept[i * BZ : i * BZ + BZ, :], got[i * BZ : i * BZ + BZ, :]
         rows = (jnp.where(top, a, rs(b, 4)), jnp.where(top, rs(a, 4), b))
         mine[i * BZ : i * BZ + BZ, :] = jnp.where(first, rows[0], rows[1])
@@ -539,26 +535,32 @@
 def register_kernel(shape, mine, got, out):
     x_first, y_first, _, _ = ends(shape)
     sub = subs()
-    for h in range(2):
-        for c in range(NC):
-            row = (h * NC + c) * BZ
-            m, g = mine[row : row + BZ, :], got[row : row + BZ, :]
-            a, b = m + rs(m, 4), g + rs(g, 4)
-            s = m + g
-            ab = a + b
+    for c in range(NC):
+        m, g = mine[c * BZ : c * BZ + BZ, :], got[c * BZ : c * BZ + BZ, :]
+        m4, g4 = rs(m, 4), rs(g, 4)
+        for h in range(2):
+            same_y, same_x = (y_first, x_first) if h == 0 else (~y_first, ~x_first)
+            a, b = jnp.where(same_y, m, m4), jnp.where(same_y, g, g4)
             x0, x1 = jnp.where(x_first, a, b), jnp.where(x_first, b, a)
-            y0, y1 = jnp.where(y_first, rs(s, 1), rs(s, 5)), jnp.where(y_first, rs(s, 5), rs(s, 1))
-            t = jnp.where(sub == 0, x0, jnp.where(sub == 1, rs(x1, 1), rs(ab, 2)))
-            t = jnp.where(sub == 2, y0, jnp.where(sub == 3, rs(y1, 1), t))
-            out[0, 0, c, :, h * L : h * L + L] = t[:6]
-
-
-def second_kernel(shape, moved, rates, partial, core_first, link_first, out):
+            t, t4 = jnp.where(same_x, m, g), jnp.where(same_x, m4, g4)
+            y0, y1 = jnp.where(y_first, rs(t, 1), rs(t, 5)), jnp.where(y_first, rs(t, 6), rs(t, 2))
+            rows = jnp.where(sub == 0, x0, jnp.where(sub == 1, rs(x1, 1), rs(t + t4, 2)))
+            rows = jnp.where(sub == 2, y0, jnp.where(sub == 3, y1, rows))
+            out[0, 0, c, :, h * L : h * L + L] = rows[:6]
+
+
+def second_kernel(shape, moved, rates, partial, core_first, link_first, far_sent, out, own_far):
     x_first, _, _, _ = ends(shape)
     lane, sub = lanes(), subs()
     swap = swap_index(lane)
     for c in range(NC):
         rate = rates[c * BZ : c * BZ + BZ, :]
+        scale = 1.0 / (1.0 + 6.0 * rate)
+        own, own1 = pair_at(far_sent, 0, c), pair_at(far_sent, 1, c)
+        sums, line = inner(own, lane, sub, swap), corner(extra_at(far_sent, c), lane < E, lane >= L - E)
+        for h in range(2):
+            row = (h * NC + c) * BZ
+            own_far[row : row + BZ, :] = (own[h] + rate * (sums[h] + line[h] + own1[h])) * scale
         core, link = pair_at(core_first, 0, c), pair_at(link_first, 0, c)
         low = [jnp.where(x_first, b, a) for a, b in zip(core, link)]
         high = [jnp.where(x_first, a, b) for a, b in zip(core, link)]
@@ -681,16 +683,12 @@
     odd_got = swap(odd, odd_pairs)
     even_rest_got = swap(even_rest, even_pairs)
     odd_rest_got = swap(odd_rest, odd_pairs)
-    stayed, rates = call(
-        k(stay_kernel),
-        [(a, "vmem") for a in (boxes, slots, rates)],
-        [(big, "vmem"), ((PLANE, L), "vmem")],
-    )
     core, link, rates = call(
         k(xsend_kernel),
-        [(a, "vmem") for a in (even_got, odd_got, stayed, rates)],
+        [(a, "vmem") for a in (even_got, odd_got, boxes, slots, rates)],
         [((XFACE, L), "vmem"), ((XFACE, L), "vmem"), ((PLANE, L), "vmem")],
     )
+    (stayed,) = call(k(stay_kernel), [(boxes, "vmem"), (slots, "vmem")], [(big, "vmem")])
     core_got = swap(core, core_pairs)
     link_got = swap(link, link_pairs)
     moved, near, far = call(
@@ -710,15 +708,15 @@
         [(a, "vmem") for a in (moved, rates, link_got, core_got, core, link)],
         [(big, "vmem"), ((3 * PLANE, L), "vmem"), ((3 * PLANE, L), "vmem"), ((PLANE, L), "vmem")],
     )
-    (second,) = call(
+    second, own_far = call(
         k(second_kernel),
-        [(a, "vmem") for a in (moved, rates, part, core_first, link_first)],
-        [(big, "vmem")],
+        [(a, "vmem") for a in (moved, rates, part, core_first, link_first, far)],
+        [(big, "vmem"), plane],
     )
     y_far, kept, sent = call(
         k(flux_kernel),
-        [(a, "vmem") for a in (part, rates, masks, tops, link_first, far_got, near_got, far, second)],
-        [plane] * 3,
+        [(a, "vmem") for a in (part, rates, masks, tops, link_first, far_got, near_got, far, own_far)],
+        [plane, ((PLANE, L), "vmem"), ((PLANE, L), "vmem")],
     )
     got = swap(sent, even_pairs)
 
@@ -733,7 +731,7 @@
             pltpu.SemaphoreType.DMA((NC,)),
         ],
     )
-    mine, sent = call(k(half_kernel), [(kept, "vmem"), (got, "vmem"), (done, "vmem")], [plane, plane])
+    mine, sent = call(k(half_kernel), [(a, "vmem") for a in (kept, got, done)], [((PLANE, L), "vmem")] * 2)
     got = swap(sent, core_pairs)
     (registers,) = call(
         k(register_kernel), [(mine, "vmem"), (got, "vmem")], [((1, 1, NC, 6, 2 * L), "out")]

time: 30.2 us -> 29.6 us (0.980)
  starting transfers between devices: 11.9 us -> 11.4 us
    ppermute x10, starting transfers between devices: 11.9 us -> 11.4 us  [swap(): return lax.ppermute(array, both, pairs)]
  transfers between devices with their start and end apart: 10 -> 10, of which waited for: 6 -> 6; matrix products, arithmetic and copies ran while one was open for 0% -> 0% of each run, Pallas kernels for 15% -> 16%
where the time goes in v5:
time: 29.6 us; the launch traced here: 29.4 us
  starting transfers between devices  11.4 us (39%)
  waiting for transfers between devices  10.1 us (34%)
  Pallas kernels  6.57 us (22%)
  between operations  0.74 us (2%)
  local copies, waits for them, and re-layouts  0.64 us (2%)
    ppermute x10, starting transfers between devices, swap(): return lax.ppermute(array, both, pairs)  11.4 us
    ppermute x10, waiting for transfers between devices, swap(): return lax.ppermute(array, both, pairs)  10.1 us
    pallas_call x11, Pallas kernels, call(): pl.pallas_call(kernel, out_shape=shapes, in_specs=in_specs, out_specs=out...  6.57 us
    unnamed x1, local copies, waits for them, and re-layouts  0.64 us
  transfers between devices with their start and end apart: 10, of which 6 were waited for; matrix products, arithmetic and copies ran while one was open for 0% of the time, Pallas kernels for 16%

profile of v5, /device:TPU:0, one launch (start us, length us, event | category | flops | bytes accessed | tf_op | source)
XLA Modules:
  0.0 29.4 jit_solution(9933297750531757427)
XLA Ops:
  0.6 1.2 %shard_map.59 = (f32[48,256]{1,0:T(8,128)S(1)}, f32[48,256]{1,0:T(8,128)S(1)}, f32[120,256]{1,0:T(8,128)S(1)}, f32[120,256]{1,0:T(8,128)S(1)}, f32[8,5,16,256]{3...) custom-call(s32[1,1,8]{2,1,0:T(1,128)} %place_hbm.1, ...), custom_call_target="tpu_custom_call" | custom-call | flops 1000 | tf_op jit(solution)/shard_map/pallas_call | solution.py:48
  1.8 3.0 %collective-permute-start = (f32[48,256]{1,0:T(8,128)S(1)}, f32[48,256]{1,0:T(8,128)S(1)}, u32[]{:S(2)}, u32[]{:S(2)}) collective-permute-start(f32[48,256]{1,0:T(8,128)S(1)} %get-tuple-element.31), channel_id=1, source_target_pairs={{0,1},{1,0},{2,3},{3,2},{4,5},{5,4},{6,7},{7,6},{8,9},{9,8},{10,11... | collective-permute-start | bytes 147464 | tf_op jit(solution)/shard_map/ppermute | solution.py:642
  4.9 3.6 %collective-permute-start.1 = (f32[48,256]{1,0:T(8,128)S(1)}, f32[48,256]{1,0:T(8,128)S(1)}, u32[]{:S(2)}, u32[]{:S(2)}) collective-permute-start(f32[48,256]{1,0:T(8,128)S(1)} %get-tuple-element.32), channel_id=1, source_target_pairs={{0,31},{1,2},{2,1},{3,4},{4,3},{5,6},{6,5},{7,8},{8,7},{9,10},{10,... | collective-permute-start | bytes 147464 | tf_op jit(solution)/shard_map/ppermute | solution.py:642
  8.5 1.7 %collective-permute-start.3 = (f32[120,256]{1,0:T(8,128)S(1)}, f32[120,256]{1,0:T(8,128)S(1)}, u32[]{:S(2)}, u32[]{:S(2)}) collective-permute-start(f32[120,256]{1,0:T(8,128)S(1)} %get-tuple-element.38), channel_id=1, source_target_pairs={{0,31},{1,2},{2,1},{3,4},{4,3},{5,6},{6,5},{7,8},{8,7},{9,10},{10,... | collective-permute-start | bytes 368648 | tf_op jit(solution)/shard_map/ppermute | solution.py:642
  10.2 2.2 %collective-permute-done.1.odd = f32[48,256]{1,0:T(8,128)S(1)} collective-permute-done((f32[48,256]{1,0:T(8,128)S(1)}, f32[48,256]{1,0:T(8,128)S(1)}, u32[]{:S(2)}, u32[]{:S(2)}) %collective-permute-start.1) | collective-permute-done | bytes 49184 | tf_op jit(solution)/shard_map/ppermute | solution.py:642
  12.4 0.1 shard_map.60
  12.5 0.1 collective-permute-start.4
  12.6 1.3 %collective-permute-start.5 = (f32[168,128]{1,0:T(8,128)S(1)}, f32[168,128]{1,0:T(8,128)S(1)}, u32[]{:S(2)}, u32[]{:S(2)}) collective-permute-start(f32[168,128]{1,0:T(8,128)S(1)} %get-tuple-element.41.core_sent), channel_id=1, source_target_pairs={{0,8},{1,9},{2,10},{3,11},{4,12},{5,13},{6,14},{7,15},{8,0},{9,1},... | collective-permute-start | bytes 258056 | tf_op jit(solution)/shard_map/ppermute | solution.py:642
  13.9 0.3 shard_map.61.moved
  14.2 0.1 collective-permute-done.2.even_rest
  14.3 3.2 %collective-permute-done.3.odd_rest = f32[120,256]{1,0:T(8,128)S(1)} collective-permute-done((f32[120,256]{1,0:T(8,128)S(1)}, f32[120,256]{1,0:T(8,128)S(1)}, u32[]{:S(2)}, u32[]{:S(2)}) %collective-permute-start.3) | collective-permute-done | bytes 122912 | tf_op jit(solution)/shard_map/ppermute | solution.py:642
  17.5 0.4 %shard_map.62 = (f32[2,640,128]{2,1,0:T(8,128)S(1)}, f32[160,128]{1,0:T(8,128)S(1)}, f32[160,128]{1,0:T(8,128)S(1)}) custom-call(f32[48,256]{1,0:T(8,128)S(1)} %collective-permute-done.even, f32[48,256]{1,0:T(8,128)S(1)} %collective-permute-done.1.odd, f32[120,256]{1,0:T(8,128)S(1)} %collective-permute-done.2.even_rest, ...), custom_call_target="tpu_custom_call" | custom-call | flops 1000 | tf_op jit(solution)/shard_map/pallas_call | solution.py:48
  17.9 0.1 shard_map.64
  18.1 0.2 collective-permute-start.7
  18.3 1.4 %shard_map.63 = (f32[2,640,128]{2,1,0:T(8,128)S(1)}, f32[120,128]{1,0:T(8,128)S(1)}, f32[120,128]{1,0:T(8,128)S(1)}, f32[40,128]{1,0:T(8,128)S(1)}) custom-call(f32[2,640,128]{2,1,0:T(8,128)S(1)} %get-tuple-element.39.moved, f32[40,128]{1,0:T(8,128)S(1)} %get-tuple-element.36.rates.moved_rates, f32[168,128]{1,0:T(8,128)S(1)} %collective-permute-done.4.link, ...), custom_call_target="tpu_custom_call" | custom-call | flops 1000 | tf_op jit(solution)/shard_map/pallas_call | solution.py:48
  19.7 1.1 %shard_map.65 = (f32[2,640,128]{2,1,0:T(8,128)S(1)}, f32[80,128]{1,0:T(8,128)S(1)}) custom-call(f32[2,640,128]{2,1,0:T(8,128)S(1)} %get-tuple-element.39.moved, f32[40,128]{1,0:T(8,128)S(1)} %get-tuple-element.36.rates.moved_rates, f32[2,640,128]{2,1,0:T(8,128)S(1)} %get-tuple-element.42.partial, f32[120,128]{1,0:T(8,128)S(1)} %get-tuple-element.43.core_first, ...), custom_call_target="tpu_custom_call" | custom-call | flops 1000 | tf_op jit(solution)/shard_map/pallas_call | solution.py:48
  20.8 2.3 %collective-permute-done.7.near = f32[176,128]{1,0:T(8,128)S(1)} collective-permute-done((f32[176,128]{1,0:T(8,128)S(1)}, f32[176,128]{1,0:T(8,128)S(1)}, u32[]{:S(2)}, u32[]{:S(2)}) %collective-permute-start.7) | collective-permute-done | bytes 90144 | tf_op jit(solution)/shard_map/ppermute | solution.py:642
  23.2 0.5 %shard_map.66 = (f32[80,128]{1,0:T(8,128)S(1)}, f32[40,128]{1,0:T(8,128)S(1)}, f32[40,128]{1,0:T(8,128)S(1)}) custom-call(f32[2,640,128]{2,1,0:T(8,128)S(1)} %get-tuple-element.42.partial, f32[40,128]{1,0:T(8,128)S(1)} %get-tuple-element.36.rates.moved_rates, f32[24,128]{1,0:T(8,128)S(1)} %get-tuple-element.50.masks, f32[40,128]{1,0:T(8,128)S(1)} %get-tuple-element.51.tops, ...), custom_call_target="tpu_custom_call" | custom-call | flops 1000 | tf_op jit(solution)/shard_map/pallas_call | solution.py:48
  23.6 1.3 %collective-permute-start.8 = (f32[40,128]{1,0:T(8,128)S(1)}, f32[40,128]{1,0:T(8,128)S(1)}, u32[]{:S(2)}, u32[]{:S(2)}) collective-permute-start(f32[40,128]{1,0:T(8,128)S(1)} %get-tuple-element.56), channel_id=1, source_target_pairs={{0,1},{1,0},{2,3},{3,2},{4,5},{5,4},{6,7},{7,6},{8,9},{9,8},{10,11... | collective-permute-start | bytes 61448 | tf_op jit(solution)/shard_map/ppermute | solution.py:642
  24.9 1.4 %shard_map.67 = (f32[1,1,8,5,16,256]{5,4,3,2,1,0:T(8,128)}, f32[8,128]{1,0:T(8,128)S(1)}) custom-call(f32[40,128]{1,0:T(8,128)S(1)} %get-tuple-element.36.rates.moved_rates, f32[2,640,128]{2,1,0:T(8,128)S(1)} %get-tuple-element.48.partial, f32[120,128]{1,0:T(8,128)S(1)} %get-tuple-element.43.core_first, f32[120,128]{1,0:T(8,128)S(1)} %get-tuple-element.44.link_first, ...), custom_call_target="tpu_custom_call" | custom-call | flops 1000 | tf_op jit(solution)/shard_map/pallas_call | solution.py:48
  26.4 1.1 %collective-permute-done.8.got = f32[40,128]{1,0:T(8,128)S(1)} collective-permute-done((f32[40,128]{1,0:T(8,128)S(1)}, f32[40,128]{1,0:T(8,128)S(1)}, u32[]{:S(2)}, u32[]{:S(2)}) %collective-permute-start.8) | collective-permute-done | bytes 20512 | tf_op jit(solution)/shard_map/ppermute | solution.py:642
  27.5 0.1 collective-permute-start.9
  27.6 1.2 %collective-permute-done.9.got = f32[40,128]{1,0:T(8,128)S(1)} collective-permute-done((f32[40,128]{1,0:T(8,128)S(1)}, f32[40,128]{1,0:T(8,128)S(1)}, u32[]{:S(2)}, u32[]{:S(2)}) %collective-permute-start.9) | collective-permute-done | bytes 20512 | tf_op jit(solution)/shard_map/ppermute | solution.py:642
  28.8 0.6 %copy.6 = f32[1,1,5,6,256]{4,1,3,2,0:T(1,128)} copy(f32[1,1,5,6,256]{4,3,2,1,0:T(8,128)S(1)} %shard_map.69) | data formatting | bytes 61440
  (8 shorter events, 0.1 us)
Async XLA Ops:
  1.8 8.4 %collective-permute-start = (f32[48,256]{1,0:T(8,128)S(1)}, f32[48,256]{1,0:T(8,128)S(1)}, u32[]{:S(2)}, u32[]{:S(2)}) collective-permute-start(f32[48,256]{1,0:T(8,128)S(1)} %get-tuple-element.31), channel_id=1, source_target_pairs={{0,1},{1,0},{2,3},{3,2},{4,5},{5,4},{6,7},{7,6},{8,9},{9,8},{10,11... | collective-permute-start | bytes 147464 | tf_op jit(solution)/shard_map/ppermute | solution.py:642
  4.9 7.5 %collective-permute-start.1 = (f32[48,256]{1,0:T(8,128)S(1)}, f32[48,256]{1,0:T(8,128)S(1)}, u32[]{:S(2)}, u32[]{:S(2)}) collective-permute-start(f32[48,256]{1,0:T(8,128)S(1)} %get-tuple-element.32), channel_id=1, source_target_pairs={{0,31},{1,2},{2,1},{3,4},{4,3},{5,6},{6,5},{7,8},{8,7},{9,10},{10,... | collective-permute-start | bytes 147464 | tf_op jit(solution)/shard_map/ppermute | solution.py:642
  8.5 5.8 %collective-permute-start.2 = (f32[120,256]{1,0:T(8,128)S(1)}, f32[120,256]{1,0:T(8,128)S(1)}, u32[]{:S(2)}, u32[]{:S(2)}) collective-permute-start(f32[120,256]{1,0:T(8,128)S(1)} %get-tuple-element.37), channel_id=1, source_target_pairs={{0,1},{1,0},{2,3},{3,2},{4,5},{5,4},{6,7},{7,6},{8,9},{9,8},{10,11... | collective-permute-start | bytes 368648 | tf_op jit(solution)/shard_map/ppermute | solution.py:642
  8.5 9.0 %collective-permute-start.3 = (f32[120,256]{1,0:T(8,128)S(1)}, f32[120,256]{1,0:T(8,128)S(1)}, u32[]{:S(2)}, u32[]{:S(2)}) collective-permute-start(f32[120,256]{1,0:T(8,128)S(1)} %get-tuple-element.38), channel_id=1, source_target_pairs={{0,31},{1,2},{2,1},{3,4},{4,3},{5,6},{6,5},{7,8},{8,7},{9,10},{10,... | collective-permute-start | bytes 368648 | tf_op jit(solution)/shard_map/ppermute | solution.py:642
  12.5 5.4 %collective-permute-start.4 = (f32[168,128]{1,0:T(8,128)S(1)}, f32[168,128]{1,0:T(8,128)S(1)}, u32[]{:S(2)}, u32[]{:S(2)}) collective-permute-start(f32[168,128]{1,0:T(8,128)S(1)} %get-tuple-element.40.link_sent), channel_id=1, source_target_pairs={{0,24},{1,25},{2,26},{3,27},{4,28},{5,29},{6,30},{7,31},{8,16},{9,... | collective-permute-start | bytes 258056 | tf_op jit(solution)/shard_map/ppermute | solution.py:642
  12.6 5.3 %collective-permute-start.5 = (f32[168,128]{1,0:T(8,128)S(1)}, f32[168,128]{1,0:T(8,128)S(1)}, u32[]{:S(2)}, u32[]{:S(2)}) collective-permute-start(f32[168,128]{1,0:T(8,128)S(1)} %get-tuple-element.41.core_sent), channel_id=1, source_target_pairs={{0,8},{1,9},{2,10},{3,11},{4,12},{5,13},{6,14},{7,15},{8,0},{9,1},... | collective-permute-start | bytes 258056 | tf_op jit(solution)/shard_map/ppermute | solution.py:642
  18.0 2.8 %collective-permute-start.6 = (f32[176,128]{1,0:T(8,128)S(1)}, f32[176,128]{1,0:T(8,128)S(1)}, u32[]{:S(2)}, u32[]{:S(2)}) collective-permute-start(f32[176,128]{1,0:T(8,128)S(1)} %get-tuple-element.47.far_sent), channel_id=1, source_target_pairs={{0,8},{1,2},{2,1},{3,4},{4,3},{5,6},{6,5},{7,15},{8,0},{9,10},{10,... | collective-permute-start | bytes 270344 | tf_op jit(solution)/shard_map/ppermute | solution.py:642
  18.1 5.0 %collective-permute-start.7 = (f32[176,128]{1,0:T(8,128)S(1)}, f32[176,128]{1,0:T(8,128)S(1)}, u32[]{:S(2)}, u32[]{:S(2)}) collective-permute-start(f32[176,128]{1,0:T(8,128)S(1)} %get-tuple-element.49.near_sent), channel_id=1, source_target_pairs={{0,1},{1,0},{2,3},{3,2},{4,5},{5,4},{6,7},{7,6},{8,9},{9,8},{10,11... | collective-permute-start | bytes 270344 | tf_op jit(solution)/shard_map/ppermute | solution.py:642
  23.6 3.8 %collective-permute-start.8 = (f32[40,128]{1,0:T(8,128)S(1)}, f32[40,128]{1,0:T(8,128)S(1)}, u32[]{:S(2)}, u32[]{:S(2)}) collective-permute-start(f32[40,128]{1,0:T(8,128)S(1)} %get-tuple-element.56), channel_id=1, source_target_pairs={{0,1},{1,0},{2,3},{3,2},{4,5},{5,4},{6,7},{7,6},{8,9},{9,8},{10,11... | collective-permute-start | bytes 61448 | tf_op jit(solution)/shard_map/ppermute | solution.py:642
  27.5 1.3 %collective-permute-start.9 = (f32[40,128]{1,0:T(8,128)S(1)}, f32[40,128]{1,0:T(8,128)S(1)}, u32[]{:S(2)}, u32[]{:S(2)}) collective-permute-start(f32[40,128]{1,0:T(8,128)S(1)} %get-tuple-element.59), channel_id=1, source_target_pairs={{0,8},{1,9},{2,10},{3,11},{4,12},{5,13},{6,14},{7,15},{8,0},{9,1},... | collective-permute-start | bytes 61448 | tf_op jit(solution)/shard_map/ppermute | solution.py:642

commit v6 on v5

--- a/solution.py
+++ b/solution.py
@@ -521,29 +521,18 @@
         sent[row : row + BZ, :] = jnp.where(y_first, columns[1], columns[0])
 
 
-def half_kernel(shape, kept, got, _, mine, sent):
-    gx, _, _ = place_of(shape)
-    first = gx % 2 == 0
-    top = subs() < 4
-    for i in range(NC):
-        a, b = kept[i * BZ : i * BZ + BZ, :], got[i * BZ : i * BZ + BZ, :]
-        rows = (jnp.where(top, a, rs(b, 4)), jnp.where(top, rs(a, 4), b))
-        mine[i * BZ : i * BZ + BZ, :] = jnp.where(first, rows[0], rows[1])
-        sent[i * BZ : i * BZ + BZ, :] = jnp.where(first, rows[1], rows[0])
-
-
-def register_kernel(shape, mine, got, out):
+def register_kernel(shape, kept, by_both, by_column, by_row, _, out):
     x_first, y_first, _, _ = ends(shape)
     sub = subs()
     for c in range(NC):
-        m, g = mine[c * BZ : c * BZ + BZ, :], got[c * BZ : c * BZ + BZ, :]
-        m4, g4 = rs(m, 4), rs(g, 4)
+        own, column, row, both = (ref[c * BZ : c * BZ + BZ, :] for ref in (kept, by_column, by_row, by_both))
+        m, m4, g, g4 = (jnp.where(x_first, t, rs(t, 4)) for t in (own, column, row, both))
         for h in range(2):
             same_y, same_x = (y_first, x_first) if h == 0 else (~y_first, ~x_first)
             a, b = jnp.where(same_y, m, m4), jnp.where(same_y, g, g4)
             x0, x1 = jnp.where(x_first, a, b), jnp.where(x_first, b, a)
             t, t4 = jnp.where(same_x, m, g), jnp.where(same_x, m4, g4)
-            y0, y1 = jnp.where(y_first, rs(t, 1), rs(t, 5)), jnp.where(y_first, rs(t, 6), rs(t, 2))
+            y0, y1 = jnp.where(y_first, rs(t, 1), rs(t4, 1)), jnp.where(y_first, rs(t4, 2), rs(t, 2))
             rows = jnp.where(sub == 0, x0, jnp.where(sub == 1, rs(x1, 1), rs(t + t4, 2)))
             rows = jnp.where(sub == 2, y0, jnp.where(sub == 3, y1, rows))
             out[0, 0, c, :, h * L : h * L + L] = rows[:6]
@@ -645,6 +634,7 @@
     odd_pairs = [(i, (i + 1) % count if i % 2 else (i - 1) % count) for i in range(count)]
     at = lambda a, b: a * columns + b
     core_pairs = [(at(a, b), at(a ^ 1, b)) for a in range(rows) for b in range(columns)]
+    both_pairs = [(at(a, b), at(a ^ 1, b ^ 1)) for a in range(rows) for b in range(columns)]
     link_pairs = [
         (at(a, b), at((a + 1) % rows if a % 2 else (a - 1) % rows, b)) for a in range(rows) for b in range(columns)
     ]
@@ -718,8 +708,9 @@
         [(a, "vmem") for a in (part, rates, masks, tops, link_first, far_got, near_got, far, own_far)],
         [plane, ((PLANE, L), "vmem"), ((PLANE, L), "vmem")],
     )
-    got = swap(sent, even_pairs)
-
+    by_both = swap(sent, both_pairs)
+    by_column = swap(sent, even_pairs)
+    by_row = swap(kept, core_pairs)
     smoothed, done = call(
         k(smooth_kernel),
         [(a, "vmem") for a in (rates, second, core_first, link_first, far_got, near_got, near, y_far)],
@@ -731,10 +722,10 @@
             pltpu.SemaphoreType.DMA((NC,)),
         ],
     )
-    mine, sent = call(k(half_kernel), [(a, "vmem") for a in (kept, got, done)], [((PLANE, L), "vmem")] * 2)
-    got = swap(sent, core_pairs)
     (registers,) = call(
-        k(register_kernel), [(mine, "vmem"), (got, "vmem")], [((1, 1, NC, 6, 2 * L), "out")]
+        k(register_kernel),
+        [(a, "vmem") for a in (kept, by_both, by_column, by_row, done)],
+        [((1, 1, NC, 6, 2 * L), "out")],
     )
     return smoothed, registers
 

time: 29.6 us -> 29 us (0.980)
  waiting for transfers between devices: 10.1 us -> 8.97 us
  starting transfers between devices: 11.4 us -> 11.9 us
    ppermute x10 -> x11, waiting for transfers between devices: 10.1 us -> 8.97 us  [swap(): return lax.ppermute(array, both, pairs)]
    ppermute x10 -> x11, starting transfers between devices: 11.4 us -> 11.9 us  [swap(): return lax.ppermute(array, both, pairs)]
    pallas_call x11 -> x10, Pallas kernels: 6.57 us -> 6.57 us  [call(): pl.pallas_call(kernel, out_shape=shapes, in_specs=in_specs, out_specs=out...]
  transfers between devices with their start and end apart: 10 -> 11, of which waited for: 6 -> 5; matrix products, arithmetic and copies ran while one was open for 0% -> 0% of each run, Pallas kernels for 16% -> 16%
where the time goes in v6:
time: 29 us; the launch traced here: 28.9 us
  starting transfers between devices  11.9 us (41%)
  waiting for transfers between devices  8.97 us (31%)
  Pallas kernels  6.57 us (23%)
  between operations  0.74 us (3%)
  local copies, waits for them, and re-layouts  0.64 us (2%)
    ppermute x11, starting transfers between devices, swap(): return lax.ppermute(array, both, pairs)  11.9 us
    ppermute x11, waiting for transfers between devices, swap(): return lax.ppermute(array, both, pairs)  8.97 us
    pallas_call x10, Pallas kernels, call(): pl.pallas_call(kernel, out_shape=shapes, in_specs=in_specs, out_specs=out...  6.57 us
    unnamed x1, local copies, waits for them, and re-layouts  0.64 us
  transfers between devices with their start and end apart: 11, of which 5 were waited for; matrix products, arithmetic and copies ran while one was open for 0% of the time, Pallas kernels for 16%

profile of v6, /device:TPU:0, one launch (start us, length us, event | category | flops | bytes accessed | tf_op | source)
XLA Modules:
  0.0 28.9 jit_solution(18395297960661317490)
XLA Ops:
  0.6 1.2 %shard_map.59 = (f32[48,256]{1,0:T(8,128)S(1)}, f32[48,256]{1,0:T(8,128)S(1)}, f32[120,256]{1,0:T(8,128)S(1)}, f32[120,256]{1,0:T(8,128)S(1)}, f32[8,5,16,256]{3...) custom-call(s32[1,1,8]{2,1,0:T(1,128)} %place_hbm.1, ...), custom_call_target="tpu_custom_call" | custom-call | flops 1000 | tf_op jit(solution)/shard_map/pallas_call | solution.py:48
  1.8 3.0 %collective-permute-start = (f32[48,256]{1,0:T(8,128)S(1)}, f32[48,256]{1,0:T(8,128)S(1)}, u32[]{:S(2)}, u32[]{:S(2)}) collective-permute-start(f32[48,256]{1,0:T(8,128)S(1)} %get-tuple-element.29), channel_id=1, source_target_pairs={{0,1},{1,0},{2,3},{3,2},{4,5},{5,4},{6,7},{7,6},{8,9},{9,8},{10,11... | collective-permute-start | bytes 147464 | tf_op jit(solution)/shard_map/ppermute | solution.py:631
  4.9 3.6 %collective-permute-start.1 = (f32[48,256]{1,0:T(8,128)S(1)}, f32[48,256]{1,0:T(8,128)S(1)}, u32[]{:S(2)}, u32[]{:S(2)}) collective-permute-start(f32[48,256]{1,0:T(8,128)S(1)} %get-tuple-element.30), channel_id=1, source_target_pairs={{0,31},{1,2},{2,1},{3,4},{4,3},{5,6},{6,5},{7,8},{8,7},{9,10},{10,... | collective-permute-start | bytes 147464 | tf_op jit(solution)/shard_map/ppermute | solution.py:631
  8.5 1.7 %collective-permute-start.3 = (f32[120,256]{1,0:T(8,128)S(1)}, f32[120,256]{1,0:T(8,128)S(1)}, u32[]{:S(2)}, u32[]{:S(2)}) collective-permute-start(f32[120,256]{1,0:T(8,128)S(1)} %get-tuple-element.36), channel_id=1, source_target_pairs={{0,31},{1,2},{2,1},{3,4},{4,3},{5,6},{6,5},{7,8},{8,7},{9,10},{10,... | collective-permute-start | bytes 368648 | tf_op jit(solution)/shard_map/ppermute | solution.py:631
  10.2 2.2 %collective-permute-done.1.odd = f32[48,256]{1,0:T(8,128)S(1)} collective-permute-done((f32[48,256]{1,0:T(8,128)S(1)}, f32[48,256]{1,0:T(8,128)S(1)}, u32[]{:S(2)}, u32[]{:S(2)}) %collective-permute-start.1) | collective-permute-done | bytes 49184 | tf_op jit(solution)/shard_map/ppermute | solution.py:631
  12.4 0.1 shard_map.60
  12.5 0.1 collective-permute-start.4
  12.6 1.3 %collective-permute-start.5 = (f32[168,128]{1,0:T(8,128)S(1)}, f32[168,128]{1,0:T(8,128)S(1)}, u32[]{:S(2)}, u32[]{:S(2)}) collective-permute-start(f32[168,128]{1,0:T(8,128)S(1)} %get-tuple-element.39.core_sent), channel_id=1, source_target_pairs={{0,8},{1,9},{2,10},{3,11},{4,12},{5,13},{6,14},{7,15},{8,0},{9,1},... | collective-permute-start | bytes 258056 | tf_op jit(solution)/shard_map/ppermute | solution.py:631
  13.9 0.3 shard_map.61.moved
  14.2 0.1 collective-permute-done.2.even_rest
  14.3 3.2 %collective-permute-done.3.odd_rest = f32[120,256]{1,0:T(8,128)S(1)} collective-permute-done((f32[120,256]{1,0:T(8,128)S(1)}, f32[120,256]{1,0:T(8,128)S(1)}, u32[]{:S(2)}, u32[]{:S(2)}) %collective-permute-start.3) | collective-permute-done | bytes 122912 | tf_op jit(solution)/shard_map/ppermute | solution.py:631
  17.5 0.4 %shard_map.62 = (f32[2,640,128]{2,1,0:T(8,128)S(1)}, f32[160,128]{1,0:T(8,128)S(1)}, f32[160,128]{1,0:T(8,128)S(1)}) custom-call(f32[48,256]{1,0:T(8,128)S(1)} %collective-permute-done.even, f32[48,256]{1,0:T(8,128)S(1)} %collective-permute-done.1.odd, f32[120,256]{1,0:T(8,128)S(1)} %collective-permute-done.2.even_rest, ...), custom_call_target="tpu_custom_call" | custom-call | flops 1000 | tf_op jit(solution)/shard_map/pallas_call | solution.py:48
  17.9 0.1 shard_map.64
  18.1 0.2 collective-permute-start.7
  18.3 1.4 %shard_map.63 = (f32[2,640,128]{2,1,0:T(8,128)S(1)}, f32[120,128]{1,0:T(8,128)S(1)}, f32[120,128]{1,0:T(8,128)S(1)}, f32[40,128]{1,0:T(8,128)S(1)}) custom-call(f32[2,640,128]{2,1,0:T(8,128)S(1)} %get-tuple-element.37.moved, f32[40,128]{1,0:T(8,128)S(1)} %get-tuple-element.34.rates.moved_rates, f32[168,128]{1,0:T(8,128)S(1)} %collective-permute-done.4.link, ...), custom_call_target="tpu_custom_call" | custom-call | flops 1000 | tf_op jit(solution)/shard_map/pallas_call | solution.py:48
  19.7 1.1 %shard_map.65 = (f32[2,640,128]{2,1,0:T(8,128)S(1)}, f32[80,128]{1,0:T(8,128)S(1)}) custom-call(f32[2,640,128]{2,1,0:T(8,128)S(1)} %get-tuple-element.37.moved, f32[40,128]{1,0:T(8,128)S(1)} %get-tuple-element.34.rates.moved_rates, f32[2,640,128]{2,1,0:T(8,128)S(1)} %get-tuple-element.40.partial, f32[120,128]{1,0:T(8,128)S(1)} %get-tuple-element.41.core_first, ...), custom_call_target="tpu_custom_call" | custom-call | flops 1000 | tf_op jit(solution)/shard_map/pallas_call | solution.py:48
  20.8 2.3 %collective-permute-done.7.near = f32[176,128]{1,0:T(8,128)S(1)} collective-permute-done((f32[176,128]{1,0:T(8,128)S(1)}, f32[176,128]{1,0:T(8,128)S(1)}, u32[]{:S(2)}, u32[]{:S(2)}) %collective-permute-start.7) | collective-permute-done | bytes 90144 | tf_op jit(solution)/shard_map/ppermute | solution.py:631
  23.2 0.5 %shard_map.66 = (f32[80,128]{1,0:T(8,128)S(1)}, f32[40,128]{1,0:T(8,128)S(1)}, f32[40,128]{1,0:T(8,128)S(1)}) custom-call(f32[2,640,128]{2,1,0:T(8,128)S(1)} %get-tuple-element.40.partial, f32[40,128]{1,0:T(8,128)S(1)} %get-tuple-element.34.rates.moved_rates, f32[24,128]{1,0:T(8,128)S(1)} %get-tuple-element.48.masks, f32[40,128]{1,0:T(8,128)S(1)} %get-tuple-element.49.tops, ...), custom_call_target="tpu_custom_call" | custom-call | flops 1000 | tf_op jit(solution)/shard_map/pallas_call | solution.py:48
  23.6 0.7 %collective-permute-start.8 = (f32[40,128]{1,0:T(8,128)S(1)}, f32[40,128]{1,0:T(8,128)S(1)}, u32[]{:S(2)}, u32[]{:S(2)}) collective-permute-start(f32[40,128]{1,0:T(8,128)S(1)} %get-tuple-element.54), channel_id=1, source_target_pairs={{0,9},{1,8},{2,11},{3,10},{4,13},{5,12},{6,15},{7,14},{8,1},{9,0},... | collective-permute-start | bytes 61448 | tf_op jit(solution)/shard_map/ppermute | solution.py:631
  24.4 0.6 %collective-permute-start.9 = (f32[40,128]{1,0:T(8,128)S(1)}, f32[40,128]{1,0:T(8,128)S(1)}, u32[]{:S(2)}, u32[]{:S(2)}) collective-permute-start(f32[40,128]{1,0:T(8,128)S(1)} %get-tuple-element.54), channel_id=1, source_target_pairs={{0,1},{1,0},{2,3},{3,2},{4,5},{5,4},{6,7},{7,6},{8,9},{9,8},{10,11... | collective-permute-start | bytes 61448 | tf_op jit(solution)/shard_map/ppermute | solution.py:631
  25.0 0.5 %collective-permute-start.10 = (f32[40,128]{1,0:T(8,128)S(1)}, f32[40,128]{1,0:T(8,128)S(1)}, u32[]{:S(2)}, u32[]{:S(2)}) collective-permute-start(f32[40,128]{1,0:T(8,128)S(1)} %get-tuple-element.53.kept), channel_id=1, source_target_pairs={{0,8},{1,9},{2,10},{3,11},{4,12},{5,13},{6,14},{7,15},{8,0},{9,1},... | collective-permute-start | bytes 61448 | tf_op jit(solution)/shard_map/ppermute | solution.py:631
  25.6 1.4 %shard_map.67 = (f32[1,1,8,5,16,256]{5,4,3,2,1,0:T(8,128)}, f32[8,128]{1,0:T(8,128)S(1)}) custom-call(f32[40,128]{1,0:T(8,128)S(1)} %get-tuple-element.34.rates.moved_rates, f32[2,640,128]{2,1,0:T(8,128)S(1)} %get-tuple-element.46.partial, f32[120,128]{1,0:T(8,128)S(1)} %get-tuple-element.41.core_first, f32[120,128]{1,0:T(8,128)S(1)} %get-tuple-element.42.link_first, ...), custom_call_target="tpu_custom_call" | custom-call | flops 1000 | tf_op jit(solution)/shard_map/pallas_call | solution.py:48
  27.0 1.1 %collective-permute-done.9.by_column = f32[40,128]{1,0:T(8,128)S(1)} collective-permute-done((f32[40,128]{1,0:T(8,128)S(1)}, f32[40,128]{1,0:T(8,128)S(1)}, u32[]{:S(2)}, u32[]{:S(2)}) %collective-permute-start.9) | collective-permute-done | bytes 20512 | tf_op jit(solution)/shard_map/ppermute | solution.py:631
  28.2 0.6 %copy.6 = f32[1,1,5,6,256]{4,1,3,2,0:T(1,128)} copy(f32[1,1,5,6,256]{4,3,2,1,0:T(8,128)S(1)} %shard_map.68) | data formatting | bytes 61440
  (9 shorter events, 0.1 us)
Async XLA Ops:
  1.8 8.4 %collective-permute-start = (f32[48,256]{1,0:T(8,128)S(1)}, f32[48,256]{1,0:T(8,128)S(1)}, u32[]{:S(2)}, u32[]{:S(2)}) collective-permute-start(f32[48,256]{1,0:T(8,128)S(1)} %get-tuple-element.29), channel_id=1, source_target_pairs={{0,1},{1,0},{2,3},{3,2},{4,5},{5,4},{6,7},{7,6},{8,9},{9,8},{10,11... | collective-permute-start | bytes 147464 | tf_op jit(solution)/shard_map/ppermute | solution.py:631
  4.9 7.5 %collective-permute-start.1 = (f32[48,256]{1,0:T(8,128)S(1)}, f32[48,256]{1,0:T(8,128)S(1)}, u32[]{:S(2)}, u32[]{:S(2)}) collective-permute-start(f32[48,256]{1,0:T(8,128)S(1)} %get-tuple-element.30), channel_id=1, source_target_pairs={{0,31},{1,2},{2,1},{3,4},{4,3},{5,6},{6,5},{7,8},{8,7},{9,10},{10,... | collective-permute-start | bytes 147464 | tf_op jit(solution)/shard_map/ppermute | solution.py:631
  8.5 5.8 %collective-permute-start.2 = (f32[120,256]{1,0:T(8,128)S(1)}, f32[120,256]{1,0:T(8,128)S(1)}, u32[]{:S(2)}, u32[]{:S(2)}) collective-permute-start(f32[120,256]{1,0:T(8,128)S(1)} %get-tuple-element.35), channel_id=1, source_target_pairs={{0,1},{1,0},{2,3},{3,2},{4,5},{5,4},{6,7},{7,6},{8,9},{9,8},{10,11... | collective-permute-start | bytes 368648 | tf_op jit(solution)/shard_map/ppermute | solution.py:631
  8.5 9.0 %collective-permute-start.3 = (f32[120,256]{1,0:T(8,128)S(1)}, f32[120,256]{1,0:T(8,128)S(1)}, u32[]{:S(2)}, u32[]{:S(2)}) collective-permute-start(f32[120,256]{1,0:T(8,128)S(1)} %get-tuple-element.36), channel_id=1, source_target_pairs={{0,31},{1,2},{2,1},{3,4},{4,3},{5,6},{6,5},{7,8},{8,7},{9,10},{10,... | collective-permute-start | bytes 368648 | tf_op jit(solution)/shard_map/ppermute | solution.py:631
  12.5 5.4 %collective-permute-start.4 = (f32[168,128]{1,0:T(8,128)S(1)}, f32[168,128]{1,0:T(8,128)S(1)}, u32[]{:S(2)}, u32[]{:S(2)}) collective-permute-start(f32[168,128]{1,0:T(8,128)S(1)} %get-tuple-element.38.link_sent), channel_id=1, source_target_pairs={{0,24},{1,25},{2,26},{3,27},{4,28},{5,29},{6,30},{7,31},{8,16},{9,... | collective-permute-start | bytes 258056 | tf_op jit(solution)/shard_map/ppermute | solution.py:631
  12.6 5.3 %collective-permute-start.5 = (f32[168,128]{1,0:T(8,128)S(1)}, f32[168,128]{1,0:T(8,128)S(1)}, u32[]{:S(2)}, u32[]{:S(2)}) collective-permute-start(f32[168,128]{1,0:T(8,128)S(1)} %get-tuple-element.39.core_sent), channel_id=1, source_target_pairs={{0,8},{1,9},{2,10},{3,11},{4,12},{5,13},{6,14},{7,15},{8,0},{9,1},... | collective-permute-start | bytes 258056 | tf_op jit(solution)/shard_map/ppermute | solution.py:631
  18.0 2.8 %collective-permute-start.6 = (f32[176,128]{1,0:T(8,128)S(1)}, f32[176,128]{1,0:T(8,128)S(1)}, u32[]{:S(2)}, u32[]{:S(2)}) collective-permute-start(f32[176,128]{1,0:T(8,128)S(1)} %get-tuple-element.45.far_sent), channel_id=1, source_target_pairs={{0,8},{1,2},{2,1},{3,4},{4,3},{5,6},{6,5},{7,15},{8,0},{9,10},{10,... | collective-permute-start | bytes 270344 | tf_op jit(solution)/shard_map/ppermute | solution.py:631
  18.1 5.0 %collective-permute-start.7 = (f32[176,128]{1,0:T(8,128)S(1)}, f32[176,128]{1,0:T(8,128)S(1)}, u32[]{:S(2)}, u32[]{:S(2)}) collective-permute-start(f32[176,128]{1,0:T(8,128)S(1)} %get-tuple-element.47.near_sent), channel_id=1, source_target_pairs={{0,1},{1,0},{2,3},{3,2},{4,5},{5,4},{6,7},{7,6},{8,9},{9,8},{10,11... | collective-permute-start | bytes 270344 | tf_op jit(solution)/shard_map/ppermute | solution.py:631
  23.6 3.4 %collective-permute-start.8 = (f32[40,128]{1,0:T(8,128)S(1)}, f32[40,128]{1,0:T(8,128)S(1)}, u32[]{:S(2)}, u32[]{:S(2)}) collective-permute-start(f32[40,128]{1,0:T(8,128)S(1)} %get-tuple-element.54), channel_id=1, source_target_pairs={{0,9},{1,8},{2,11},{3,10},{4,13},{5,12},{6,15},{7,14},{8,1},{9,0},... | collective-permute-start | bytes 61448 | tf_op jit(solution)/shard_map/ppermute | solution.py:631
  24.4 3.8 %collective-permute-start.9 = (f32[40,128]{1,0:T(8,128)S(1)}, f32[40,128]{1,0:T(8,128)S(1)}, u32[]{:S(2)}, u32[]{:S(2)}) collective-permute-start(f32[40,128]{1,0:T(8,128)S(1)} %get-tuple-element.54), channel_id=1, source_target_pairs={{0,1},{1,0},{2,3},{3,2},{4,5},{5,4},{6,7},{7,6},{8,9},{9,8},{10,11... | collective-permute-start | bytes 61448 | tf_op jit(solution)/shard_map/ppermute | solution.py:631
  25.0 3.1 %collective-permute-start.10 = (f32[40,128]{1,0:T(8,128)S(1)}, f32[40,128]{1,0:T(8,128)S(1)}, u32[]{:S(2)}, u32[]{:S(2)}) collective-permute-start(f32[40,128]{1,0:T(8,128)S(1)} %get-tuple-element.53.kept), channel_id=1, source_target_pairs={{0,8},{1,9},{2,10},{3,11},{4,12},{5,13},{6,14},{7,15},{8,0},{9,1},... | collective-permute-start | bytes 61448 | tf_op jit(solution)/shard_map/ppermute | solution.py:631

commit v7 on v6

--- a/solution.py
+++ b/solution.py
@@ -23,6 +23,7 @@
 REST = MOVE * NC * 12
 XFACE = FACE + BZ
 YFACE = FACE + 2 * BZ
+YNEAR = 2 * PLANE + 2 * BZ
 
 VM = pltpu.VMEM
 SM = pltpu.SMEM
@@ -258,10 +259,11 @@
     return x_first, y_first, link_ok, far_ok
 
 
-def ysend_kernel(shape, link, core, rates, near, far, near_out, far_out):
+def ysend_kernel(shape, link, core, rates, near, far, near_out, next_out, far_out):
     x_first, y_first, link_ok, _ = ends(shape)
     lane = lanes()
-    near_out[:FACE, :] = near[...]
+    near_out[: 2 * PLANE, :] = near[: 2 * PLANE, :]
+    next_out[...] = near[2 * PLANE :, :]
     far_out[:FACE, :] = far[...]
     bottoms = [jnp.zeros((BZ, L), F32)] * 2
     tops = [jnp.zeros((BZ, L), F32)] * 2
@@ -283,17 +285,17 @@
         tops[1] = jnp.where(lane == L // 2 + c, rate, tops[1])
     for i in range(2):
         at = FACE + i * BZ
-        near_out[at : at + BZ, :] = jnp.where(y_first, tops[i], bottoms[i])
+        near_out[at - 2 * PLANE : at - 2 * PLANE + BZ, :] = jnp.where(y_first, tops[i], bottoms[i])
         far_out[at : at + BZ, :] = jnp.where(y_first, bottoms[i], tops[i])
 
 
-def extra_at(ref, c):
+def extra_at(ref, c, start=FACE):
     i, at = divmod(c, 4)
-    return rl(ref[FACE + i * BZ : FACE + i * BZ + BZ, :], -2 * E * at)
+    return rl(ref[start + i * BZ : start + i * BZ + BZ, :], -2 * E * at)
 
 
 def y_rate(ref, c):
-    return spread(ref[FACE + BZ : FACE + 2 * BZ, :], L // 2 + c)
+    return spread(ref[ref.shape[0] - BZ :, :], L // 2 + c)
 
 
 def z_parts(x, lane, sub, swap):
@@ -420,6 +422,11 @@
     return g0, g1, extra
 
 
+def near_ghosts(got, following, c):
+    second = None if following is None else pair_at(following, 0, c)
+    return pair_at(got, 0, c), second, extra_at(got, c, 2 * PLANE)
+
+
 def y_first_sweep(got, sent, ok, ghost, c, lane, sub, swap):
     g0, g1, extra = ghost
     own = pair_at(sent, 0, c)
@@ -459,7 +466,7 @@
     rate = [moved_rates[c * BZ : c * BZ + BZ, :] for c in each]
     scale = [1.0 / (1.0 + 6.0 * r) for r in rate]
     weight = [r * q for r, q in zip(rate, scale)]
-    near_g = [y_ghosts(near, None, c) for c in each]
+    near_g = [near_ghosts(near, None, c) for c in each]
     far_g = [y_ghosts(far, far_ok, c) for c in each]
     far_f = []
     for c in each:
@@ -565,7 +572,7 @@
 
 
 def smooth_kernel(
-    shape, rates, partial, core_first, link_first, far, near, near_sent, y_far, out, done, planes, held, boxes, sem
+    shape, rates, partial, core_first, link_first, far, near, following, near_sent, y_far, out, done, planes, held, boxes, sem
 ):
     done[...] = jnp.zeros((BZ, L), F32)
     x_first, y_first, _, far_ok = ends(shape)
@@ -581,7 +588,7 @@
     for c in range(NC):
         rate = rates[c * BZ : c * BZ + BZ, :]
         weight = rate / (1.0 + 6.0 * rate)
-        near_g, far_g = y_ghosts(near, None, c), y_ghosts(far, far_ok, c)
+        near_g, far_g = near_ghosts(near, following, c), y_ghosts(far, far_ok, c)
         near_f = y_first_sweep(near, near_sent, None, near_g, c, lane, sub, swap)
         ghosts_f = by_side(near_f, pair_at(y_far, 0, c), y_first)
         ghosts_r = by_side(near_g[0], far_g[0], y_first)
@@ -686,13 +693,14 @@
         [(a, "vmem") for a in (even_got, odd_got, even_rest_got, odd_rest_got, stayed)],
         [(big, "vmem"), ((FACE, L), "vmem"), ((FACE, L), "vmem")],
     )
-    near, far = call(
+    near, following, far = call(
         k(ysend_kernel),
         [(a, "vmem") for a in (link_got, core_got, rates, near, far)],
-        [((YFACE, L), "vmem"), ((YFACE, L), "vmem")],
+        [((YNEAR, L), "vmem"), ((2 * PLANE, L), "vmem"), ((YFACE, L), "vmem")],
     )
     near_got = swap(near, even_pairs)
     far_got = swap(far, far_pairs)
+    next_got = swap(following, even_pairs)
     part, core_first, link_first, tops = call(
         k(sweep_kernel),
         [(a, "vmem") for a in (moved, rates, link_got, core_got, core, link)],
@@ -713,7 +721,7 @@
     by_row = swap(kept, core_pairs)
     smoothed, done = call(
         k(smooth_kernel),
-        [(a, "vmem") for a in (rates, second, core_first, link_first, far_got, near_got, near, y_far)],
+        [(a, "vmem") for a in (rates, second, core_first, link_first, far_got, near_got, next_got, near, y_far)],
         [((1, 1, BZ, NC, E, 2 * L), "hbm"), ((BZ, L), "vmem")],
         [
             VM((2, 4 * PLANE, L), F32),

time: 29 us -> 28.3 us (0.976)
  waiting for transfers between devices: 8.97 us -> 6.41 us
  starting transfers between devices: 11.9 us -> 13.8 us
    ppermute x11 -> x12, waiting for transfers between devices: 8.97 us -> 6.41 us  [swap(): return lax.ppermute(array, both, pairs)]
    ppermute x11 -> x12, starting transfers between devices: 11.9 us -> 13.8 us  [swap(): return lax.ppermute(array, both, pairs)]
  transfers between devices with their start and end apart: 11 -> 12, of which waited for: 5 -> 4; matrix products, arithmetic and copies ran while one was open for 0% -> 0% of each run, Pallas kernels for 16% -> 19%
where the time goes in v7:
time: 28.3 us; the launch traced here: 28.2 us
  starting transfers between devices  13.8 us (49%)
  Pallas kernels  6.58 us (23%)
  waiting for transfers between devices  6.41 us (23%)
  between operations  0.73 us (3%)
  local copies, waits for them, and re-layouts  0.64 us (2%)
    ppermute x12, starting transfers between devices, swap(): return lax.ppermute(array, both, pairs)  13.8 us
    pallas_call x10, Pallas kernels, call(): pl.pallas_call(kernel, out_shape=shapes, in_specs=in_specs, out_specs=out...  6.58 us
    ppermute x12, waiting for transfers between devices, swap(): return lax.ppermute(array, both, pairs)  6.41 us
    unnamed x1, local copies, waits for them, and re-layouts  0.64 us
  transfers between devices with their start and end apart: 12, of which 4 were waited for; matrix products, arithmetic and copies ran while one was open for 0% of the time, Pallas kernels for 19%

profile of v7, /device:TPU:0, one launch (start us, length us, event | category | flops | bytes accessed | tf_op | source)
XLA Modules:
  0.0 28.2 jit_solution(2147655461842706417)
XLA Ops:
  0.6 1.2 %shard_map.59 = (f32[48,256]{1,0:T(8,128)S(1)}, f32[48,256]{1,0:T(8,128)S(1)}, f32[120,256]{1,0:T(8,128)S(1)}, f32[120,256]{1,0:T(8,128)S(1)}, f32[8,5,16,256]{3...) custom-call(s32[1,1,8]{2,1,0:T(1,128)} %place_hbm.1, ...), custom_call_target="tpu_custom_call" | custom-call | flops 1000 | tf_op jit(solution)/shard_map/pallas_call | solution.py:49
  1.8 3.0 %collective-permute-start = (f32[48,256]{1,0:T(8,128)S(1)}, f32[48,256]{1,0:T(8,128)S(1)}, u32[]{:S(2)}, u32[]{:S(2)}) collective-permute-start(f32[48,256]{1,0:T(8,128)S(1)} %get-tuple-element.30), channel_id=1, source_target_pairs={{0,1},{1,0},{2,3},{3,2},{4,5},{5,4},{6,7},{7,6},{8,9},{9,8},{10,11... | collective-permute-start | bytes 147464 | tf_op jit(solution)/shard_map/ppermute | solution.py:638
  4.9 3.6 %collective-permute-start.1 = (f32[48,256]{1,0:T(8,128)S(1)}, f32[48,256]{1,0:T(8,128)S(1)}, u32[]{:S(2)}, u32[]{:S(2)}) collective-permute-start(f32[48,256]{1,0:T(8,128)S(1)} %get-tuple-element.31), channel_id=1, source_target_pairs={{0,31},{1,2},{2,1},{3,4},{4,3},{5,6},{6,5},{7,8},{8,7},{9,10},{10,... | collective-permute-start | bytes 147464 | tf_op jit(solution)/shard_map/ppermute | solution.py:638
  8.5 1.7 %collective-permute-start.3 = (f32[120,256]{1,0:T(8,128)S(1)}, f32[120,256]{1,0:T(8,128)S(1)}, u32[]{:S(2)}, u32[]{:S(2)}) collective-permute-start(f32[120,256]{1,0:T(8,128)S(1)} %get-tuple-element.37), channel_id=1, source_target_pairs={{0,31},{1,2},{2,1},{3,4},{4,3},{5,6},{6,5},{7,8},{8,7},{9,10},{10,... | collective-permute-start | bytes 368648 | tf_op jit(solution)/shard_map/ppermute | solution.py:638
  10.2 2.2 %collective-permute-done.1.odd = f32[48,256]{1,0:T(8,128)S(1)} collective-permute-done((f32[48,256]{1,0:T(8,128)S(1)}, f32[48,256]{1,0:T(8,128)S(1)}, u32[]{:S(2)}, u32[]{:S(2)}) %collective-permute-start.1) | collective-permute-done | bytes 49184 | tf_op jit(solution)/shard_map/ppermute | solution.py:638
  12.4 0.1 shard_map.60
  12.5 0.1 collective-permute-start.4
  12.6 1.3 %collective-permute-start.5 = (f32[168,128]{1,0:T(8,128)S(1)}, f32[168,128]{1,0:T(8,128)S(1)}, u32[]{:S(2)}, u32[]{:S(2)}) collective-permute-start(f32[168,128]{1,0:T(8,128)S(1)} %get-tuple-element.40.core_sent), channel_id=1, source_target_pairs={{0,8},{1,9},{2,10},{3,11},{4,12},{5,13},{6,14},{7,15},{8,0},{9,1},... | collective-permute-start | bytes 258056 | tf_op jit(solution)/shard_map/ppermute | solution.py:638
  13.9 0.3 shard_map.61.moved
  14.2 0.1 collective-permute-done.2.even_rest
  14.3 3.2 %collective-permute-done.3.odd_rest = f32[120,256]{1,0:T(8,128)S(1)} collective-permute-done((f32[120,256]{1,0:T(8,128)S(1)}, f32[120,256]{1,0:T(8,128)S(1)}, u32[]{:S(2)}, u32[]{:S(2)}) %collective-permute-start.3) | collective-permute-done | bytes 122912 | tf_op jit(solution)/shard_map/ppermute | solution.py:638
  17.5 0.4 %shard_map.62 = (f32[2,640,128]{2,1,0:T(8,128)S(1)}, f32[160,128]{1,0:T(8,128)S(1)}, f32[160,128]{1,0:T(8,128)S(1)}) custom-call(f32[48,256]{1,0:T(8,128)S(1)} %collective-permute-done.even, f32[48,256]{1,0:T(8,128)S(1)} %collective-permute-done.1.odd, f32[120,256]{1,0:T(8,128)S(1)} %collective-permute-done.2.even_rest, ...), custom_call_target="tpu_custom_call" | custom-call | flops 1000 | tf_op jit(solution)/shard_map/pallas_call | solution.py:49
  17.9 0.1 shard_map.64
  18.1 0.2 collective-permute-start.7
  18.3 1.9 %collective-permute-start.8 = (f32[80,128]{1,0:T(8,128)S(1)}, f32[80,128]{1,0:T(8,128)S(1)}, u32[]{:S(2)}, u32[]{:S(2)}) collective-permute-start(f32[80,128]{1,0:T(8,128)S(1)} %get-tuple-element.49), channel_id=1, source_target_pairs={{0,1},{1,0},{2,3},{3,2},{4,5},{5,4},{6,7},{7,6},{8,9},{9,8},{10,11... | collective-permute-start | bytes 122888 | tf_op jit(solution)/shard_map/ppermute | solution.py:638
  20.2 1.4 %shard_map.63 = (f32[2,640,128]{2,1,0:T(8,128)S(1)}, f32[120,128]{1,0:T(8,128)S(1)}, f32[120,128]{1,0:T(8,128)S(1)}, f32[40,128]{1,0:T(8,128)S(1)}) custom-call(f32[2,640,128]{2,1,0:T(8,128)S(1)} %get-tuple-element.38.moved, f32[40,128]{1,0:T(8,128)S(1)} %get-tuple-element.35.rates.moved_rates, f32[168,128]{1,0:T(8,128)S(1)} %collective-permute-done.4.link, ...), custom_call_target="tpu_custom_call" | custom-call | flops 1000 | tf_op jit(solution)/shard_map/pallas_call | solution.py:49
  21.6 1.1 %shard_map.65 = (f32[2,640,128]{2,1,0:T(8,128)S(1)}, f32[80,128]{1,0:T(8,128)S(1)}) custom-call(f32[2,640,128]{2,1,0:T(8,128)S(1)} %get-tuple-element.38.moved, f32[40,128]{1,0:T(8,128)S(1)} %get-tuple-element.35.rates.moved_rates, f32[2,640,128]{2,1,0:T(8,128)S(1)} %get-tuple-element.41.partial, f32[120,128]{1,0:T(8,128)S(1)} %get-tuple-element.42.core_first, ...), custom_call_target="tpu_custom_call" | custom-call | flops 1000 | tf_op jit(solution)/shard_map/pallas_call | solution.py:49
  22.7 0.5 %shard_map.66 = (f32[80,128]{1,0:T(8,128)S(1)}, f32[40,128]{1,0:T(8,128)S(1)}, f32[40,128]{1,0:T(8,128)S(1)}) custom-call(f32[2,640,128]{2,1,0:T(8,128)S(1)} %get-tuple-element.41.partial, f32[40,128]{1,0:T(8,128)S(1)} %get-tuple-element.35.rates.moved_rates, f32[24,128]{1,0:T(8,128)S(1)} %get-tuple-element.50.masks, f32[40,128]{1,0:T(8,128)S(1)} %get-tuple-element.51.tops, ...), custom_call_target="tpu_custom_call" | custom-call | flops 1000 | tf_op jit(solution)/shard_map/pallas_call | solution.py:49
  23.2 0.3 %collective-permute-start.9 = (f32[40,128]{1,0:T(8,128)S(1)}, f32[40,128]{1,0:T(8,128)S(1)}, u32[]{:S(2)}, u32[]{:S(2)}) collective-permute-start(f32[40,128]{1,0:T(8,128)S(1)} %get-tuple-element.56), channel_id=1, source_target_pairs={{0,9},{1,8},{2,11},{3,10},{4,13},{5,12},{6,15},{7,14},{8,1},{9,0},... | collective-permute-start | bytes 61448 | tf_op jit(solution)/shard_map/ppermute | solution.py:638
  23.5 1.3 %collective-permute-start.10 = (f32[40,128]{1,0:T(8,128)S(1)}, f32[40,128]{1,0:T(8,128)S(1)}, u32[]{:S(2)}, u32[]{:S(2)}) collective-permute-start(f32[40,128]{1,0:T(8,128)S(1)} %get-tuple-element.56), channel_id=1, source_target_pairs={{0,1},{1,0},{2,3},{3,2},{4,5},{5,4},{6,7},{7,6},{8,9},{9,8},{10,11... | collective-permute-start | bytes 61448 | tf_op jit(solution)/shard_map/ppermute | solution.py:638
  24.8 0.3 %collective-permute-start.11 = (f32[40,128]{1,0:T(8,128)S(1)}, f32[40,128]{1,0:T(8,128)S(1)}, u32[]{:S(2)}, u32[]{:S(2)}) collective-permute-start(f32[40,128]{1,0:T(8,128)S(1)} %get-tuple-element.55.kept), channel_id=1, source_target_pairs={{0,8},{1,9},{2,10},{3,11},{4,12},{5,13},{6,14},{7,15},{8,0},{9,1},... | collective-permute-start | bytes 61448 | tf_op jit(solution)/shard_map/ppermute | solution.py:638
  25.2 1.4 %shard_map.67 = (f32[1,1,8,5,16,256]{5,4,3,2,1,0:T(8,128)}, f32[8,128]{1,0:T(8,128)S(1)}) custom-call(f32[40,128]{1,0:T(8,128)S(1)} %get-tuple-element.35.rates.moved_rates, f32[2,640,128]{2,1,0:T(8,128)S(1)} %get-tuple-element.47.partial, f32[120,128]{1,0:T(8,128)S(1)} %get-tuple-element.42.core_first, f32[120,128]{1,0:T(8,128)S(1)} %get-tuple-element.43.link_first, ...), custom_call_target="tpu_custom_call" | custom-call | flops 1000 | tf_op jit(solution)/shard_map/pallas_call | solution.py:49
  26.6 0.9 %collective-permute-done.10.by_column = f32[40,128]{1,0:T(8,128)S(1)} collective-permute-done((f32[40,128]{1,0:T(8,128)S(1)}, f32[40,128]{1,0:T(8,128)S(1)}, u32[]{:S(2)}, u32[]{:S(2)}) %collective-permute-start.10) | collective-permute-done | bytes 20512 | tf_op jit(solution)/shard_map/ppermute | solution.py:638
  27.6 0.6 %copy.6 = f32[1,1,5,6,256]{4,1,3,2,0:T(1,128)} copy(f32[1,1,5,6,256]{4,3,2,1,0:T(8,128)S(1)} %shard_map.68) | data formatting | bytes 61440
  (11 shorter events, 0.2 us)
Async XLA Ops:
  1.8 8.4 %collective-permute-start = (f32[48,256]{1,0:T(8,128)S(1)}, f32[48,256]{1,0:T(8,128)S(1)}, u32[]{:S(2)}, u32[]{:S(2)}) collective-permute-start(f32[48,256]{1,0:T(8,128)S(1)} %get-tuple-element.30), channel_id=1, source_target_pairs={{0,1},{1,0},{2,3},{3,2},{4,5},{5,4},{6,7},{7,6},{8,9},{9,8},{10,11... | collective-permute-start | bytes 147464 | tf_op jit(solution)/shard_map/ppermute | solution.py:638
  4.9 7.5 %collective-permute-start.1 = (f32[48,256]{1,0:T(8,128)S(1)}, f32[48,256]{1,0:T(8,128)S(1)}, u32[]{:S(2)}, u32[]{:S(2)}) collective-permute-start(f32[48,256]{1,0:T(8,128)S(1)} %get-tuple-element.31), channel_id=1, source_target_pairs={{0,31},{1,2},{2,1},{3,4},{4,3},{5,6},{6,5},{7,8},{8,7},{9,10},{10,... | collective-permute-start | bytes 147464 | tf_op jit(solution)/shard_map/ppermute | solution.py:638
  8.5 5.8 %collective-permute-start.2 = (f32[120,256]{1,0:T(8,128)S(1)}, f32[120,256]{1,0:T(8,128)S(1)}, u32[]{:S(2)}, u32[]{:S(2)}) collective-permute-start(f32[120,256]{1,0:T(8,128)S(1)} %get-tuple-element.36), channel_id=1, source_target_pairs={{0,1},{1,0},{2,3},{3,2},{4,5},{5,4},{6,7},{7,6},{8,9},{9,8},{10,11... | collective-permute-start | bytes 368648 | tf_op jit(solution)/shard_map/ppermute | solution.py:638
  8.5 9.0 %collective-permute-start.3 = (f32[120,256]{1,0:T(8,128)S(1)}, f32[120,256]{1,0:T(8,128)S(1)}, u32[]{:S(2)}, u32[]{:S(2)}) collective-permute-start(f32[120,256]{1,0:T(8,128)S(1)} %get-tuple-element.37), channel_id=1, source_target_pairs={{0,31},{1,2},{2,1},{3,4},{4,3},{5,6},{6,5},{7,8},{8,7},{9,10},{10,... | collective-permute-start | bytes 368648 | tf_op jit(solution)/shard_map/ppermute | solution.py:638
  12.5 5.4 %collective-permute-start.4 = (f32[168,128]{1,0:T(8,128)S(1)}, f32[168,128]{1,0:T(8,128)S(1)}, u32[]{:S(2)}, u32[]{:S(2)}) collective-permute-start(f32[168,128]{1,0:T(8,128)S(1)} %get-tuple-element.39.link_sent), channel_id=1, source_target_pairs={{0,24},{1,25},{2,26},{3,27},{4,28},{5,29},{6,30},{7,31},{8,16},{9,... | collective-permute-start | bytes 258056 | tf_op jit(solution)/shard_map/ppermute | solution.py:638
  12.6 5.3 %collective-permute-start.5 = (f32[168,128]{1,0:T(8,128)S(1)}, f32[168,128]{1,0:T(8,128)S(1)}, u32[]{:S(2)}, u32[]{:S(2)}) collective-permute-start(f32[168,128]{1,0:T(8,128)S(1)} %get-tuple-element.40.core_sent), channel_id=1, source_target_pairs={{0,8},{1,9},{2,10},{3,11},{4,12},{5,13},{6,14},{7,15},{8,0},{9,1},... | collective-permute-start | bytes 258056 | tf_op jit(solution)/shard_map/ppermute | solution.py:638
  18.0 4.7 %collective-permute-start.6 = (f32[176,128]{1,0:T(8,128)S(1)}, f32[176,128]{1,0:T(8,128)S(1)}, u32[]{:S(2)}, u32[]{:S(2)}) collective-permute-start(f32[176,128]{1,0:T(8,128)S(1)} %get-tuple-element.46.far_sent), channel_id=1, source_target_pairs={{0,8},{1,2},{2,1},{3,4},{4,3},{5,6},{6,5},{7,15},{8,0},{9,10},{10,... | collective-permute-start | bytes 270344 | tf_op jit(solution)/shard_map/ppermute | solution.py:638
  18.1 4.6 %collective-permute-start.7 = (f32[96,128]{1,0:T(8,128)S(1)}, f32[96,128]{1,0:T(8,128)S(1)}, u32[]{:S(2)}, u32[]{:S(2)}) collective-permute-start(f32[96,128]{1,0:T(8,128)S(1)} %get-tuple-element.48.near_sent), channel_id=1, source_target_pairs={{0,1},{1,0},{2,3},{3,2},{4,5},{5,4},{6,7},{7,6},{8,9},{9,8},{10,11... | collective-permute-start | bytes 147464 | tf_op jit(solution)/shard_map/ppermute | solution.py:638
  18.3 6.8 %collective-permute-start.8 = (f32[80,128]{1,0:T(8,128)S(1)}, f32[80,128]{1,0:T(8,128)S(1)}, u32[]{:S(2)}, u32[]{:S(2)}) collective-permute-start(f32[80,128]{1,0:T(8,128)S(1)} %get-tuple-element.49), channel_id=1, source_target_pairs={{0,1},{1,0},{2,3},{3,2},{4,5},{5,4},{6,7},{7,6},{8,9},{9,8},{10,11... | collective-permute-start | bytes 122888 | tf_op jit(solution)/shard_map/ppermute | solution.py:638
  23.2 3.4 %collective-permute-start.9 = (f32[40,128]{1,0:T(8,128)S(1)}, f32[40,128]{1,0:T(8,128)S(1)}, u32[]{:S(2)}, u32[]{:S(2)}) collective-permute-start(f32[40,128]{1,0:T(8,128)S(1)} %get-tuple-element.56), channel_id=1, source_target_pairs={{0,9},{1,8},{2,11},{3,10},{4,13},{5,12},{6,15},{7,14},{8,1},{9,0},... | collective-permute-start | bytes 61448 | tf_op jit(solution)/shard_map/ppermute | solution.py:638
  23.5 4.0 %collective-permute-start.10 = (f32[40,128]{1,0:T(8,128)S(1)}, f32[40,128]{1,0:T(8,128)S(1)}, u32[]{:S(2)}, u32[]{:S(2)}) collective-permute-start(f32[40,128]{1,0:T(8,128)S(1)} %get-tuple-element.56), channel_id=1, source_target_pairs={{0,1},{1,0},{2,3},{3,2},{4,5},{5,4},{6,7},{7,6},{8,9},{9,8},{10,11... | collective-permute-start | bytes 61448 | tf_op jit(solution)/shard_map/ppermute | solution.py:638
  24.8 2.7 %collective-permute-start.11 = (f32[40,128]{1,0:T(8,128)S(1)}, f32[40,128]{1,0:T(8,128)S(1)}, u32[]{:S(2)}, u32[]{:S(2)}) collective-permute-start(f32[40,128]{1,0:T(8,128)S(1)} %get-tuple-element.55.kept), channel_id=1, source_target_pairs={{0,8},{1,9},{2,10},{3,11},{4,12},{5,13},{6,14},{7,15},{8,0},{9,1},... | collective-permute-start | bytes 61448 | tf_op jit(solution)/shard_map/ppermute | solution.py:638

commit v8 on v7

--- a/solution.py
+++ b/solution.py
@@ -452,7 +452,7 @@
 
 
 def flux_kernel(
-    shape, partial, moved_rates, masks, tops, link_first, far, near, far_sent, own_far, y_far, kept, sent
+    shape, partial, moved_rates, masks, tops, link_first, far, near, far_sent, own_far, y_far, kept, to_row, to_column, to_both
 ):
     x_first, y_first, link_ok, far_ok = ends(shape)
     gx, gy, _ = place_of(shape)
@@ -520,20 +520,29 @@
         add = jnp.where((z == 8 * par_y) | (z == 8 * par_y + 7), add, 0.0)
         faces_z.append((tops[c * BZ : c * BZ + BZ, :] + add) * (0.25 * rate[c] * masks[2 * BZ :, :]))
     left = sub % 4 < 2
+    top = sub < 4
+    own_tiles, other_tiles = [], []
     for c in each:
         outer = jnp.where(upper, faces_y[c], faces_x[c])
         columns = (jnp.where(left, outer, rs(faces_z[c], 2)), jnp.where(left, rs(outer, -2), faces_z[c]))
-        row = c * BZ
-        kept[row : row + BZ, :] = jnp.where(y_first, columns[0], columns[1])
-        sent[row : row + BZ, :] = jnp.where(y_first, columns[1], columns[0])
+        own_tiles.append(jnp.where(y_first, columns[0], columns[1]))
+        other_tiles.append(jnp.where(y_first, columns[1], columns[0]))
+    for tiles, same, other in ((own_tiles, kept, to_row), (other_tiles, to_column, to_both)):
+        turned = [rs(t, 4) for t in tiles]
+        for i in range(0, NC, 2):
+            j = min(i + 1, NC - 1)
+            low, high = jnp.where(top, tiles[i], turned[j]), jnp.where(top, turned[i], tiles[j])
+            row = i // 2 * BZ
+            same[row : row + BZ, :] = jnp.where(x_first, low, high)
+            other[row : row + BZ, :] = jnp.where(x_first, high, low)
 
 
 def register_kernel(shape, kept, by_both, by_column, by_row, _, out):
     x_first, y_first, _, _ = ends(shape)
     sub = subs()
     for c in range(NC):
-        own, column, row, both = (ref[c * BZ : c * BZ + BZ, :] for ref in (kept, by_column, by_row, by_both))
-        m, m4, g, g4 = (jnp.where(x_first, t, rs(t, 4)) for t in (own, column, row, both))
+        at = c // 2 * BZ
+        m, m4, g, g4 = (rs(ref[at : at + BZ, :], 4 * (c % 2)) for ref in (kept, by_column, by_row, by_both))
         for h in range(2):
             same_y, same_x = (y_first, x_first) if h == 0 else (~y_first, ~x_first)
             a, b = jnp.where(same_y, m, m4), jnp.where(same_y, g, g4)
@@ -643,7 +652,9 @@
     core_pairs = [(at(a, b), at(a ^ 1, b)) for a in range(rows) for b in range(columns)]
     both_pairs = [(at(a, b), at(a ^ 1, b ^ 1)) for a in range(rows) for b in range(columns)]
     link_pairs = [
-        (at(a, b), at((a + 1) % rows if a % 2 else (a - 1) % rows, b)) for a in range(rows) for b in range(columns)
+        (at(a, b), at(a, b ^ 2) if a in (0, rows - 1) else at(a + 1 if a % 2 else a - 1, b))
+        for a in range(rows)
+        for b in range(columns)
     ]
     far_pairs = [
         (at(a, b), at(a ^ 1, b) if b in (0, columns - 1) else at(a, b + 1 if b % 2 else b - 1))
@@ -711,14 +722,14 @@
         [(a, "vmem") for a in (moved, rates, part, core_first, link_first, far)],
         [(big, "vmem"), plane],
     )
-    y_far, kept, sent = call(
+    y_far, kept, to_row, to_column, to_both = call(
         k(flux_kernel),
         [(a, "vmem") for a in (part, rates, masks, tops, link_first, far_got, near_got, far, own_far)],
-        [plane, ((PLANE, L), "vmem"), ((PLANE, L), "vmem")],
-    )
-    by_both = swap(sent, both_pairs)
-    by_column = swap(sent, even_pairs)
-    by_row = swap(kept, core_pairs)
+        [plane] + [(((NC + 1) // 2 * BZ, L), "vmem")] * 4,
+    )
+    by_both = swap(to_both, both_pairs)
+    by_column = swap(to_column, even_pairs)
+    by_row = swap(to_row, core_pairs)
     smoothed, done = call(
         k(smooth_kernel),
         [(a, "vmem") for a in (rates, second, core_first, link_first, far_got, near_got, next_got, near, y_far)],

time: 28.3 us -> 27.9 us (0.986)
  waiting for transfers between devices: 6.41 us -> 5.96 us
    ppermute x12, waiting for transfers between devices: 6.41 us -> 5.96 us  [swap(): return lax.ppermute(array, both, pairs)]
where the time goes in v8:
time: 27.9 us; the launch traced here: 27.8 us
  starting transfers between devices  13.8 us (49%)
  Pallas kernels  6.58 us (24%)
  waiting for transfers between devices  5.96 us (21%)
  between operations  0.74 us (3%)
  local copies, waits for them, and re-layouts  0.64 us (2%)
    ppermute x12, starting transfers between devices, swap(): return lax.ppermute(array, both, pairs)  13.8 us
    pallas_call x10, Pallas kernels, call(): pl.pallas_call(kernel, out_shape=shapes, in_specs=in_specs, out_specs=out...  6.58 us
    ppermute x12, waiting for transfers between devices, swap(): return lax.ppermute(array, both, pairs)  5.96 us
    unnamed x1, local copies, waits for them, and re-layouts  0.64 us
  transfers between devices with their start and end apart: 12, of which 4 were waited for; matrix products, arithmetic and copies ran while one was open for 0% of the time, Pallas kernels for 19%

profile of v8, /device:TPU:0, one launch (start us, length us, event | category | flops | bytes accessed | tf_op | source)
XLA Modules:
  0.0 27.8 jit_solution(2558908448693246749)
XLA Ops:
  0.6 1.2 %shard_map.59 = (f32[48,256]{1,0:T(8,128)S(1)}, f32[48,256]{1,0:T(8,128)S(1)}, f32[120,256]{1,0:T(8,128)S(1)}, f32[120,256]{1,0:T(8,128)S(1)}, f32[8,5,16,256]{3...) custom-call(s32[1,1,8]{2,1,0:T(1,128)} %place_hbm.1, ...), custom_call_target="tpu_custom_call" | custom-call | flops 1000 | tf_op jit(solution)/shard_map/pallas_call | solution.py:49
  1.8 3.0 %collective-permute-start = (f32[48,256]{1,0:T(8,128)S(1)}, f32[48,256]{1,0:T(8,128)S(1)}, u32[]{:S(2)}, u32[]{:S(2)}) collective-permute-start(f32[48,256]{1,0:T(8,128)S(1)} %get-tuple-element.32), channel_id=1, source_target_pairs={{0,1},{1,0},{2,3},{3,2},{4,5},{5,4},{6,7},{7,6},{8,9},{9,8},{10,11... | collective-permute-start | bytes 147464 | tf_op jit(solution)/shard_map/ppermute | solution.py:647
  4.9 3.6 %collective-permute-start.1 = (f32[48,256]{1,0:T(8,128)S(1)}, f32[48,256]{1,0:T(8,128)S(1)}, u32[]{:S(2)}, u32[]{:S(2)}) collective-permute-start(f32[48,256]{1,0:T(8,128)S(1)} %get-tuple-element.33), channel_id=1, source_target_pairs={{0,31},{1,2},{2,1},{3,4},{4,3},{5,6},{6,5},{7,8},{8,7},{9,10},{10,... | collective-permute-start | bytes 147464 | tf_op jit(solution)/shard_map/ppermute | solution.py:647
  8.5 1.7 %collective-permute-start.3 = (f32[120,256]{1,0:T(8,128)S(1)}, f32[120,256]{1,0:T(8,128)S(1)}, u32[]{:S(2)}, u32[]{:S(2)}) collective-permute-start(f32[120,256]{1,0:T(8,128)S(1)} %get-tuple-element.39), channel_id=1, source_target_pairs={{0,31},{1,2},{2,1},{3,4},{4,3},{5,6},{6,5},{7,8},{8,7},{9,10},{10,... | collective-permute-start | bytes 368648 | tf_op jit(solution)/shard_map/ppermute | solution.py:647
  10.2 2.2 %collective-permute-done.1.odd = f32[48,256]{1,0:T(8,128)S(1)} collective-permute-done((f32[48,256]{1,0:T(8,128)S(1)}, f32[48,256]{1,0:T(8,128)S(1)}, u32[]{:S(2)}, u32[]{:S(2)}) %collective-permute-start.1) | collective-permute-done | bytes 49184 | tf_op jit(solution)/shard_map/ppermute | solution.py:647
  12.4 0.1 shard_map.60
  12.5 0.1 collective-permute-start.4
  12.6 1.3 %collective-permute-start.5 = (f32[168,128]{1,0:T(8,128)S(1)}, f32[168,128]{1,0:T(8,128)S(1)}, u32[]{:S(2)}, u32[]{:S(2)}) collective-permute-start(f32[168,128]{1,0:T(8,128)S(1)} %get-tuple-element.42.core_sent), channel_id=1, source_target_pairs={{0,8},{1,9},{2,10},{3,11},{4,12},{5,13},{6,14},{7,15},{8,0},{9,1},... | collective-permute-start | bytes 258056 | tf_op jit(solution)/shard_map/ppermute | solution.py:647
  13.9 0.3 shard_map.61.moved
  14.2 0.1 collective-permute-done.2.even_rest
  14.3 3.2 %collective-permute-done.3.odd_rest = f32[120,256]{1,0:T(8,128)S(1)} collective-permute-done((f32[120,256]{1,0:T(8,128)S(1)}, f32[120,256]{1,0:T(8,128)S(1)}, u32[]{:S(2)}, u32[]{:S(2)}) %collective-permute-start.3) | collective-permute-done | bytes 122912 | tf_op jit(solution)/shard_map/ppermute | solution.py:647
  17.5 0.4 %shard_map.62 = (f32[2,640,128]{2,1,0:T(8,128)S(1)}, f32[160,128]{1,0:T(8,128)S(1)}, f32[160,128]{1,0:T(8,128)S(1)}) custom-call(f32[48,256]{1,0:T(8,128)S(1)} %collective-permute-done.even, f32[48,256]{1,0:T(8,128)S(1)} %collective-permute-done.1.odd, f32[120,256]{1,0:T(8,128)S(1)} %collective-permute-done.2.even_rest, ...), custom_call_target="tpu_custom_call" | custom-call | flops 1000 | tf_op jit(solution)/shard_map/pallas_call | solution.py:49
  17.9 0.1 shard_map.64
  18.1 0.6 %collective-permute-start.7 = (f32[96,128]{1,0:T(8,128)S(1)}, f32[96,128]{1,0:T(8,128)S(1)}, u32[]{:S(2)}, u32[]{:S(2)}) collective-permute-start(f32[96,128]{1,0:T(8,128)S(1)} %get-tuple-element.50.near_sent), channel_id=1, source_target_pairs={{0,1},{1,0},{2,3},{3,2},{4,5},{5,4},{6,7},{7,6},{8,9},{9,8},{10,11... | collective-permute-start | bytes 147464 | tf_op jit(solution)/shard_map/ppermute | solution.py:647
  18.7 1.5 %collective-permute-start.8 = (f32[80,128]{1,0:T(8,128)S(1)}, f32[80,128]{1,0:T(8,128)S(1)}, u32[]{:S(2)}, u32[]{:S(2)}) collective-permute-start(f32[80,128]{1,0:T(8,128)S(1)} %get-tuple-element.51), channel_id=1, source_target_pairs={{0,1},{1,0},{2,3},{3,2},{4,5},{5,4},{6,7},{7,6},{8,9},{9,8},{10,11... | collective-permute-start | bytes 122888 | tf_op jit(solution)/shard_map/ppermute | solution.py:647
  20.2 1.4 %shard_map.63 = (f32[2,640,128]{2,1,0:T(8,128)S(1)}, f32[120,128]{1,0:T(8,128)S(1)}, f32[120,128]{1,0:T(8,128)S(1)}, f32[40,128]{1,0:T(8,128)S(1)}) custom-call(f32[2,640,128]{2,1,0:T(8,128)S(1)} %get-tuple-element.40.moved, f32[40,128]{1,0:T(8,128)S(1)} %get-tuple-element.37.rates.moved_rates, f32[168,128]{1,0:T(8,128)S(1)} %collective-permute-done.4.link, ...), custom_call_target="tpu_custom_call" | custom-call | flops 1000 | tf_op jit(solution)/shard_map/pallas_call | solution.py:49
  21.6 1.1 %shard_map.65 = (f32[2,640,128]{2,1,0:T(8,128)S(1)}, f32[80,128]{1,0:T(8,128)S(1)}) custom-call(f32[2,640,128]{2,1,0:T(8,128)S(1)} %get-tuple-element.40.moved, f32[40,128]{1,0:T(8,128)S(1)} %get-tuple-element.37.rates.moved_rates, f32[2,640,128]{2,1,0:T(8,128)S(1)} %get-tuple-element.43.partial, f32[120,128]{1,0:T(8,128)S(1)} %get-tuple-element.44.core_first, ...), custom_call_target="tpu_custom_call" | custom-call | flops 1000 | tf_op jit(solution)/shard_map/pallas_call | solution.py:49
  22.7 0.5 %shard_map.66 = (f32[80,128]{1,0:T(8,128)S(1)}, f32[24,128]{1,0:T(8,128)S(1)}, f32[24,128]{1,0:T(8,128)S(1)}, f32[24,128]{1,0:T(8,128)S(1)}, f32[24,128]{1,0:T(8,128)S(1)}) custom-call(f32[2,640,128]{2,1,0:T(8,128)S(1)} %get-tuple-element.43.partial, f32[40,128]{1,0:T(8,128)S(1)} %get-tuple-element.37.rates.moved_rates, ...), custom_call_target="tpu_custom_call" | custom-call | flops 1000 | tf_op jit(solution)/shard_map/pallas_call | solution.py:49
  23.2 0.1 collective-permute-start.9
  23.3 1.5 %collective-permute-start.10 = (f32[24,128]{1,0:T(8,128)S(1)}, f32[24,128]{1,0:T(8,128)S(1)}, u32[]{:S(2)}, u32[]{:S(2)}) collective-permute-start(f32[24,128]{1,0:T(8,128)S(1)} %get-tuple-element.59), channel_id=1, source_target_pairs={{0,1},{1,0},{2,3},{3,2},{4,5},{5,4},{6,7},{7,6},{8,9},{9,8},{10,11... | collective-permute-start | bytes 36872 | tf_op jit(solution)/shard_map/ppermute | solution.py:647
  24.8 0.3 %collective-permute-start.11 = (f32[24,128]{1,0:T(8,128)S(1)}, f32[24,128]{1,0:T(8,128)S(1)}, u32[]{:S(2)}, u32[]{:S(2)}) collective-permute-start(f32[24,128]{1,0:T(8,128)S(1)} %get-tuple-element.60), channel_id=1, source_target_pairs={{0,8},{1,9},{2,10},{3,11},{4,12},{5,13},{6,14},{7,15},{8,0},{9,1},... | collective-permute-start | bytes 36872 | tf_op jit(solution)/shard_map/ppermute | solution.py:647
  25.2 1.4 %shard_map.67 = (f32[1,1,8,5,16,256]{5,4,3,2,1,0:T(8,128)}, f32[8,128]{1,0:T(8,128)S(1)}) custom-call(f32[40,128]{1,0:T(8,128)S(1)} %get-tuple-element.37.rates.moved_rates, f32[2,640,128]{2,1,0:T(8,128)S(1)} %get-tuple-element.49.partial, f32[120,128]{1,0:T(8,128)S(1)} %get-tuple-element.44.core_first, f32[120,128]{1,0:T(8,128)S(1)} %get-tuple-element.45.link_first, ...), custom_call_target="tpu_custom_call" | custom-call | flops 1000 | tf_op jit(solution)/shard_map/pallas_call | solution.py:49
  26.6 0.4 %collective-permute-done.10.by_column = f32[24,128]{1,0:T(8,128)S(1)} collective-permute-done((f32[24,128]{1,0:T(8,128)S(1)}, f32[24,128]{1,0:T(8,128)S(1)}, u32[]{:S(2)}, u32[]{:S(2)}) %collective-permute-start.10) | collective-permute-done | bytes 12320 | tf_op jit(solution)/shard_map/ppermute | solution.py:647
  27.1 0.6 %copy.6 = f32[1,1,5,6,256]{4,1,3,2,0:T(1,128)} copy(f32[1,1,5,6,256]{4,3,2,1,0:T(8,128)S(1)} %shard_map.68) | data formatting | bytes 61440
  (11 shorter events, 0.1 us)
Async XLA Ops:
  1.8 8.4 %collective-permute-start = (f32[48,256]{1,0:T(8,128)S(1)}, f32[48,256]{1,0:T(8,128)S(1)}, u32[]{:S(2)}, u32[]{:S(2)}) collective-permute-start(f32[48,256]{1,0:T(8,128)S(1)} %get-tuple-element.32), channel_id=1, source_target_pairs={{0,1},{1,0},{2,3},{3,2},{4,5},{5,4},{6,7},{7,6},{8,9},{9,8},{10,11... | collective-permute-start | bytes 147464 | tf_op jit(solution)/shard_map/ppermute | solution.py:647
  4.9 7.5 %collective-permute-start.1 = (f32[48,256]{1,0:T(8,128)S(1)}, f32[48,256]{1,0:T(8,128)S(1)}, u32[]{:S(2)}, u32[]{:S(2)}) collective-permute-start(f32[48,256]{1,0:T(8,128)S(1)} %get-tuple-element.33), channel_id=1, source_target_pairs={{0,31},{1,2},{2,1},{3,4},{4,3},{5,6},{6,5},{7,8},{8,7},{9,10},{10,... | collective-permute-start | bytes 147464 | tf_op jit(solution)/shard_map/ppermute | solution.py:647
  8.5 5.8 %collective-permute-start.2 = (f32[120,256]{1,0:T(8,128)S(1)}, f32[120,256]{1,0:T(8,128)S(1)}, u32[]{:S(2)}, u32[]{:S(2)}) collective-permute-start(f32[120,256]{1,0:T(8,128)S(1)} %get-tuple-element.38), channel_id=1, source_target_pairs={{0,1},{1,0},{2,3},{3,2},{4,5},{5,4},{6,7},{7,6},{8,9},{9,8},{10,11... | collective-permute-start | bytes 368648 | tf_op jit(solution)/shard_map/ppermute | solution.py:647
  8.5 9.0 %collective-permute-start.3 = (f32[120,256]{1,0:T(8,128)S(1)}, f32[120,256]{1,0:T(8,128)S(1)}, u32[]{:S(2)}, u32[]{:S(2)}) collective-permute-start(f32[120,256]{1,0:T(8,128)S(1)} %get-tuple-element.39), channel_id=1, source_target_pairs={{0,31},{1,2},{2,1},{3,4},{4,3},{5,6},{6,5},{7,8},{8,7},{9,10},{10,... | collective-permute-start | bytes 368648 | tf_op jit(solution)/shard_map/ppermute | solution.py:647
  12.5 5.4 %collective-permute-start.4 = (f32[168,128]{1,0:T(8,128)S(1)}, f32[168,128]{1,0:T(8,128)S(1)}, u32[]{:S(2)}, u32[]{:S(2)}) collective-permute-start(f32[168,128]{1,0:T(8,128)S(1)} %get-tuple-element.41.link_sent), channel_id=1, source_target_pairs={{0,2},{1,3},{2,0},{3,1},{4,6},{5,7},{6,4},{7,5},{8,16},{9,17},{10,... | collective-permute-start | bytes 258056 | tf_op jit(solution)/shard_map/ppermute | solution.py:647
  12.6 5.3 %collective-permute-start.5 = (f32[168,128]{1,0:T(8,128)S(1)}, f32[168,128]{1,0:T(8,128)S(1)}, u32[]{:S(2)}, u32[]{:S(2)}) collective-permute-start(f32[168,128]{1,0:T(8,128)S(1)} %get-tuple-element.42.core_sent), channel_id=1, source_target_pairs={{0,8},{1,9},{2,10},{3,11},{4,12},{5,13},{6,14},{7,15},{8,0},{9,1},... | collective-permute-start | bytes 258056 | tf_op jit(solution)/shard_map/ppermute | solution.py:647
  18.0 4.7 %collective-permute-start.6 = (f32[176,128]{1,0:T(8,128)S(1)}, f32[176,128]{1,0:T(8,128)S(1)}, u32[]{:S(2)}, u32[]{:S(2)}) collective-permute-start(f32[176,128]{1,0:T(8,128)S(1)} %get-tuple-element.48.far_sent), channel_id=1, source_target_pairs={{0,8},{1,2},{2,1},{3,4},{4,3},{5,6},{6,5},{7,15},{8,0},{9,10},{10,... | collective-permute-start | bytes 270344 | tf_op jit(solution)/shard_map/ppermute | solution.py:647
  18.1 4.6 %collective-permute-start.7 = (f32[96,128]{1,0:T(8,128)S(1)}, f32[96,128]{1,0:T(8,128)S(1)}, u32[]{:S(2)}, u32[]{:S(2)}) collective-permute-start(f32[96,128]{1,0:T(8,128)S(1)} %get-tuple-element.50.near_sent), channel_id=1, source_target_pairs={{0,1},{1,0},{2,3},{3,2},{4,5},{5,4},{6,7},{7,6},{8,9},{9,8},{10,11... | collective-permute-start | bytes 147464 | tf_op jit(solution)/shard_map/ppermute | solution.py:647
  18.7 6.5 %collective-permute-start.8 = (f32[80,128]{1,0:T(8,128)S(1)}, f32[80,128]{1,0:T(8,128)S(1)}, u32[]{:S(2)}, u32[]{:S(2)}) collective-permute-start(f32[80,128]{1,0:T(8,128)S(1)} %get-tuple-element.51), channel_id=1, source_target_pairs={{0,1},{1,0},{2,3},{3,2},{4,5},{5,4},{6,7},{7,6},{8,9},{9,8},{10,11... | collective-permute-start | bytes 122888 | tf_op jit(solution)/shard_map/ppermute | solution.py:647
  23.2 3.4 %collective-permute-start.9 = (f32[24,128]{1,0:T(8,128)S(1)}, f32[24,128]{1,0:T(8,128)S(1)}, u32[]{:S(2)}, u32[]{:S(2)}) collective-permute-start(f32[24,128]{1,0:T(8,128)S(1)} %get-tuple-element.58), channel_id=1, source_target_pairs={{0,9},{1,8},{2,11},{3,10},{4,13},{5,12},{6,15},{7,14},{8,1},{9,0},... | collective-permute-start | bytes 36872 | tf_op jit(solution)/shard_map/ppermute | solution.py:647
  23.3 3.8 %collective-permute-start.10 = (f32[24,128]{1,0:T(8,128)S(1)}, f32[24,128]{1,0:T(8,128)S(1)}, u32[]{:S(2)}, u32[]{:S(2)}) collective-permute-start(f32[24,128]{1,0:T(8,128)S(1)} %get-tuple-element.59), channel_id=1, source_target_pairs={{0,1},{1,0},{2,3},{3,2},{4,5},{5,4},{6,7},{7,6},{8,9},{9,8},{10,11... | collective-permute-start | bytes 36872 | tf_op jit(solution)/shard_map/ppermute | solution.py:647
  24.8 2.3 %collective-permute-start.11 = (f32[24,128]{1,0:T(8,128)S(1)}, f32[24,128]{1,0:T(8,128)S(1)}, u32[]{:S(2)}, u32[]{:S(2)}) collective-permute-start(f32[24,128]{1,0:T(8,128)S(1)} %get-tuple-element.60), channel_id=1, source_target_pairs={{0,8},{1,9},{2,10},{3,11},{4,12},{5,13},{6,14},{7,15},{8,0},{9,1},... | collective-permute-start | bytes 36872 | tf_op jit(solution)/shard_map/ppermute | solution.py:647

commit v9 on v8

--- a/solution.py
+++ b/solution.py
@@ -736,7 +736,7 @@
         [((1, 1, BZ, NC, E, 2 * L), "hbm"), ((BZ, L), "vmem")],
         [
             VM((2, 4 * PLANE, L), F32),
-            VM(big, F32),
+            VM((2, NC * E * BZ + BZ, L), F32),
             VM((NC, BZ, E, 2 * L), F32),
             pltpu.SemaphoreType.DMA((NC,)),
         ],

time: 27.9 us -> 27.9 us (level)
  no operation moved by 1% of the time
where the time goes in v9:
time: 27.9 us; the launch traced here: 27.8 us
  starting transfers between devices  13.8 us (49%)
  Pallas kernels  6.58 us (24%)
  waiting for transfers between devices  5.96 us (21%)
  between operations  0.74 us (3%)
  local copies, waits for them, and re-layouts  0.64 us (2%)
    ppermute x12, starting transfers between devices, swap(): return lax.ppermute(array, both, pairs)  13.8 us
    pallas_call x10, Pallas kernels, call(): pl.pallas_call(kernel, out_shape=shapes, in_specs=in_specs, out_specs=out...  6.58 us
    ppermute x12, waiting for transfers between devices, swap(): return lax.ppermute(array, both, pairs)  5.96 us
    unnamed x1, local copies, waits for them, and re-layouts  0.64 us
  transfers between devices with their start and end apart: 12, of which 4 were waited for; matrix products, arithmetic and copies ran while one was open for 0% of the time, Pallas kernels for 19%

profile of v9, /device:TPU:0, one launch (start us, length us, event | category | flops | bytes accessed | tf_op | source)
XLA Modules:
  0.0 27.8 jit_solution(623908192058793941)
XLA Ops:
  0.6 1.2 %shard_map.59 = (f32[48,256]{1,0:T(8,128)S(1)}, f32[48,256]{1,0:T(8,128)S(1)}, f32[120,256]{1,0:T(8,128)S(1)}, f32[120,256]{1,0:T(8,128)S(1)}, f32[8,5,16,256]{3...) custom-call(s32[1,1,8]{2,1,0:T(1,128)} %place_hbm.1, ...), custom_call_target="tpu_custom_call" | custom-call | flops 1000 | tf_op jit(solution)/shard_map/pallas_call | solution.py:49
  1.8 3.0 %collective-permute-start = (f32[48,256]{1,0:T(8,128)S(1)}, f32[48,256]{1,0:T(8,128)S(1)}, u32[]{:S(2)}, u32[]{:S(2)}) collective-permute-start(f32[48,256]{1,0:T(8,128)S(1)} %get-tuple-element.32), channel_id=1, source_target_pairs={{0,1},{1,0},{2,3},{3,2},{4,5},{5,4},{6,7},{7,6},{8,9},{9,8},{10,11... | collective-permute-start | bytes 147464 | tf_op jit(solution)/shard_map/ppermute | solution.py:647
  4.9 3.6 %collective-permute-start.1 = (f32[48,256]{1,0:T(8,128)S(1)}, f32[48,256]{1,0:T(8,128)S(1)}, u32[]{:S(2)}, u32[]{:S(2)}) collective-permute-start(f32[48,256]{1,0:T(8,128)S(1)} %get-tuple-element.33), channel_id=1, source_target_pairs={{0,31},{1,2},{2,1},{3,4},{4,3},{5,6},{6,5},{7,8},{8,7},{9,10},{10,... | collective-permute-start | bytes 147464 | tf_op jit(solution)/shard_map/ppermute | solution.py:647
  8.5 1.7 %collective-permute-start.3 = (f32[120,256]{1,0:T(8,128)S(1)}, f32[120,256]{1,0:T(8,128)S(1)}, u32[]{:S(2)}, u32[]{:S(2)}) collective-permute-start(f32[120,256]{1,0:T(8,128)S(1)} %get-tuple-element.39), channel_id=1, source_target_pairs={{0,31},{1,2},{2,1},{3,4},{4,3},{5,6},{6,5},{7,8},{8,7},{9,10},{10,... | collective-permute-start | bytes 368648 | tf_op jit(solution)/shard_map/ppermute | solution.py:647
  10.2 2.2 %collective-permute-done.1.odd = f32[48,256]{1,0:T(8,128)S(1)} collective-permute-done((f32[48,256]{1,0:T(8,128)S(1)}, f32[48,256]{1,0:T(8,128)S(1)}, u32[]{:S(2)}, u32[]{:S(2)}) %collective-permute-start.1) | collective-permute-done | bytes 49184 | tf_op jit(solution)/shard_map/ppermute | solution.py:647
  12.4 0.1 shard_map.60
  12.5 0.1 collective-permute-start.4
  12.6 1.3 %collective-permute-start.5 = (f32[168,128]{1,0:T(8,128)S(1)}, f32[168,128]{1,0:T(8,128)S(1)}, u32[]{:S(2)}, u32[]{:S(2)}) collective-permute-start(f32[168,128]{1,0:T(8,128)S(1)} %get-tuple-element.42.core_sent), channel_id=1, source_target_pairs={{0,8},{1,9},{2,10},{3,11},{4,12},{5,13},{6,14},{7,15},{8,0},{9,1},... | collective-permute-start | bytes 258056 | tf_op jit(solution)/shard_map/ppermute | solution.py:647
  13.9 0.3 shard_map.61.moved
  14.2 0.1 collective-permute-done.2.even_rest
  14.3 3.2 %collective-permute-done.3.odd_rest = f32[120,256]{1,0:T(8,128)S(1)} collective-permute-done((f32[120,256]{1,0:T(8,128)S(1)}, f32[120,256]{1,0:T(8,128)S(1)}, u32[]{:S(2)}, u32[]{:S(2)}) %collective-permute-start.3) | collective-permute-done | bytes 122912 | tf_op jit(solution)/shard_map/ppermute | solution.py:647
  17.5 0.4 %shard_map.62 = (f32[2,640,128]{2,1,0:T(8,128)S(1)}, f32[160,128]{1,0:T(8,128)S(1)}, f32[160,128]{1,0:T(8,128)S(1)}) custom-call(f32[48,256]{1,0:T(8,128)S(1)} %collective-permute-done.even, f32[48,256]{1,0:T(8,128)S(1)} %collective-permute-done.1.odd, f32[120,256]{1,0:T(8,128)S(1)} %collective-permute-done.2.even_rest, ...), custom_call_target="tpu_custom_call" | custom-call | flops 1000 | tf_op jit(solution)/shard_map/pallas_call | solution.py:49
  17.9 0.1 shard_map.64
  18.1 0.6 %collective-permute-start.7 = (f32[96,128]{1,0:T(8,128)S(1)}, f32[96,128]{1,0:T(8,128)S(1)}, u32[]{:S(2)}, u32[]{:S(2)}) collective-permute-start(f32[96,128]{1,0:T(8,128)S(1)} %get-tuple-element.50.near_sent), channel_id=1, source_target_pairs={{0,1},{1,0},{2,3},{3,2},{4,5},{5,4},{6,7},{7,6},{8,9},{9,8},{10,11... | collective-permute-start | bytes 147464 | tf_op jit(solution)/shard_map/ppermute | solution.py:647
  18.7 1.5 %collective-permute-start.8 = (f32[80,128]{1,0:T(8,128)S(1)}, f32[80,128]{1,0:T(8,128)S(1)}, u32[]{:S(2)}, u32[]{:S(2)}) collective-permute-start(f32[80,128]{1,0:T(8,128)S(1)} %get-tuple-element.51), channel_id=1, source_target_pairs={{0,1},{1,0},{2,3},{3,2},{4,5},{5,4},{6,7},{7,6},{8,9},{9,8},{10,11... | collective-permute-start | bytes 122888 | tf_op jit(solution)/shard_map/ppermute | solution.py:647
  20.2 1.4 %shard_map.63 = (f32[2,640,128]{2,1,0:T(8,128)S(1)}, f32[120,128]{1,0:T(8,128)S(1)}, f32[120,128]{1,0:T(8,128)S(1)}, f32[40,128]{1,0:T(8,128)S(1)}) custom-call(f32[2,640,128]{2,1,0:T(8,128)S(1)} %get-tuple-element.40.moved, f32[40,128]{1,0:T(8,128)S(1)} %get-tuple-element.37.rates.moved_rates, f32[168,128]{1,0:T(8,128)S(1)} %collective-permute-done.4.link, ...), custom_call_target="tpu_custom_call" | custom-call | flops 1000 | tf_op jit(solution)/shard_map/pallas_call | solution.py:49
  21.6 1.1 %shard_map.65 = (f32[2,640,128]{2,1,0:T(8,128)S(1)}, f32[80,128]{1,0:T(8,128)S(1)}) custom-call(f32[2,640,128]{2,1,0:T(8,128)S(1)} %get-tuple-element.40.moved, f32[40,128]{1,0:T(8,128)S(1)} %get-tuple-element.37.rates.moved_rates, f32[2,640,128]{2,1,0:T(8,128)S(1)} %get-tuple-element.43.partial, f32[120,128]{1,0:T(8,128)S(1)} %get-tuple-element.44.core_first, ...), custom_call_target="tpu_custom_call" | custom-call | flops 1000 | tf_op jit(solution)/shard_map/pallas_call | solution.py:49
  22.7 0.5 %shard_map.66 = (f32[80,128]{1,0:T(8,128)S(1)}, f32[24,128]{1,0:T(8,128)S(1)}, f32[24,128]{1,0:T(8,128)S(1)}, f32[24,128]{1,0:T(8,128)S(1)}, f32[24,128]{1,0:T(8,128)S(1)}) custom-call(f32[2,640,128]{2,1,0:T(8,128)S(1)} %get-tuple-element.43.partial, f32[40,128]{1,0:T(8,128)S(1)} %get-tuple-element.37.rates.moved_rates, ...), custom_call_target="tpu_custom_call" | custom-call | flops 1000 | tf_op jit(solution)/shard_map/pallas_call | solution.py:49
  23.2 0.1 collective-permute-start.9
  23.3 1.5 %collective-permute-start.10 = (f32[24,128]{1,0:T(8,128)S(1)}, f32[24,128]{1,0:T(8,128)S(1)}, u32[]{:S(2)}, u32[]{:S(2)}) collective-permute-start(f32[24,128]{1,0:T(8,128)S(1)} %get-tuple-element.59), channel_id=1, source_target_pairs={{0,1},{1,0},{2,3},{3,2},{4,5},{5,4},{6,7},{7,6},{8,9},{9,8},{10,11... | collective-permute-start | bytes 36872 | tf_op jit(solution)/shard_map/ppermute | solution.py:647
  24.8 0.3 %collective-permute-start.11 = (f32[24,128]{1,0:T(8,128)S(1)}, f32[24,128]{1,0:T(8,128)S(1)}, u32[]{:S(2)}, u32[]{:S(2)}) collective-permute-start(f32[24,128]{1,0:T(8,128)S(1)} %get-tuple-element.60), channel_id=1, source_target_pairs={{0,8},{1,9},{2,10},{3,11},{4,12},{5,13},{6,14},{7,15},{8,0},{9,1},... | collective-permute-start | bytes 36872 | tf_op jit(solution)/shard_map/ppermute | solution.py:647
  25.2 1.4 %shard_map.67 = (f32[1,1,8,5,16,256]{5,4,3,2,1,0:T(8,128)}, f32[8,128]{1,0:T(8,128)S(1)}) custom-call(f32[40,128]{1,0:T(8,128)S(1)} %get-tuple-element.37.rates.moved_rates, f32[2,640,128]{2,1,0:T(8,128)S(1)} %get-tuple-element.49.partial, f32[120,128]{1,0:T(8,128)S(1)} %get-tuple-element.44.core_first, f32[120,128]{1,0:T(8,128)S(1)} %get-tuple-element.45.link_first, ...), custom_call_target="tpu_custom_call" | custom-call | flops 1000 | tf_op jit(solution)/shard_map/pallas_call | solution.py:49
  26.6 0.4 %collective-permute-done.10.by_column = f32[24,128]{1,0:T(8,128)S(1)} collective-permute-done((f32[24,128]{1,0:T(8,128)S(1)}, f32[24,128]{1,0:T(8,128)S(1)}, u32[]{:S(2)}, u32[]{:S(2)}) %collective-permute-start.10) | collective-permute-done | bytes 12320 | tf_op jit(solution)/shard_map/ppermute | solution.py:647
  27.1 0.6 %copy.6 = f32[1,1,5,6,256]{4,1,3,2,0:T(1,128)} copy(f32[1,1,5,6,256]{4,3,2,1,0:T(8,128)S(1)} %shard_map.68) | data formatting | bytes 61440
  (11 shorter events, 0.1 us)
Async XLA Ops:
  1.8 8.4 %collective-permute-start = (f32[48,256]{1,0:T(8,128)S(1)}, f32[48,256]{1,0:T(8,128)S(1)}, u32[]{:S(2)}, u32[]{:S(2)}) collective-permute-start(f32[48,256]{1,0:T(8,128)S(1)} %get-tuple-element.32), channel_id=1, source_target_pairs={{0,1},{1,0},{2,3},{3,2},{4,5},{5,4},{6,7},{7,6},{8,9},{9,8},{10,11... | collective-permute-start | bytes 147464 | tf_op jit(solution)/shard_map/ppermute | solution.py:647
  4.9 7.5 %collective-permute-start.1 = (f32[48,256]{1,0:T(8,128)S(1)}, f32[48,256]{1,0:T(8,128)S(1)}, u32[]{:S(2)}, u32[]{:S(2)}) collective-permute-start(f32[48,256]{1,0:T(8,128)S(1)} %get-tuple-element.33), channel_id=1, source_target_pairs={{0,31},{1,2},{2,1},{3,4},{4,3},{5,6},{6,5},{7,8},{8,7},{9,10},{10,... | collective-permute-start | bytes 147464 | tf_op jit(solution)/shard_map/ppermute | solution.py:647
  8.5 5.8 %collective-permute-start.2 = (f32[120,256]{1,0:T(8,128)S(1)}, f32[120,256]{1,0:T(8,128)S(1)}, u32[]{:S(2)}, u32[]{:S(2)}) collective-permute-start(f32[120,256]{1,0:T(8,128)S(1)} %get-tuple-element.38), channel_id=1, source_target_pairs={{0,1},{1,0},{2,3},{3,2},{4,5},{5,4},{6,7},{7,6},{8,9},{9,8},{10,11... | collective-permute-start | bytes 368648 | tf_op jit(solution)/shard_map/ppermute | solution.py:647
  8.5 9.0 %collective-permute-start.3 = (f32[120,256]{1,0:T(8,128)S(1)}, f32[120,256]{1,0:T(8,128)S(1)}, u32[]{:S(2)}, u32[]{:S(2)}) collective-permute-start(f32[120,256]{1,0:T(8,128)S(1)} %get-tuple-element.39), channel_id=1, source_target_pairs={{0,31},{1,2},{2,1},{3,4},{4,3},{5,6},{6,5},{7,8},{8,7},{9,10},{10,... | collective-permute-start | bytes 368648 | tf_op jit(solution)/shard_map/ppermute | solution.py:647
  12.5 5.4 %collective-permute-start.4 = (f32[168,128]{1,0:T(8,128)S(1)}, f32[168,128]{1,0:T(8,128)S(1)}, u32[]{:S(2)}, u32[]{:S(2)}) collective-permute-start(f32[168,128]{1,0:T(8,128)S(1)} %get-tuple-element.41.link_sent), channel_id=1, source_target_pairs={{0,2},{1,3},{2,0},{3,1},{4,6},{5,7},{6,4},{7,5},{8,16},{9,17},{10,... | collective-permute-start | bytes 258056 | tf_op jit(solution)/shard_map/ppermute | solution.py:647
  12.6 5.3 %collective-permute-start.5 = (f32[168,128]{1,0:T(8,128)S(1)}, f32[168,128]{1,0:T(8,128)S(1)}, u32[]{:S(2)}, u32[]{:S(2)}) collective-permute-start(f32[168,128]{1,0:T(8,128)S(1)} %get-tuple-element.42.core_sent), channel_id=1, source_target_pairs={{0,8},{1,9},{2,10},{3,11},{4,12},{5,13},{6,14},{7,15},{8,0},{9,1},... | collective-permute-start | bytes 258056 | tf_op jit(solution)/shard_map/ppermute | solution.py:647
  18.0 4.7 %collective-permute-start.6 = (f32[176,128]{1,0:T(8,128)S(1)}, f32[176,128]{1,0:T(8,128)S(1)}, u32[]{:S(2)}, u32[]{:S(2)}) collective-permute-start(f32[176,128]{1,0:T(8,128)S(1)} %get-tuple-element.48.far_sent), channel_id=1, source_target_pairs={{0,8},{1,2},{2,1},{3,4},{4,3},{5,6},{6,5},{7,15},{8,0},{9,10},{10,... | collective-permute-start | bytes 270344 | tf_op jit(solution)/shard_map/ppermute | solution.py:647
  18.1 4.6 %collective-permute-start.7 = (f32[96,128]{1,0:T(8,128)S(1)}, f32[96,128]{1,0:T(8,128)S(1)}, u32[]{:S(2)}, u32[]{:S(2)}) collective-permute-start(f32[96,128]{1,0:T(8,128)S(1)} %get-tuple-element.50.near_sent), channel_id=1, source_target_pairs={{0,1},{1,0},{2,3},{3,2},{4,5},{5,4},{6,7},{7,6},{8,9},{9,8},{10,11... | collective-permute-start | bytes 147464 | tf_op jit(solution)/shard_map/ppermute | solution.py:647
  18.7 6.5 %collective-permute-start.8 = (f32[80,128]{1,0:T(8,128)S(1)}, f32[80,128]{1,0:T(8,128)S(1)}, u32[]{:S(2)}, u32[]{:S(2)}) collective-permute-start(f32[80,128]{1,0:T(8,128)S(1)} %get-tuple-element.51), channel_id=1, source_target_pairs={{0,1},{1,0},{2,3},{3,2},{4,5},{5,4},{6,7},{7,6},{8,9},{9,8},{10,11... | collective-permute-start | bytes 122888 | tf_op jit(solution)/shard_map/ppermute | solution.py:647
  23.2 3.4 %collective-permute-start.9 = (f32[24,128]{1,0:T(8,128)S(1)}, f32[24,128]{1,0:T(8,128)S(1)}, u32[]{:S(2)}, u32[]{:S(2)}) collective-permute-start(f32[24,128]{1,0:T(8,128)S(1)} %get-tuple-element.58), channel_id=1, source_target_pairs={{0,9},{1,8},{2,11},{3,10},{4,13},{5,12},{6,15},{7,14},{8,1},{9,0},... | collective-permute-start | bytes 36872 | tf_op jit(solution)/shard_map/ppermute | solution.py:647
  23.3 3.8 %collective-permute-start.10 = (f32[24,128]{1,0:T(8,128)S(1)}, f32[24,128]{1,0:T(8,128)S(1)}, u32[]{:S(2)}, u32[]{:S(2)}) collective-permute-start(f32[24,128]{1,0:T(8,128)S(1)} %get-tuple-element.59), channel_id=1, source_target_pairs={{0,1},{1,0},{2,3},{3,2},{4,5},{5,4},{6,7},{7,6},{8,9},{9,8},{10,11... | collective-permute-start | bytes 36872 | tf_op jit(solution)/shard_map/ppermute | solution.py:647
  24.8 2.3 %collective-permute-start.11 = (f32[24,128]{1,0:T(8,128)S(1)}, f32[24,128]{1,0:T(8,128)S(1)}, u32[]{:S(2)}, u32[]{:S(2)}) collective-permute-start(f32[24,128]{1,0:T(8,128)S(1)} %get-tuple-element.60), channel_id=1, source_target_pairs={{0,8},{1,9},{2,10},{3,11},{4,12},{5,13},{6,14},{7,15},{8,0},{9,1},... | collective-permute-start | bytes 36872 | tf_op jit(solution)/shard_map/ppermute | solution.py:647
